TPU v7x, 32 devices: a whole 2x2x4 slice. The times are simulated.
32 devices in a mesh: groups: 2 (over y), dp: 4 (over z), tensor: 4 (over x, core).
Axes of the slice: x: 2, y: 2, z: 4, core: 2. Of those that a mesh axis runs over, the one named last changes fastest.
Arguments:
- tokens: bfloat16 [1024, 1792], P(('groups', 'dp')), parts along dimension 0, may hold values from -6 to 6
- expert_ids: int32 [1024, 8], P(('groups', 'dp')), parts along dimension 0, may hold values from 0 to 31, all different within a row; in each aligned block of 128 rows (0 to 127, 128 to 255, ...) at most 48 rows name the same one
- route_gates: float32 [1024, 8], P(('groups', 'dp')), parts along dimension 0, may hold values from 0.05 to 0.5
- shared_gate_vec: bfloat16 [1792], replicated, may hold values from -0.125 to 0.125
- w_shared_gate: bfloat16 [1792, 10240], P('dp', 'tensor'), may hold values from -0.125 to 0.125
- w_shared_up: bfloat16 [1792, 10240], P('dp', 'tensor'), may hold values from -0.125 to 0.125
- w_shared_down_t: bfloat16 [1792, 10240], P('dp', 'tensor'), may hold values from -0.0625 to 0.0625
- w_expert_gate_t: bfloat16 [32, 2560, 1792], P('dp', 'tensor'), may hold values from -0.125 to 0.125
- w_expert_up_t: bfloat16 [32, 2560, 1792], P('dp', 'tensor'), may hold values from -0.125 to 0.125
- w_expert_down: bfloat16 [32, 2560, 1792], P('dp', 'tensor'), may hold values from -0.125 to 0.125
Outputs:
- moe_out: bfloat16 [1024, 1792], P(('groups', 'dp'), 'tensor'), parts along dimension 0
There are 2 independent parts, one for each index of `groups`. A program takes and returns all parts, laid end to end along the dimension named above; an argument that names none is the same for every part. Nothing has to cross between parts.
Inputs may be any that keep to these rules, and one draw needn't show every extreme that they name: `expert_ids`: each row names 8 different experts. Within the rows of one index of dp (aligned blocks of 128 rows), no expert is named more than 48 times, a bound that some block reaches.
All inputs are finite; a program needn't handle non-finite values.
Results may differ from a plain program's by a relative error of at most 0.0049.
Values may be sent and summed in bfloat16 or wider, within the bound.
No kernel may reach another device: no remote copies, remote signals or barrier semaphores. Data moves between devices by JAX's collectives and lax.ppermute only.
A program may use at most 256 MiB of HBM per device.

v0:
```python
import jax
import jax.numpy as jnp
from jax import lax
from jax.sharding import PartitionSpec as P

CAP = 48


def slot_places(expert_ids, experts):
    flat_ids = expert_ids.reshape(-1)
    labels = jnp.arange(experts, dtype=jnp.int32)
    onehot = (flat_ids[:, None] == labels[None, :]).astype(jnp.int32)
    before = jnp.cumsum(onehot, axis=0, dtype=jnp.int32) - onehot
    return (jnp.sum(before * onehot, axis=1, dtype=jnp.int32), flat_ids)


def on_device(
    tokens,
    expert_ids,
    route_gates,
    shared_gate_vec,
    w_shared_gate,
    w_shared_up,
    w_shared_down_t,
    w_expert_gate_t,
    w_expert_up_t,
    w_expert_down,
):
    n_dp = lax.axis_size("dp")
    row_count, model_width = tokens.shape
    top_k = expert_ids.shape[1]
    exp_dev = w_expert_gate_t.shape[0]
    experts = exp_dev * n_dp
    portion_gate = lax.all_gather(w_shared_gate, "dp", axis=0, tiled=True)
    portion_up = lax.all_gather(w_shared_up, "dp", axis=0, tiled=True)
    portion_down = lax.all_gather(w_shared_down_t, "dp", axis=0, tiled=True)
    acc_gate = jnp.dot(tokens, portion_gate, preferred_element_type=jnp.float32)
    acc_up = jnp.dot(tokens, portion_up, preferred_element_type=jnp.float32)
    down_full = portion_down
    shared_gate, shared_up, down_full = (acc_gate, acc_up, down_full)
    shared_hidden = (jax.nn.silu(shared_gate) * shared_up).astype(jnp.bfloat16)
    shared_part = lax.dot_general(
        shared_hidden, down_full, (((1,), (1,)), ((), ())), preferred_element_type=jnp.float32
    )
    shared_scale = jax.nn.sigmoid(
        jnp.dot(tokens, shared_gate_vec, preferred_element_type=jnp.float32)
    )
    places, flat_ids = slot_places(expert_ids, experts)
    target = flat_ids * CAP + places
    source_rows = jnp.arange(row_count * top_k, dtype=jnp.int32) // top_k
    outgoing = (
        jnp.zeros((experts * CAP, model_width), jnp.bfloat16).at[target].set(tokens[source_rows])
    )
    arrived = lax.all_to_all(
        outgoing.reshape(n_dp, exp_dev * CAP, model_width),
        "dp",
        split_axis=0,
        concat_axis=0,
        tiled=True,
    )
    arrived = arrived.reshape(n_dp, exp_dev, CAP, model_width)
    ex_gate = jnp.einsum(
        "sjcd,jfd->sjcf", arrived, w_expert_gate_t, preferred_element_type=jnp.float32
    )
    ex_up = jnp.einsum("sjcd,jfd->sjcf", arrived, w_expert_up_t, preferred_element_type=jnp.float32)
    ex_hidden = (jax.nn.silu(ex_gate) * ex_up).astype(jnp.bfloat16)
    ex_part = jnp.einsum(
        "sjcf,jfd->sjcd", ex_hidden, w_expert_down, preferred_element_type=jnp.float32
    )
    returned = lax.all_to_all(
        ex_part.reshape(n_dp, exp_dev * CAP, model_width),
        "dp",
        split_axis=0,
        concat_axis=0,
        tiled=True,
    )
    returned = returned.reshape(experts * CAP, model_width)
    picked = returned[target].reshape(row_count, top_k, model_width)
    routed = jnp.sum(picked * route_gates[:, :, None], axis=1)
    combined = shared_scale[:, None] * shared_part + routed
    return lax.psum_scatter(combined, "tensor", scatter_dimension=1, tiled=True).astype(
        jnp.bfloat16
    )


def solution(mesh):
    return jax.shard_map(
        on_device,
        mesh=mesh,
        in_specs=(
            P(("groups", "dp"), None),
            P(("groups", "dp"), None),
            P(("groups", "dp"), None),
            P(),
            P("dp", "tensor"),
            P("dp", "tensor"),
            P("dp", "tensor"),
            P("dp", "tensor", None),
            P("dp", "tensor", None),
            P("dp", "tensor", None),
        ),
        out_specs=P(("groups", "dp"), "tensor"),
        check_vma=False,
    )
```

profile of v0, /device:TPU:0, one launch (start us, length us, event | category | flops | bytes accessed | tf_op | source)
XLA Modules:
  0.0 883.3 jit_solution(4710868842151652355)
XLA Ops:
  6.5 0.7 all-gather.4.cloned.1.call-update
  7.3 0.8 copy.21
  8.0 0.1 eq.29
  8.1 0.1 eq.25
  8.3 9.0 %reduce-window.6 = s32[32,8,128]{2,1,0:T(8,128)S(1)} reduce-window(s32[32,8,128]{2,1,0:T(8,128)S(1)} %fusion.36, s32[]{:T(128)} %constant.32.clone.1), window={size=1x1x128 pad=0_0x0_0x127_0}, to_apply=%region_0.1 | reduce-window | flops 4161536 | bytes 262148 | tf_op jit(solution)/shard_map/reduce-window
  17.3 0.1 slice.12
  17.4 0.1 copy.23
  17.5 0.1 copy.24
  17.6 0.7 broadcast_multiply_fusion
  18.3 0.1 copy.20
  18.4 0.1 mul.55
  18.5 0.1 broadcast_add_fusion
  18.7 21.1 %scatter_custom_fusion = bf16[1536,1792]{1,0:T(8,128)(2,1)} fusion(s32[1024]{0:T(1024)S(1)} %bitcast.95, bf16[128,1792]{1,0:T(8,128)(2,1)S(1)} %copy-done, s32[1024]{0:T(1024)S(1)} %broadcast_clamp_fusion.1, bf16[]{:T(256)} %constant.30.clone.1), kind=kCustom, calls=%fused_computation.22 | custom fusion | bytes 5505026 | tf_op jit(solution)/shard_map/scatter | solution.py:52
  39.8 6.3 all-to-all-start
  46.1 0.7 all-gather.6.cloned.1.call-update
  46.9 241.9 %all-to-all-done = bf16[4,384,1792]{2,1,0:T(8,128)(2,1)} async-done(((bf16[4,384,1792]{2,1,0:T(8,128)(2,1)}), bf16[4,384,1792]{2,1,0:T(8,128)(2,1)}, u32[]{:S(2)}, u32[]{:S(2)}) %all-to-all-start) | async-done | bytes 5505056 | tf_op jit(solution)/shard_map/all_to_all | solution.py:54
  288.8 13.1 %fusion.2 = f32[8,4,48,640]{3,2,1,0:T(8,128)} fusion(bf16[8,640,1792]{2,1,0:T(8,128)(2,1)} %param.18, bf16[4,8,48,1792]{3,2,1,0:T(8,128)(2,1)} %bitcast.7), kind=kOutput, calls=%fused_computation.5 | convolution fusion | flops 3523215360 | bytes 27787264 | tf_op jit(solution)/shard_map/sjcd,jfd->sjcf/dot_general | solution.py:65
  301.9 22.3 %fusion.7 = f32[4,8,48,1792]{3,2,0,1:T(8,128)} fusion(bf16[8,640,1792]{2,1,0:T(8,128)(2,1)} %param.19, f32[8,4,48,640]{3,2,1,0:T(8,128)} %fusion.2, bf16[8,640,1792]{2,1,0:T(8,128)(2,1)} %param.17, bf16[4,8,48,1792]{3,2,1,0:T(8,128)(2,1)} %bitcast.7), kind=kOutput, calls=%fused_computation.11 | convolution fusion | flops 7052328960 | bytes 57147392 | tf_op jit(solution)/shard_map/sjcf,jfd->sjcd/dot_general | solution.py:67
  324.2 9.2 %copy.27 = f32[4,8,48,1792]{3,2,1,0:T(8,128)} copy(f32[4,8,48,1792]{3,2,0,1:T(8,128)} %fusion.7) | data formatting | bytes 22020096 | tf_op jit(solution)/shard_map/sjcf,jfd->sjcd/transpose | solution.py:67
  333.3 6.2 all-to-all-start.1
  339.6 0.7 all-gather.8.cloned.1.call-update
  340.3 0.3 reduce-scatter.2.cloned.1.call-start
  340.6 0.1 copy.28
  340.7 0.2 fusion.28
  340.9 5.0 fusion.39
  346.0 476.0 %all-to-all-done.1 = f32[4,384,1792]{2,1,0:T(8,128)} async-done(((f32[4,384,1792]{2,1,0:T(8,128)}), f32[4,384,1792]{2,1,0:T(8,128)}, u32[]{:S(2)}, u32[]{:S(2)}) %all-to-all-start.1) | async-done | bytes 11010080 | tf_op jit(solution)/shard_map/all_to_all | solution.py:70
  822.0 12.4 %gather_fusion = f32[1024,1792]{1,0:T(8,128)} fusion(f32[1536,1792]{1,0:T(8,128)} %bitcast.18, s32[1024]{0:T(1024)S(1)} %broadcast_clamp_fusion), kind=kCustom, calls=%fused_computation.1 | custom fusion | bytes 14684160 | tf_op jit(solution)/shard_map/gather | solution.py:78
  834.4 5.6 fusion.6
  840.0 1.2 copy.29
  841.2 11.4 %fusion.20 = f32[128,1792]{0,1:T(8,128)} fusion(f32[128,1792]{0,1:T(8,128)} %copy.29, bf16[1792,2560]{1,0:T(8,128)(2,1)} %all-gather.8.cloned.1.call-done, bf16[128,1792]{1,0:T(8,128)(2,1)S(1)} %copy-done, bf16[1792,2560]{1,0:T(8,128)(2,1)} %all-gather.6.cloned.1.call-done, f32[128,2560]{1,0:T(8,128)S(1)} %fusion.39, f32[128]{0:T(128)S(1)} %fusion.28), kind=kOutput, calls=%fused_computation.27 | convolution fusion | flops 2351235072 | bytes 21955072 | tf_op jit(solution)/shard_map/dot_general | solution.py:42
  852.6 22.6 %reduce-scatter.2.cloned.1.call-done = f32[128,448]{0,1:T(8,128)} async-done(((f32[128,1792]{0,1:T(8,128)}), f32[128,448]{0,1:T(8,128)}) %reduce-scatter.2.cloned.1.call-update) | async-done | bytes 229392 | tf_op jit(solution)/shard_map/reduce_scatter | solution.py:81
  875.2 1.6 convert_element_type.20
  (22 shorter events, 0.2 us)
Async XLA Ops:
  6.5 12.2 %copy-start = (bf16[128,1792]{1,0:T(8,128)(2,1)S(1)}, bf16[128,1792]{1,0:T(8,128)(2,1)}, u32[]{:S(2)}) copy-start(bf16[128,1792]{1,0:T(8,128)(2,1)} %param.10) | copy-start | bytes 1376260
  6.5 334.4 %all-gather.4.cloned.1.call-start = ((), (), s32[]{:S(2)}) async-start(), calls=%async_computation.3 | async-start | bytes 11468800 | tf_op jit(solution)/shard_map/all_gather | solution.py:34
  39.8 249.0 %all-to-all-start = ((bf16[4,384,1792]{2,1,0:T(8,128)(2,1)}), bf16[4,384,1792]{2,1,0:T(8,128)(2,1)}, u32[]{:S(2)}, u32[]{:S(2)}) async-start(bf16[4,384,1792]{2,1,0:T(8,128)(2,1)} %bitcast.91), calls=%async_computation | async-start | bytes 11010048 | tf_op jit(solution)/shard_map/all_to_all | solution.py:54
  46.1 795.1 %all-gather.6.cloned.1.call-start = ((), (), s32[]{:S(2)}) async-start(), calls=%async_computation.4 | async-start | bytes 11468800 | tf_op jit(solution)/shard_map/all_gather | solution.py:35
  333.3 7.3 copy-start.1
  333.3 7.4 copy-start.2
  333.3 488.7 %all-to-all-start.1 = ((f32[4,384,1792]{2,1,0:T(8,128)}), f32[4,384,1792]{2,1,0:T(8,128)}, u32[]{:S(2)}, u32[]{:S(2)}) async-start(f32[4,384,1792]{2,1,0:T(8,128)} %bitcast.90), calls=%async_computation.1 | async-start | bytes 22020096 | tf_op jit(solution)/shard_map/all_to_all | solution.py:70
  339.6 501.6 %all-gather.8.cloned.1.call-start = ((), (), s32[]{:S(2)}) async-start(), calls=%async_computation.5 | async-start | bytes 11468800 | tf_op jit(solution)/shard_map/all_gather | solution.py:36
  340.3 534.9 %reduce-scatter.2.cloned.1.call-start = ((), (), s32[]{:S(2)}) async-start(), calls=%async_computation.6 | async-start | bytes 1146880 | tf_op jit(solution)/shard_map/reduce_scatter | solution.py:81
Sparse Core Ops, SparseCore 0:
  8.9 282.7 all-gather.3
  293.3 274.5 all-gather.5
  569.5 267.6 all-gather.7
  852.7 22.3 reduce-scatter.1
where the time goes:
time: 884 us; the launch traced here: 883 us
  waiting for transfers between devices  743 us (84%)
  matrix products  52 us (6%)
  local copies, waits for them, and re-layouts  45.5 us (5%)
  other arithmetic  17.1 us (2%)
  between operations  13.2 us (1%)
  starting transfers between devices  12.9 us (1%)
    all_to_all x1, waiting for transfers between devices, on_device(): lax.all_to_all(ex_part.reshape(n_dp, exp_dev * CAP, model_width), 'dp', s...  476 us
    all_to_all x1, waiting for transfers between devices, on_device(): lax.all_to_all(outgoing.reshape(n_dp, exp_dev * CAP, model_width), 'dp',...  242 us
    reduce_scatter x1, waiting for transfers between devices, on_device(): lax.psum_scatter(combined, 'tensor', scatter_dimension=1, tiled=True)  22.6 us
    dot_general x1, matrix products, on_device(): jnp.einsum('sjcf,jfd->sjcd', ex_hidden, w_expert_down, preferred_element_...  22.3 us
    scatter x1, local copies, waits for them, and re-layouts, on_device(): jnp.zeros((experts * CAP, model_width), jnp.bfloat16).at[target]  21.1 us
  transfers between devices with their start and end apart: 6, of which 3 were waited for; matrix products, arithmetic and copies ran while one was open for 11% of the time, Pallas kernels for 0%

commit v1 on v0

--- a/solution.py
+++ b/solution.py
@@ -4,6 +4,9 @@
 from jax.sharding import PartitionSpec as P
 
 CAP = 48
+BF = jnp.bfloat16
+F32 = jnp.float32
+CHUNKS = 2
 
 
 def slot_places(expert_ids, experts):
@@ -14,7 +17,7 @@
     return (jnp.sum(before * onehot, axis=1, dtype=jnp.int32), flat_ids)
 
 
-def on_device(
+def general(
     tokens,
     expert_ids,
     route_gates,
@@ -36,11 +39,9 @@
     portion_down = lax.all_gather(w_shared_down_t, "dp", axis=0, tiled=True)
     acc_gate = jnp.dot(tokens, portion_gate, preferred_element_type=jnp.float32)
     acc_up = jnp.dot(tokens, portion_up, preferred_element_type=jnp.float32)
-    down_full = portion_down
-    shared_gate, shared_up, down_full = (acc_gate, acc_up, down_full)
-    shared_hidden = (jax.nn.silu(shared_gate) * shared_up).astype(jnp.bfloat16)
+    shared_hidden = (jax.nn.silu(acc_gate) * acc_up).astype(jnp.bfloat16)
     shared_part = lax.dot_general(
-        shared_hidden, down_full, (((1,), (1,)), ((), ())), preferred_element_type=jnp.float32
+        shared_hidden, portion_down, (((1,), (1,)), ((), ())), preferred_element_type=jnp.float32
     )
     shared_scale = jax.nn.sigmoid(
         jnp.dot(tokens, shared_gate_vec, preferred_element_type=jnp.float32)
@@ -83,7 +84,172 @@
     )
 
 
+def swap(x, axis, bit):
+    n = lax.axis_size(axis)
+    return lax.ppermute(x, axis, [(i, i ^ bit) for i in range(n)])
+
+
+def pack_pair(first, second, start, side, width):
+    rows = first.shape[0]
+    whole = width - 64
+    wide = start + side * (width + 64)
+    mid = start + whole
+
+    def part(m):
+        body = lax.dynamic_slice(m, (0, wide), (rows, whole))
+        tile = lax.dynamic_slice(m, (0, mid), (rows, 128))
+        return body, jnp.where(side == 0, tile[:, :64], tile[:, 64:])
+
+    body_a, half_a = part(first)
+    body_b, half_b = part(second)
+    return jnp.concatenate([body_a, half_a, half_b, body_b], axis=1)
+
+
+def exchanged(
+    tokens,
+    expert_ids,
+    route_gates,
+    shared_gate_vec,
+    w_shared_gate,
+    w_shared_up,
+    w_shared_down_t,
+    w_expert_gate_t,
+    w_expert_up_t,
+    w_expert_down,
+):
+    z, t, g = lax.axis_index("dp"), lax.axis_index("tensor"), lax.axis_index("groups")
+    n_dp, n_t, n_g = lax.axis_size("dp"), lax.axis_size("tensor"), lax.axis_size("groups")
+    rows, d = tokens.shape
+    e_dev, ff_e, _ = w_expert_gate_t.shape
+    d_part, ff = w_shared_gate.shape
+    width = ff // (n_dp * n_g)
+    whole = width - 64
+    step = d_part // CHUNKS
+    half = step // 2
+
+    gu_pieces, down_pieces = [], []
+    for k in range(n_dp):
+        start = (z ^ k) * (2 * width)
+        gu_pieces.append(pack_pair(w_shared_gate, w_shared_up, start, g, width))
+        down_pieces.append(
+            [
+                pack_pair(
+                    w_shared_down_t[step * c : step * c + half],
+                    w_shared_down_t[step * c + half : step * (c + 1)],
+                    start,
+                    g,
+                    width,
+                )
+                for c in range(CHUNKS)
+            ]
+        )
+
+    quarter = rows // n_t
+    mine = lax.dynamic_slice(tokens, (t * quarter, 0), (quarter, d))
+    over_z = jnp.stack([mine] + [swap(mine, "dp", k) for k in range(1, n_dp)])
+
+    def spread(q):
+        other = swap(q, "tensor", 2)
+        q1, other1 = swap(q, "tensor", 1), swap(other, "tensor", 1)
+        full = jnp.zeros((n_dp, n_t, quarter, d), BF)
+        for piece, idx in ((q, t), (other, t ^ 2), (q1, t ^ 1), (other1, t ^ 3)):
+            full = lax.dynamic_update_slice(full, piece[:, None], (0, idx, 0, 0))
+        return full.reshape(n_dp * rows, d)
+
+    tok_own = spread(over_z)
+    tok_other = spread(swap(over_z, "groups", 1))
+
+    def gates_for(owner):
+        labels = owner * e_dev + jnp.arange(e_dev, dtype=jnp.int32)
+        hit = expert_ids[None, :, :] == labels[:, None, None]
+        return jnp.sum(jnp.where(hit, route_gates[None, :, :], 0.0), axis=2)
+
+    gate_cols = [gates_for(z)] + [swap(gates_for(z ^ k), "dp", k) for k in range(1, n_dp)]
+    gate_matrix = jnp.concatenate(gate_cols, axis=1)
+
+    dims = (((1,), (1,)), ((), ()))
+    eg = lax.dot_general(
+        tok_own, w_expert_gate_t.reshape(e_dev * ff_e, d), dims, preferred_element_type=F32
+    )
+    eu = lax.dot_general(
+        tok_own, w_expert_up_t.reshape(e_dev * ff_e, d), dims, preferred_element_type=F32
+    )
+    spread_gates = jnp.repeat(gate_matrix.T, ff_e, axis=1)
+    eh = (jax.nn.silu(eg) * eu * spread_gates).astype(BF)
+    routed = jnp.dot(eh, w_expert_down.reshape(e_dev * ff_e, d), preferred_element_type=F32)
+    routed_t = routed.T
+
+    gu = [gu_pieces[0]] + [swap(gu_pieces[k], "dp", k) for k in range(1, n_dp)]
+    w_gu = jnp.zeros((n_dp * d_part, 2 * width), BF)
+    for k in range(n_dp):
+        w_gu = lax.dynamic_update_slice(w_gu, gu[k], ((z ^ k) * d_part, 0))
+    tok_all = jnp.concatenate([tok_own, tok_other], axis=0)
+    acc = jnp.dot(tok_all, w_gu, preferred_element_type=F32)
+    s_gate, s_up = acc[:, :width], jnp.concatenate([acc[:, width + 64 :], acc[:, width : width + 64]], 1)
+    s_hidden = (jax.nn.silu(s_gate) * s_up).astype(BF)
+    zero = jnp.zeros_like(s_hidden)
+    left = jnp.concatenate([s_hidden, zero], axis=1)
+    right = jnp.concatenate([zero[:, :width], s_hidden[:, whole:], s_hidden[:, :whole]], axis=1)
+    scale = jax.nn.sigmoid(
+        lax.dot_general(
+            shared_gate_vec[None, :], tok_all, dims, preferred_element_type=F32
+        )
+    )
+    n_tok = n_dp * rows
+
+    routed_blocks = routed_t.reshape(n_t, d // n_t, n_tok)
+    out_rows = []
+    for c in range(CHUNKS):
+        wd = [down_pieces[0][c]] + [swap(down_pieces[k][c], "dp", k) for k in range(1, n_dp)]
+        w_d = jnp.zeros((n_dp, half, 2 * width), BF)
+        for k in range(n_dp):
+            w_d = lax.dynamic_update_slice(w_d, wd[k][None], (z ^ k, 0, 0))
+        w_d = w_d.reshape(n_dp * half, 2 * width)
+        top = lax.dot_general(w_d, left, dims, preferred_element_type=F32)
+        bottom = lax.dot_general(w_d, right, dims, preferred_element_type=F32)
+        part = jnp.concatenate(
+            [top.reshape(n_dp, half, -1), bottom.reshape(n_dp, half, -1)], axis=1
+        )
+        part = part * scale
+        own = part[:, :, :n_tok] + routed_blocks[:, step * c : step * (c + 1), :]
+        part = jnp.concatenate([own, part[:, :, n_tok:]], axis=2)
+        pairs = part.reshape(n_t // 2, 2, step, 2 * n_tok)
+        keep = lax.dynamic_index_in_dim(pairs, t & 1, 1, keepdims=False)
+        give = lax.dynamic_index_in_dim(pairs, (t & 1) ^ 1, 1, keepdims=False).astype(BF)
+        keep = keep + swap(give, "tensor", 1).astype(F32)
+        here = lax.dynamic_index_in_dim(keep, t >> 1, 0, keepdims=False)
+        there = lax.dynamic_index_in_dim(keep, (t >> 1) ^ 1, 0, keepdims=False).astype(BF)
+        total = here[:, :n_tok] + swap(there[:, :n_tok], "tensor", 2).astype(F32)
+        total = total + swap(here[:, n_tok:].astype(BF), "groups", 1).astype(F32)
+        far = there[:, n_tok:]
+        n_pair = n_g * n_t
+        total = total + lax.ppermute(
+            far, ("groups", "tensor"), [(i, i ^ (n_t + 2)) for i in range(n_pair)]
+        ).astype(F32)
+        done = total[:, :rows]
+        for k in range(1, n_dp):
+            piece = total[:, rows * k : rows * (k + 1)].astype(BF)
+            done = done + swap(piece, "dp", k).astype(F32)
+        out_rows.append(done)
+    return jnp.concatenate(out_rows, axis=0).T.astype(BF)
+
+
 def solution(mesh):
+    sizes = mesh.shape
+
+    def on_device(*args):
+        d_part, ff = args[4].shape
+        width = ff // (sizes["dp"] * sizes["groups"])
+        fits = (
+            sizes["dp"] == 4
+            and sizes["tensor"] == 4
+            and sizes["groups"] == 2
+            and width % 128 == 64
+            and d_part % (32 * CHUNKS) == 0
+            and args[0].shape[0] % 128 == 0
+        )
+        return (exchanged if fits else general)(*args)
+
     return jax.shard_map(
         on_device,
         mesh=mesh,

time: 884 us -> 231 us (0.26)
  waiting for transfers between devices: 743 us -> 53.3 us
  starting transfers between devices: 12.9 us -> 55.1 us
  between operations: 13.2 us -> 1.02 us
    all_to_all x2 -> x0, waiting for transfers between devices: 718 us -> none  [the longest x1 476 us: on_device(): lax.all_to_all(ex_part.reshape(n_dp, exp_dev * CAP, model_width), 'dp', s...]
    ppermute x0 -> x36, starting transfers between devices: none -> 55.1 us  [the longest x34 54 us: swap(): return lax.ppermute(x, axis, [(i, i ^ bit) for i in range(n)])]
    ppermute x0 -> x36, waiting for transfers between devices: none -> 53.3 us  [the longest x34 50.4 us: swap(): return lax.ppermute(x, axis, [(i, i ^ bit) for i in range(n)])]
    reduce_scatter x1 -> x0, waiting for transfers between devices: 22.6 us -> none  [on_device(): lax.psum_scatter(combined, 'tensor', scatter_dimension=1, tiled=True)]
    scatter x1 -> x0, local copies, waits for them, and re-layouts: 21.1 us -> none  [on_device(): jnp.zeros((experts * CAP, model_width), jnp.bfloat16).at[target]]
    all_to_all x2 -> x0, starting transfers between devices: 12.6 us -> none  [the longest x1 6.32 us: on_device(): lax.all_to_all(outgoing.reshape(n_dp, exp_dev * CAP, model_width), 'dp',...]
    gather x1 -> x0, local copies, waits for them, and re-layouts: 12.4 us -> none  [on_device(): picked = returned[target].reshape(row_count, top_k, model_width)]
    unnamed x9 -> x106, local copies, waits for them, and re-layouts: 0.91 us -> 12.4 us
  transfers between devices with their start and end apart: 6 -> 36, of which waited for: 3 -> 8; matrix products, arithmetic and copies ran while one was open for 11% -> 41% of each run, Pallas kernels for 0% -> 0%
where the time goes in v1:
time: 231 us; the launch traced here: 230 us
  matrix products  57.4 us (25%)
  starting transfers between devices  55.1 us (24%)
  waiting for transfers between devices  53.3 us (23%)
  local copies, waits for them, and re-layouts  37.6 us (16%)
  other arithmetic  25.9 us (11%)
    ppermute x34, starting transfers between devices, swap(): return lax.ppermute(x, axis, [(i, i ^ bit) for i in range(n)])  54 us
    ppermute x34, waiting for transfers between devices, swap(): return lax.ppermute(x, axis, [(i, i ^ bit) for i in range(n)])  50.4 us
    dot_general x1, matrix products, exchanged(): jnp.dot(eh, w_expert_down.reshape(e_dev * ff_e, d), preferred_element_typ...  28.8 us
    dot_general x1, matrix products, exchanged(): lax.dot_general(tok_own, w_expert_gate_t.reshape(e_dev * ff_e, d), dims,...  16.4 us
    unnamed x106, local copies, waits for them, and re-layouts  12.4 us
    concatenate x9, other arithmetic, pack_pair(): return jnp.concatenate([body_a, half_a, half_b, body_b], axis=1)  8.99 us
    transpose x1, local copies, waits for them, and re-layouts, exchanged(): routed_t = routed.T  5.12 us
    dynamic_update_slice x7, local copies, waits for them, and re-layouts, spread(): full = lax.dynamic_update_slice(full, piece[:, None], (0, idx, 0, 0))  4.75 us
  transfers between devices with their start and end apart: 36, of which 8 were waited for; matrix products, arithmetic and copies ran while one was open for 41% of the time, Pallas kernels for 0%

profile of v1, /device:TPU:0, one launch (start us, length us, event | category | flops | bytes accessed | tf_op | source)
XLA Modules:
  0.0 230.4 jit_solution(13387715673493432736)
XLA Ops:
  1.7 5.0 %collective-permute-start.5 = (bf16[32,1792]{1,0:T(8,128)(2,1)}, bf16[32,1792]{1,0:T(8,128)(2,1)}, u32[]{:S(2)}, u32[]{:S(2)}) collective-permute-start(bf16[32,1792]{1,0:T(8,128)(2,1)} %constant_dynamic-slice_fusion.16), channel_id=1, source_target_pairs={{0,12},{4,8},{8,4},{12,0},{1,13},{5,9},{9,5},{13,1},{2,14},{6,10},... | collective-permute-start | bytes 344072 | tf_op jit(solution)/shard_map/ppermute | solution.py:89
  8.2 1.9 collective-permute-start.18
  12.6 1.7 fusion.42
  15.2 2.5 %constant_dynamic-slice_fusion.8 = (bf16[448,256]{1,0:T(8,128)(2,1)S(1)}, bf16[448,256]{1,0:T(8,128)(2,1)S(1)}, bf16[448,256]{1,0:T(8,128)(2,1)S(1)}, bf16[448,2...) fusion(bf16[448,2560]{1,0:T(8,128)(2,1)} %param.15, ...), kind=kLoop, calls=%fused_computation.120 | loop fusion | bytes 3670032 | tf_op jit(solution)/shard_map/dynamic_slice | solution.py:99
  18.7 2.9 %dynamic-slice_select_fusion = (bf16[448,64]{1,0:T(8,128)(2,1)S(1)}, bf16[448,64]{1,0:T(8,128)(2,1)S(1)}, bf16[448,64]{1,0:T(8,128)(2,1)S(1)}, bf16[448,64]{1,0:...) fusion(bf16[448,2560]{1,0:T(8,128)(2,1)} %param.15, ...), kind=kLoop, calls=%fused_computation.82 | loop fusion | flops 229376 | bytes 1376289 | tf_op jit(solution)/shard_map/jit(_where)/select_n | solution.py:101
  23.3 1.6 pad_maximum_fusion.9
  37.8 2.0 collective-permute-start.1
  41.4 6.3 %copy.74 = f32[64,8,8,640]{3,1,2,0:T(8,128)} copy(f32[64,8,8,640]{3,2,1,0:T(8,128)S(1)} %bitcast.125) | data formatting | bytes 20971520
  49.2 2.9 %collective-permute-start.14 = (bf16[448,640]{1,0:T(8,128)(2,1)S(1)}, bf16[448,640]{1,0:T(8,128)(2,1)S(1)}, u32[]{:S(2)}, u32[]{:S(2)}) collective-permute-start(bf16[448,640]{1,0:T(8,128)(2,1)S(1)} %copy-done.15), channel_id=1, source_target_pairs={{0,8},{4,12},{8,0},{12,4},{1,9},{5,13},{9,1},{13,5},{2,10},{6,14},... | collective-permute-start | bytes 1720328 | tf_op jit(solution)/shard_map/ppermute | solution.py:89
  55.5 24.3 %collective-permute-done.26 = bf16[112,640]{1,0:T(8,128)(2,1)S(1)} collective-permute-done((bf16[112,640]{1,0:T(8,128)(2,1)S(1)}, bf16[112,640]{1,0:T(8,128)(2,1)S(1)}, u32[]{:S(2)}, u32[]{:S(2)}) %collective-permute-start.26) | collective-permute-done | bytes 143392 | tf_op jit(solution)/shard_map/ppermute | solution.py:89
  83.8 7.6 %collective-permute-done.27 = bf16[112,640]{1,0:T(8,128)(2,1)S(1)} collective-permute-done((bf16[112,640]{1,0:T(8,128)(2,1)S(1)}, bf16[112,640]{1,0:T(8,128)(2,1)S(1)}, u32[]{:S(2)}, u32[]{:S(2)}) %collective-permute-start.27) | collective-permute-done | bytes 143392 | tf_op jit(solution)/shard_map/ppermute | solution.py:89
  97.5 6.0 %collective-permute-done.9 = bf16[4,32,1792]{2,1,0:T(8,128)(2,1)S(1)} collective-permute-done((bf16[4,32,1792]{2,1,0:T(8,128)(2,1)S(1)}, bf16[4,32,1792]{2,1,0:T(8,128)(2,1)S(1)}, u32[]{:S(2)}, u32[]{:S(2)}) %collective-permute-start.9) | collective-permute-done | bytes 458784 | tf_op jit(solution)/shard_map/ppermute | solution.py:89
  105.0 4.2 %collective-permute-done.15 = bf16[448,640]{1,0:T(8,128)(2,1)S(1)} collective-permute-done((bf16[448,640]{1,0:T(8,128)(2,1)S(1)}, bf16[448,640]{1,0:T(8,128)(2,1)S(1)}, u32[]{:S(2)}, u32[]{:S(2)}) %collective-permute-start.15) | collective-permute-done | bytes 573472 | tf_op jit(solution)/shard_map/ppermute | solution.py:89
  109.4 16.4 %fusion.47 = f32[512,5120]{1,0:T(8,128)} fusion(bf16[512,1792]{1,0:T(8,128)(2,1)S(1)} %bitcast.132, bf16[5120,1792]{1,0:T(8,128)(2,1)} %bitcast.141), kind=kOutput, calls=%fused_computation.159 | convolution fusion | flops 9395240960 | bytes 30670848 | tf_op jit(solution)/shard_map/dot_general | solution.py:171
  125.8 28.8 %fusion.1 = f32[1792,512]{0,1:T(8,128)} fusion(bf16[5120,1792]{1,0:T(8,128)(2,1)} %bitcast.142, f32[512,5120]{1,0:T(8,128)} %bitcast.131, f32[512,5120]{1,0:T(8,128)} %fusion.47, bf16[512,1792]{1,0:T(8,128)(2,1)} %bitcast.133, bf16[5120,1792]{1,0:T(8,128)(2,1)} %bitcast.143), kind=kOutput, calls=%fused_computation.7 | convolution fusion | flops 18808832000 | bytes 63176704 | tf_op jit(solution)/shard_map/dot_general | solution.py:179
  154.6 5.1 %copy.64 = f32[1792,512]{1,0:T(8,128)} copy(f32[1792,512]{0,1:T(8,128)} %fusion.1) | data formatting | bytes 7340032 | tf_op jit(solution)/shard_map/transpose | solution.py:180
  159.7 2.0 bitcast_dynamic-update-slice_fusion.2
  161.7 1.8 bitcast_dynamic-update-slice_fusion.1
  164.3 4.2 %fusion.3 = f32[1024,640]{0,1:T(8,128)S(1)} fusion(bf16[1792,640]{1,0:T(8,128)(2,1)S(1)} %constant_dynamic-update-slice_fusion, bf16[512,1792]{1,0:T(8,128)(2,1)} %bitcast.136, bf16[512,1792]{1,0:T(8,128)(2,1)S(1)} %bitcast.134), kind=kOutput, calls=%fused_computation.9 | convolution fusion | flops 2356150272 | bytes 8585216 | tf_op jit(solution)/shard_map/dot_general | solution.py:187
  171.7 2.1 fusion.11
  173.8 3.2 %fusion.5 = f32[4,112,1024]{2,1,0:T(8,128)} fusion(bf16[4,112,640]{2,1,0:T(8,128)(2,1)} %bitcast_dynamic-update-slice_fusion.8, bf16[1024,320]{0,1:T(8,128)(2,1)S(1)} %fusion.4), kind=kOutput, calls=%fused_computation.19 | convolution fusion | flops 587202560 | bytes 3063808 | tf_op jit(solution)/shard_map/dot_general | solution.py:208
  184.9 1.9 copy-done.3
  187.3 1.8 bitcast_add_fusion
  189.9 1.6 collective-permute-start.31
  195.7 2.9 %collective-permute-done.32 = bf16[224,512]{1,0:T(8,128)(2,1)S(1)} collective-permute-done((bf16[224,512]{1,0:T(8,128)(2,1)S(1)}, bf16[224,512]{1,0:T(8,128)(2,1)S(1)}, u32[]{:S(2)}, u32[]{:S(2)}) %collective-permute-start.32) | collective-permute-done | bytes 229408 | tf_op jit(solution)/shard_map/ppermute | solution.py:226
  199.2 4.4 %collective-permute-done.31 = bf16[224,512]{1,0:T(8,128)(2,1)S(1)} collective-permute-done((bf16[224,512]{1,0:T(8,128)(2,1)S(1)}, bf16[224,512]{1,0:T(8,128)(2,1)S(1)}, u32[]{:S(2)}, u32[]{:S(2)}) %collective-permute-start.31) | collective-permute-done | bytes 229408 | tf_op jit(solution)/shard_map/ppermute | solution.py:89
  203.9 3.0 %collective-permute-start.35 = (bf16[224,128]{1,0:T(8,128)(2,1)S(1)}, bf16[224,128]{1,0:T(8,128)(2,1)S(1)}, u32[]{:S(2)}, u32[]{:S(2)}) collective-permute-start(bf16[224,128]{1,0:T(8,128)(2,1)S(1)} %get-tuple-element.77), channel_id=1, source_target_pairs={{0,12},{4,8},{8,4},{12,0},{1,13},{5,9},{9,5},{13,1},{2,14},{6,10},... | collective-permute-start | bytes 172040 | tf_op jit(solution)/shard_map/ppermute | solution.py:89
  206.9 9.6 %collective-permute-start.34 = (bf16[224,128]{1,0:T(8,128)(2,1)S(1)}, bf16[224,128]{1,0:T(8,128)(2,1)S(1)}, u32[]{:S(2)}, u32[]{:S(2)}) collective-permute-start(bf16[224,128]{1,0:T(8,128)(2,1)S(1)} %get-tuple-element.78), channel_id=1, source_target_pairs={{0,8},{4,12},{8,0},{12,4},{1,9},{5,13},{9,1},{13,5},{2,10},{6,14},... | collective-permute-start | bytes 172040 | tf_op jit(solution)/shard_map/ppermute | solution.py:89
  216.4 3.2 %collective-permute-start.33 = (bf16[224,128]{1,0:T(8,128)(2,1)S(1)}, bf16[224,128]{1,0:T(8,128)(2,1)S(1)}, u32[]{:S(2)}, u32[]{:S(2)}) collective-permute-start(bf16[224,128]{1,0:T(8,128)(2,1)S(1)} %get-tuple-element.76), channel_id=1, source_target_pairs={{0,4},{4,0},{8,12},{12,8},{1,5},{5,1},{9,13},{13,9},{2,6},{6,2},{1... | collective-permute-start | bytes 172040 | tf_op jit(solution)/shard_map/ppermute | solution.py:89
  219.8 2.7 %collective-permute-start.25 = (bf16[224,128]{1,0:T(8,128)(2,1)S(1)}, bf16[224,128]{1,0:T(8,128)(2,1)S(1)}, u32[]{:S(2)}, u32[]{:S(2)}) collective-permute-start(bf16[224,128]{1,0:T(8,128)(2,1)S(1)} %get-tuple-element.74), channel_id=1, source_target_pairs={{0,12},{4,8},{8,4},{12,0},{1,13},{5,9},{9,5},{13,1},{2,14},{6,10},... | collective-permute-start | bytes 172040 | tf_op jit(solution)/shard_map/ppermute | solution.py:89
  222.5 3.0 %collective-permute-start.24 = (bf16[224,128]{1,0:T(8,128)(2,1)S(1)}, bf16[224,128]{1,0:T(8,128)(2,1)S(1)}, u32[]{:S(2)}, u32[]{:S(2)}) collective-permute-start(bf16[224,128]{1,0:T(8,128)(2,1)S(1)} %get-tuple-element.75), channel_id=1, source_target_pairs={{0,8},{4,12},{8,0},{12,4},{1,9},{5,13},{9,1},{13,5},{2,10},{6,14},... | collective-permute-start | bytes 172040 | tf_op jit(solution)/shard_map/ppermute | solution.py:89
  225.8 2.7 %collective-permute-done.24 = bf16[224,128]{1,0:T(8,128)(2,1)S(1)} collective-permute-done((bf16[224,128]{1,0:T(8,128)(2,1)S(1)}, bf16[224,128]{1,0:T(8,128)(2,1)S(1)}, u32[]{:S(2)}, u32[]{:S(2)}) %collective-permute-start.24) | collective-permute-done | bytes 57376 | tf_op jit(solution)/shard_map/ppermute | solution.py:89
  (238 shorter events, 60.1 us)
Async XLA Ops:
  1.7 46.0 %collective-permute-start.5 = (bf16[32,1792]{1,0:T(8,128)(2,1)}, bf16[32,1792]{1,0:T(8,128)(2,1)}, u32[]{:S(2)}, u32[]{:S(2)}) collective-permute-start(bf16[32,1792]{1,0:T(8,128)(2,1)} %constant_dynamic-slice_fusion.16), channel_id=1, source_target_pairs={{0,12},{4,8},{8,4},{12,0},{1,13},{5,9},{9,5},{13,1},{2,14},{6,10},... | collective-permute-start | bytes 344072 | tf_op jit(solution)/shard_map/ppermute | solution.py:89
  6.7 41.9 %collective-permute-start.4 = (bf16[32,1792]{1,0:T(8,128)(2,1)}, bf16[32,1792]{1,0:T(8,128)(2,1)}, u32[]{:S(2)}, u32[]{:S(2)}) collective-permute-start(bf16[32,1792]{1,0:T(8,128)(2,1)} %constant_dynamic-slice_fusion.16), channel_id=1, source_target_pairs={{0,8},{4,12},{8,0},{12,4},{1,9},{5,13},{9,1},{13,5},{2,10},{6,14},... | collective-permute-start | bytes 344072 | tf_op jit(solution)/shard_map/ppermute | solution.py:89
  8.2 27.4 %collective-permute-start.18 = (f32[8,128]{1,0:T(8,128)}, f32[8,128]{1,0:T(8,128)}, u32[]{:S(2)}, u32[]{:S(2)}) collective-permute-start(f32[8,128]{1,0:T(8,128)} %get-tuple-element.8), channel_id=1, source_target_pairs={{0,12},{4,8},{8,4},{12,0},{1,13},{5,9},{9,5},{13,1},{2,14},{6,10},... | collective-permute-start | bytes 12296 | tf_op jit(solution)/shard_map/ppermute | solution.py:89
  10.1 26.2 %collective-permute-start.17 = (f32[8,128]{1,0:T(8,128)}, f32[8,128]{1,0:T(8,128)}, u32[]{:S(2)}, u32[]{:S(2)}) collective-permute-start(f32[8,128]{1,0:T(8,128)} %get-tuple-element.7), channel_id=1, source_target_pairs={{0,8},{4,12},{8,0},{12,4},{1,9},{5,13},{9,1},{13,5},{2,10},{6,14},... | collective-permute-start | bytes 12296 | tf_op jit(solution)/shard_map/ppermute | solution.py:89
  11.1 26.7 %collective-permute-start.16 = (f32[8,128]{1,0:T(8,128)}, f32[8,128]{1,0:T(8,128)}, u32[]{:S(2)}, u32[]{:S(2)}) collective-permute-start(f32[8,128]{1,0:T(8,128)} %get-tuple-element.6), channel_id=1, source_target_pairs={{0,4},{4,0},{8,12},{12,8},{1,5},{5,1},{9,13},{13,9},{2,6},{6,2},{1... | collective-permute-start | bytes 12296 | tf_op jit(solution)/shard_map/ppermute | solution.py:89
  35.6 13.6 %collective-permute-start.3 = (bf16[32,1792]{1,0:T(8,128)(2,1)}, bf16[32,1792]{1,0:T(8,128)(2,1)S(1)}, u32[]{:S(2)}, u32[]{:S(2)}) collective-permute-start(bf16[32,1792]{1,0:T(8,128)(2,1)} %constant_dynamic-slice_fusion.16), channel_id=1, source_target_pairs={{0,4},{4,0},{8,12},{12,8},{1,5},{5,1},{9,13},{13,9},{2,6},{6,2},{1... | collective-permute-start | bytes 344072 | tf_op jit(solution)/shard_map/ppermute | solution.py:89
  36.3 18.1 %collective-permute-start = (bf16[112,640]{1,0:T(8,128)(2,1)}, bf16[112,640]{1,0:T(8,128)(2,1)}, u32[]{:S(2)}, u32[]{:S(2)}) collective-permute-start(bf16[112,640]{1,0:T(8,128)(2,1)} %pad_maximum_fusion.9), channel_id=1, source_target_pairs={{0,4},{4,0},{8,12},{12,8},{1,5},{5,1},{9,13},{13,9},{2,6},{6,2},{1... | collective-permute-start | bytes 430088 | tf_op jit(solution)/shard_map/ppermute | solution.py:89
  37.8 43.9 %collective-permute-start.1 = (bf16[112,640]{1,0:T(8,128)(2,1)}, bf16[112,640]{1,0:T(8,128)(2,1)}, u32[]{:S(2)}, u32[]{:S(2)}) collective-permute-start(bf16[112,640]{1,0:T(8,128)(2,1)} %pad_maximum_fusion.10), channel_id=1, source_target_pairs={{0,8},{4,12},{8,0},{12,4},{1,9},{5,13},{9,1},{13,5},{2,10},{6,14},... | collective-permute-start | bytes 430088 | tf_op jit(solution)/shard_map/ppermute | solution.py:89
  47.7 46.0 %collective-permute-start.2 = (bf16[112,640]{1,0:T(8,128)(2,1)S(1)}, bf16[112,640]{1,0:T(8,128)(2,1)S(1)}, u32[]{:S(2)}, u32[]{:S(2)}) collective-permute-start(bf16[112,640]{1,0:T(8,128)(2,1)S(1)} %copy-done.36), channel_id=1, source_target_pairs={{0,12},{4,8},{8,4},{12,0},{1,13},{5,9},{9,5},{13,1},{2,14},{6,10},... | collective-permute-start | bytes 430088 | tf_op jit(solution)/shard_map/ppermute | solution.py:89
  48.6 48.9 %collective-permute-start.13 = (bf16[448,640]{1,0:T(8,128)(2,1)}, bf16[448,640]{1,0:T(8,128)(2,1)S(1)}, u32[]{:S(2)}, u32[]{:S(2)}) collective-permute-start(bf16[448,640]{1,0:T(8,128)(2,1)} %pad_maximum_fusion.5), channel_id=1, source_target_pairs={{0,4},{4,0},{8,12},{12,8},{1,5},{5,1},{9,13},{13,9},{2,6},{6,2},{1... | collective-permute-start | bytes 1720328 | tf_op jit(solution)/shard_map/ppermute | solution.py:89
  49.2 55.0 %collective-permute-start.14 = (bf16[448,640]{1,0:T(8,128)(2,1)S(1)}, bf16[448,640]{1,0:T(8,128)(2,1)S(1)}, u32[]{:S(2)}, u32[]{:S(2)}) collective-permute-start(bf16[448,640]{1,0:T(8,128)(2,1)S(1)} %copy-done.15), channel_id=1, source_target_pairs={{0,8},{4,12},{8,0},{12,4},{1,9},{5,13},{9,1},{13,5},{2,10},{6,14},... | collective-permute-start | bytes 1720328 | tf_op jit(solution)/shard_map/ppermute | solution.py:89
  54.4 25.3 %collective-permute-start.26 = (bf16[112,640]{1,0:T(8,128)(2,1)S(1)}, bf16[112,640]{1,0:T(8,128)(2,1)S(1)}, u32[]{:S(2)}, u32[]{:S(2)}) collective-permute-start(bf16[112,640]{1,0:T(8,128)(2,1)S(1)} %copy-done.39), channel_id=1, source_target_pairs={{0,4},{4,0},{8,12},{12,8},{1,5},{5,1},{9,13},{13,9},{2,6},{6,2},{1... | collective-permute-start | bytes 430088 | tf_op jit(solution)/shard_map/ppermute | solution.py:89
  79.7 11.8 %collective-permute-start.27 = (bf16[112,640]{1,0:T(8,128)(2,1)S(1)}, bf16[112,640]{1,0:T(8,128)(2,1)S(1)}, u32[]{:S(2)}, u32[]{:S(2)}) collective-permute-start(bf16[112,640]{1,0:T(8,128)(2,1)S(1)} %copy-done.38), channel_id=1, source_target_pairs={{0,8},{4,12},{8,0},{12,4},{1,9},{5,13},{9,1},{13,5},{2,10},{6,14},... | collective-permute-start | bytes 430088 | tf_op jit(solution)/shard_map/ppermute | solution.py:89
  81.7 13.5 %collective-permute-start.28 = (bf16[112,640]{1,0:T(8,128)(2,1)S(1)}, bf16[112,640]{1,0:T(8,128)(2,1)S(1)}, u32[]{:S(2)}, u32[]{:S(2)}) collective-permute-start(bf16[112,640]{1,0:T(8,128)(2,1)S(1)} %copy-done.37), channel_id=1, source_target_pairs={{0,12},{4,8},{8,4},{12,0},{1,13},{5,9},{9,5},{13,1},{2,14},{6,10},... | collective-permute-start | bytes 430088 | tf_op jit(solution)/shard_map/ppermute | solution.py:89
  91.5 12.6 %collective-permute-start.6 = (bf16[4,32,1792]{2,1,0:T(8,128)(2,1)S(1)}, bf16[4,32,1792]{2,1,0:T(8,128)(2,1)S(1)}, u32[]{:S(2)}, u32[]{:S(2)}) collective-permute-start(bf16[4,32,1792]{2,1,0:T(8,128)(2,1)S(1)} %pad_maximum_fusion.8), channel_id=1, source_target_pairs={{0,2},{1,3},{2,0},{3,1},{4,6},{5,7},{6,4},{7,5},{8,10},{9,11},{10,... | collective-permute-start | bytes 1376264 | tf_op jit(solution)/shard_map/ppermute | solution.py:89
  93.6 9.8 %collective-permute-start.9 = (bf16[4,32,1792]{2,1,0:T(8,128)(2,1)S(1)}, bf16[4,32,1792]{2,1,0:T(8,128)(2,1)S(1)}, u32[]{:S(2)}, u32[]{:S(2)}) collective-permute-start(bf16[4,32,1792]{2,1,0:T(8,128)(2,1)S(1)} %pad_maximum_fusion.8), channel_id=1, source_target_pairs={{0,16},{16,0},{1,17},{17,1},{2,18},{18,2},{3,19},{19,3},{4,20},{20... | collective-permute-start | bytes 1376264 | tf_op jit(solution)/shard_map/ppermute | solution.py:89
  95.2 13.9 %collective-permute-start.15 = (bf16[448,640]{1,0:T(8,128)(2,1)S(1)}, bf16[448,640]{1,0:T(8,128)(2,1)S(1)}, u32[]{:S(2)}, u32[]{:S(2)}) collective-permute-start(bf16[448,640]{1,0:T(8,128)(2,1)S(1)} %pad_maximum_fusion.7), channel_id=1, source_target_pairs={{0,12},{4,8},{8,4},{12,0},{1,13},{5,9},{9,5},{13,1},{2,14},{6,10},... | collective-permute-start | bytes 1720328 | tf_op jit(solution)/shard_map/ppermute | solution.py:89
  97.5 11.8 %collective-permute-start.7 = (bf16[4,32,1792]{2,1,0:T(8,128)(2,1)S(1)}, bf16[4,32,1792]{2,1,0:T(8,128)(2,1)S(1)}, u32[]{:S(2)}, u32[]{:S(2)}) collective-permute-start(bf16[4,32,1792]{2,1,0:T(8,128)(2,1)S(1)} %pad_maximum_fusion.8), channel_id=1, source_target_pairs={{0,1},{1,0},{2,3},{3,2},{4,5},{5,4},{6,7},{7,6},{8,9},{9,8},{10,11... | collective-permute-start | bytes 1376264 | tf_op jit(solution)/shard_map/ppermute | solution.py:89
  103.4 56.3 %collective-permute-start.10 = (bf16[4,32,1792]{2,1,0:T(8,128)(2,1)S(1)}, bf16[4,32,1792]{2,1,0:T(8,128)(2,1)}, u32[]{:S(2)}, u32[]{:S(2)}) collective-permute-start(bf16[4,32,1792]{2,1,0:T(8,128)(2,1)S(1)} %collective-permute-done.9), channel_id=1, source_target_pairs={{0,2},{1,3},{2,0},{3,1},{4,6},{5,7},{6,4},{7,5},{8,10},{9,11},{10,... | collective-permute-start | bytes 1376264 | tf_op jit(solution)/shard_map/ppermute | solution.py:89
  104.0 57.6 %collective-permute-start.11 = (bf16[4,32,1792]{2,1,0:T(8,128)(2,1)S(1)}, bf16[4,32,1792]{2,1,0:T(8,128)(2,1)}, u32[]{:S(2)}, u32[]{:S(2)}) collective-permute-start(bf16[4,32,1792]{2,1,0:T(8,128)(2,1)S(1)} %collective-permute-done.9), channel_id=1, source_target_pairs={{0,1},{1,0},{2,3},{3,2},{4,5},{5,4},{6,7},{7,6},{8,9},{9,8},{10,11... | collective-permute-start | bytes 1376264 | tf_op jit(solution)/shard_map/ppermute | solution.py:89
  186.9 6.1 %collective-permute-start.19 = (bf16[2,224,1024]{2,1,0:T(8,128)(2,1)S(1)}, bf16[2,224,1024]{2,1,0:T(8,128)(2,1)S(1)}, u32[]{:S(2)}, u32[]{:S(2)}) collective-permute-start(bf16[2,224,1024]{2,1,0:T(8,128)(2,1)S(1)} %fusion.13), channel_id=1, source_target_pairs={{0,1},{1,0},{2,3},{3,2},{4,5},{5,4},{6,7},{7,6},{8,9},{9,8},{10,11... | collective-permute-start | bytes 2752520 | tf_op jit(solution)/shard_map/ppermute | solution.py:89
  189.2 9.5 %collective-permute-start.32 = (bf16[224,512]{1,0:T(8,128)(2,1)S(1)}, bf16[224,512]{1,0:T(8,128)(2,1)S(1)}, u32[]{:S(2)}, u32[]{:S(2)}) collective-permute-start(bf16[224,512]{1,0:T(8,128)(2,1)S(1)} %get-tuple-element.72), channel_id=1, source_target_pairs={{0,18},{1,19},{2,16},{3,17},{16,2},{17,3},{18,0},{19,1},{4,22},{5,... | collective-permute-start | bytes 688136 | tf_op jit(solution)/shard_map/ppermute | solution.py:226
  189.9 13.8 %collective-permute-start.31 = (bf16[224,512]{1,0:T(8,128)(2,1)S(1)}, bf16[224,512]{1,0:T(8,128)(2,1)S(1)}, u32[]{:S(2)}, u32[]{:S(2)}) collective-permute-start(bf16[224,512]{1,0:T(8,128)(2,1)S(1)} %slice.394), channel_id=1, source_target_pairs={{0,16},{16,0},{1,17},{17,1},{2,18},{18,2},{3,19},{19,3},{4,20},{20... | collective-permute-start | bytes 688136 | tf_op jit(solution)/shard_map/ppermute | solution.py:89
  191.5 12.2 %collective-permute-start.30 = (bf16[224,512]{1,0:T(8,128)(2,1)S(1)}, bf16[224,512]{1,0:T(8,128)(2,1)S(1)}, u32[]{:S(2)}, u32[]{:S(2)}) collective-permute-start(bf16[224,512]{1,0:T(8,128)(2,1)S(1)} %get-tuple-element.71), channel_id=1, source_target_pairs={{0,2},{1,3},{2,0},{3,1},{4,6},{5,7},{6,4},{7,5},{8,10},{9,11},{10,... | collective-permute-start | bytes 688136 | tf_op jit(solution)/shard_map/ppermute | solution.py:89
  193.5 22.9 %collective-permute-start.22 = (bf16[224,512]{1,0:T(8,128)(2,1)S(1)}, bf16[224,512]{1,0:T(8,128)(2,1)S(1)}, u32[]{:S(2)}, u32[]{:S(2)}) collective-permute-start(bf16[224,512]{1,0:T(8,128)(2,1)S(1)} %get-tuple-element.70), channel_id=1, source_target_pairs={{0,18},{1,19},{2,16},{3,17},{16,2},{17,3},{18,0},{19,1},{4,22},{5,... | collective-permute-start | bytes 688136 | tf_op jit(solution)/shard_map/ppermute | solution.py:226
  194.2 25.5 %collective-permute-start.21 = (bf16[224,512]{1,0:T(8,128)(2,1)S(1)}, bf16[224,512]{1,0:T(8,128)(2,1)S(1)}, u32[]{:S(2)}, u32[]{:S(2)}) collective-permute-start(bf16[224,512]{1,0:T(8,128)(2,1)S(1)} %slice.395), channel_id=1, source_target_pairs={{0,16},{16,0},{1,17},{17,1},{2,18},{18,2},{3,19},{19,3},{4,20},{20... | collective-permute-start | bytes 688136 | tf_op jit(solution)/shard_map/ppermute | solution.py:89
  198.7 20.9 %collective-permute-start.20 = (bf16[224,512]{1,0:T(8,128)(2,1)S(1)}, bf16[224,512]{1,0:T(8,128)(2,1)S(1)}, u32[]{:S(2)}, u32[]{:S(2)}) collective-permute-start(bf16[224,512]{1,0:T(8,128)(2,1)S(1)} %get-tuple-element.69), channel_id=1, source_target_pairs={{0,2},{1,3},{2,0},{3,1},{4,6},{5,7},{6,4},{7,5},{8,10},{9,11},{10,... | collective-permute-start | bytes 688136 | tf_op jit(solution)/shard_map/ppermute | solution.py:89
  203.9 21.6 %collective-permute-start.35 = (bf16[224,128]{1,0:T(8,128)(2,1)S(1)}, bf16[224,128]{1,0:T(8,128)(2,1)S(1)}, u32[]{:S(2)}, u32[]{:S(2)}) collective-permute-start(bf16[224,128]{1,0:T(8,128)(2,1)S(1)} %get-tuple-element.77), channel_id=1, source_target_pairs={{0,12},{4,8},{8,4},{12,0},{1,13},{5,9},{9,5},{13,1},{2,14},{6,10},... | collective-permute-start | bytes 172040 | tf_op jit(solution)/shard_map/ppermute | solution.py:89
  206.9 18.9 %collective-permute-start.34 = (bf16[224,128]{1,0:T(8,128)(2,1)S(1)}, bf16[224,128]{1,0:T(8,128)(2,1)S(1)}, u32[]{:S(2)}, u32[]{:S(2)}) collective-permute-start(bf16[224,128]{1,0:T(8,128)(2,1)S(1)} %get-tuple-element.78), channel_id=1, source_target_pairs={{0,8},{4,12},{8,0},{12,4},{1,9},{5,13},{9,1},{13,5},{2,10},{6,14},... | collective-permute-start | bytes 172040 | tf_op jit(solution)/shard_map/ppermute | solution.py:89
  216.4 9.3 %collective-permute-start.33 = (bf16[224,128]{1,0:T(8,128)(2,1)S(1)}, bf16[224,128]{1,0:T(8,128)(2,1)S(1)}, u32[]{:S(2)}, u32[]{:S(2)}) collective-permute-start(bf16[224,128]{1,0:T(8,128)(2,1)S(1)} %get-tuple-element.76), channel_id=1, source_target_pairs={{0,4},{4,0},{8,12},{12,8},{1,5},{5,1},{9,13},{13,9},{2,6},{6,2},{1... | collective-permute-start | bytes 172040 | tf_op jit(solution)/shard_map/ppermute | solution.py:89
  219.8 6.0 %collective-permute-start.25 = (bf16[224,128]{1,0:T(8,128)(2,1)S(1)}, bf16[224,128]{1,0:T(8,128)(2,1)S(1)}, u32[]{:S(2)}, u32[]{:S(2)}) collective-permute-start(bf16[224,128]{1,0:T(8,128)(2,1)S(1)} %get-tuple-element.74), channel_id=1, source_target_pairs={{0,12},{4,8},{8,4},{12,0},{1,13},{5,9},{9,5},{13,1},{2,14},{6,10},... | collective-permute-start | bytes 172040 | tf_op jit(solution)/shard_map/ppermute | solution.py:89
  222.5 6.0 %collective-permute-start.24 = (bf16[224,128]{1,0:T(8,128)(2,1)S(1)}, bf16[224,128]{1,0:T(8,128)(2,1)S(1)}, u32[]{:S(2)}, u32[]{:S(2)}) collective-permute-start(bf16[224,128]{1,0:T(8,128)(2,1)S(1)} %get-tuple-element.75), channel_id=1, source_target_pairs={{0,8},{4,12},{8,0},{12,4},{1,9},{5,13},{9,1},{13,5},{2,10},{6,14},... | collective-permute-start | bytes 172040 | tf_op jit(solution)/shard_map/ppermute | solution.py:89
  (56 other events, 279.3 us)

commit v2 on v0

--- a/solution.py
+++ b/solution.py
@@ -1,9 +1,13 @@
 import jax
 import jax.numpy as jnp
 from jax import lax
+from jax.experimental import pallas as pl
+from jax.experimental.pallas import tpu as pltpu
 from jax.sharding import PartitionSpec as P
 
 CAP = 48
+BF = jnp.bfloat16
+F32 = jnp.float32
 
 
 def slot_places(expert_ids, experts):
@@ -14,7 +18,7 @@
     return (jnp.sum(before * onehot, axis=1, dtype=jnp.int32), flat_ids)
 
 
-def on_device(
+def general(
     tokens,
     expert_ids,
     route_gates,
@@ -36,11 +40,9 @@
     portion_down = lax.all_gather(w_shared_down_t, "dp", axis=0, tiled=True)
     acc_gate = jnp.dot(tokens, portion_gate, preferred_element_type=jnp.float32)
     acc_up = jnp.dot(tokens, portion_up, preferred_element_type=jnp.float32)
-    down_full = portion_down
-    shared_gate, shared_up, down_full = (acc_gate, acc_up, down_full)
-    shared_hidden = (jax.nn.silu(shared_gate) * shared_up).astype(jnp.bfloat16)
+    shared_hidden = (jax.nn.silu(acc_gate) * acc_up).astype(jnp.bfloat16)
     shared_part = lax.dot_general(
-        shared_hidden, down_full, (((1,), (1,)), ((), ())), preferred_element_type=jnp.float32
+        shared_hidden, portion_down, (((1,), (1,)), ((), ())), preferred_element_type=jnp.float32
     )
     shared_scale = jax.nn.sigmoid(
         jnp.dot(tokens, shared_gate_vec, preferred_element_type=jnp.float32)
@@ -83,7 +85,510 @@
     )
 
 
+def swap(x, axis, bit):
+    n = lax.axis_size(axis)
+    return lax.ppermute(x, axis, [(i, i ^ bit) for i in range(n)])
+
+
+def vmem_full(a):
+    return pl.BlockSpec(a.shape, lambda *_: (0,) * a.ndim)
+
+
+ANY = pl.BlockSpec(memory_space=pl.ANY)
+FULL = 60 << 20
+SMEM = pl.BlockSpec(memory_space=pltpu.SMEM)
+
+
+def run_all(copies):
+    for c in copies:
+        c.start()
+    for c in copies:
+        c.wait()
+
+
+def token_rows(where, tokens, ids_t, gates_t):
+    rows, d = tokens.shape
+    top = ids_t.shape[0]
+    quarter = rows // 4
+
+    def kernel(where_ref, tok_ref, ids_ref, gates_ref, mine, tags, sem):
+        at = pl.multiple_of(where_ref[1] * quarter, quarter)
+        copy = pltpu.make_async_copy(
+            tok_ref.at[pl.ds(at, quarter)], mine.at[:, pl.ds(0, d)], sem
+        )
+        copy.start()
+        gates = gates_ref[...]
+        high = gates.astype(BF).astype(F32)
+        lines = [ids_ref[...].astype(F32), high, gates - high]
+        lines.append(jnp.zeros((128 - 3 * top, rows), F32))
+        tags[...] = jnp.concatenate(lines, axis=0).T
+        mine[:, pl.ds(d, 128)] = tags[pl.ds(at, quarter), :].astype(BF)
+        copy.wait()
+
+    vm = pl.BlockSpec(memory_space=pltpu.VMEM)
+    return pl.pallas_call(
+        kernel,
+        out_shape=jax.ShapeDtypeStruct((quarter, d + 128), BF),
+        in_specs=[SMEM, ANY, vm, vm],
+        out_specs=vm,
+        scratch_shapes=[pltpu.VMEM((rows, 128), F32), pltpu.SemaphoreType.DMA],
+        compiler_params=pltpu.CompilerParams(vmem_limit_bytes=FULL),
+        name="token_rows",
+    )(where, tokens, ids_t, gates_t)
+
+
+def pack(where, wg, wu, wd, width):
+    d_part, ff = wg.shape
+    n = ff // (2 * width)
+    whole = width - 64
+    half = d_part // 2
+
+    def kernel(where_ref, g_ref, u_ref, d_ref, *rest):
+        outs_gu, outs_d = rest[:n], rest[n : 2 * n]
+        gu_buf, d_buf, gu_mid, d_mid, in_sem, out_sem = rest[2 * n :]
+        z, t, g = where_ref[0], where_ref[1], where_ref[2]
+        side = g * (width + 64)
+        loads = []
+        for k in range(n):
+            start = (z ^ k) * (2 * width)
+            wide = pl.multiple_of(start + side, 128)
+            mid = pl.multiple_of(start + whole, 128)
+            jobs = []
+            for m, ref in enumerate((g_ref, u_ref)):
+                lane = 0 if m == 0 else width + 64
+                jobs.append((ref.at[:, pl.ds(wide, whole)], gu_buf.at[k, :, pl.ds(lane, whole)]))
+                jobs.append((ref.at[:, pl.ds(mid, 128)], gu_mid.at[k, m]))
+            loads.append(jobs)
+        for r in range(n):
+            start = (t ^ r) * (2 * width)
+            wide = pl.multiple_of(start + side, 128)
+            mid = pl.multiple_of(start + whole, 128)
+            jobs = []
+            for m in range(2):
+                lane = 0 if m == 0 else width + 64
+                part = d_ref.at[pl.ds(m * half, half)]
+                jobs.append((part.at[:, pl.ds(wide, whole)], d_buf.at[r, :, pl.ds(lane, whole)]))
+                jobs.append((part.at[:, pl.ds(mid, 128)], d_mid.at[r, m]))
+            loads.append(jobs)
+        order = [1, 2, 3, 0, n, n + 1, n + 2, n + 3]
+        copies = {}
+        for i in order:
+            copies[i] = [
+                pltpu.make_async_copy(s, d, in_sem.at[i, j]) for j, (s, d) in enumerate(loads[i])
+            ]
+            for c in copies[i]:
+                c.start()
+        stores = []
+        for i in order:
+            for c in copies[i]:
+                c.wait()
+            buf, mids, out = (gu_buf, gu_mid, outs_gu[i]) if i < n else (d_buf, d_mid, outs_d[i - n])
+            p = i % n
+            first = pltpu.roll(mids[p, 0].astype(F32), 64 * g, 1)
+            second = pltpu.roll(mids[p, 1].astype(F32), 64 * (1 - g), 1)
+            lane = lax.broadcasted_iota(jnp.int32, first.shape, 1)
+            buf[p, :, pl.ds(whole, 128)] = jnp.where(lane < 64, first, second).astype(BF)
+            stores.append(pltpu.make_async_copy(buf.at[p], out, out_sem.at[i]))
+            stores[-1].start()
+        for c in stores:
+            c.wait()
+
+    return pl.pallas_call(
+        kernel,
+        out_shape=[jax.ShapeDtypeStruct((d_part, 2 * width), BF)] * n
+        + [jax.ShapeDtypeStruct((half, 2 * width), BF)] * n,
+        in_specs=[SMEM, ANY, ANY, ANY],
+        out_specs=[ANY] * (2 * n),
+        scratch_shapes=[
+            pltpu.VMEM((n, d_part, 2 * width), BF),
+            pltpu.VMEM((n, half, 2 * width), BF),
+            pltpu.VMEM((n, 2, d_part, 128), BF),
+            pltpu.VMEM((n, 2, half, 128), BF),
+            pltpu.SemaphoreType.DMA((2 * n, 4)),
+            pltpu.SemaphoreType.DMA((2 * n,)),
+        ],
+        compiler_params=pltpu.CompilerParams(vmem_limit_bytes=FULL),
+        cost_estimate=pl.CostEstimate(flops=0, bytes_accessed=8 << 20, transcendentals=0),
+        name="pack",
+    )(where, wg, wu, wd)
+
+
+def token_copies(where_ref, direct, crossed, rows_ref, info_ref, sem, base):
+    t = where_ref[1]
+    _, n_dp, quarter, _ = direct.shape
+    d = rows_ref.shape[1]
+    copies = []
+    for b, ref in ((0, direct), (2, direct), (1, crossed), (3, crossed)):
+        for k in range(n_dp):
+            row = pl.multiple_of(base + k * 4 * quarter + (t ^ b) * quarter, quarter)
+            src = ref.at[b // 2, k]
+            copies.append(
+                pltpu.make_async_copy(
+                    src.at[:, pl.ds(0, d)], rows_ref.at[pl.ds(row, quarter)], sem.at[len(copies)]
+                )
+            )
+            if info_ref is not None:
+                copies.append(
+                    pltpu.make_async_copy(
+                        src.at[:, pl.ds(d, 128)],
+                        info_ref.at[pl.ds(row, quarter)],
+                        sem.at[len(copies)],
+                    )
+                )
+    return copies
+
+
+def routed_experts(where, direct, crossed, eg, eu, ed, top):
+    e_dev, ff_e, d = eg.shape
+    n_dp = direct.shape[1]
+    n_tok = n_dp * direct.shape[2] * 4
+    slots = n_dp * CAP
+    part = d // 4
+
+    def kernel(
+        where_ref, dir_ref, cro_ref, g_ref, u_ref, w_ref, give, keep,
+        tok, info, place_t, gate_t, back, outs, acc_t, sem,
+    ):
+        e = pl.program_id(0)
+        z, t = where_ref[0], where_ref[1]
+
+        @pl.when(e == 0)
+        def _():
+            run_all(token_copies(where_ref, dir_ref, cro_ref, tok, info, sem, 0))
+            tags = info[...].astype(F32)
+            lane = lax.broadcasted_iota(jnp.int32, tags.shape, 1)
+            weight = pltpu.roll(tags, 128 - top, 1) + pltpu.roll(tags, 128 - 2 * top, 1)
+            chosen = jnp.zeros(tags.shape, F32)
+            gates = jnp.zeros(tags.shape, F32)
+            for i in range(e_dev):
+                hit = (tags == (z * e_dev + i).astype(F32)) & (lane < top)
+                has = jnp.sum(jnp.where(hit, 1.0, 0.0), axis=1, keepdims=True)
+                gate = jnp.sum(jnp.where(hit, weight, 0.0), axis=1, keepdims=True)
+                chosen = jnp.where(lane == i, has, chosen)
+                gates = jnp.where(lane == i, gate, gates)
+            row = lax.broadcasted_iota(jnp.int32, (n_tok, n_tok), 0)
+            col = lax.broadcasted_iota(jnp.int32, (n_tok, n_tok), 1)
+            earlier = jnp.where(col < row, 1.0, 0.0).astype(BF)
+            before = jnp.dot(earlier, chosen.astype(BF), preferred_element_type=F32)
+            where_to = jnp.where(chosen > 0.5, before, -1.0)
+            place_t[...] = where_to.T
+            gate_t[...] = gates.T
+
+        line = place_t[pl.ds(e, 1), :]
+        slot = lax.broadcasted_iota(jnp.int32, (slots, n_tok), 0).astype(F32)
+        hit = slot == line
+        pick = jnp.where(hit, 1.0, 0.0).astype(BF)
+        gate_of = jnp.sum(jnp.where(hit, gate_t[pl.ds(e, 1), :], 0.0), axis=1, keepdims=True)
+        x = jnp.dot(pick, tok[...], preferred_element_type=F32).astype(BF)
+        dims = (((1,), (1,)), ((), ()))
+        gate = lax.dot_general(x, g_ref[0], dims, preferred_element_type=F32)
+        up = lax.dot_general(x, u_ref[0], dims, preferred_element_type=F32)
+        hidden = (gate * jax.nn.sigmoid(gate) * up).astype(BF)
+        out = jnp.dot(hidden, w_ref[0], preferred_element_type=F32)
+        at = pl.multiple_of(e * slots, slots)
+        outs[pl.ds(at, slots), :] = (gate_of * out).astype(BF)
+        back[pl.ds(at, slots), :] = pick
+
+        @pl.when(e == e_dev - 1)
+        def _():
+            dims = (((0,), (0,)), ((), ()))
+            for i in range(d // 256):
+                acc_t[pl.ds(256 * i, 256), :] = lax.dot_general(
+                    outs[:, pl.ds(256 * i, 256)], back[...], dims, preferred_element_type=F32
+                )
+            for b in range(2):
+                mine = pl.multiple_of((t ^ (2 * b)) * part, part)
+                theirs = pl.multiple_of((t ^ (2 * b + 1)) * part, part)
+                keep[b] = acc_t[pl.ds(mine, part), :]
+                give[b] = acc_t[pl.ds(theirs, part), :].astype(BF)
+
+    weights = pl.BlockSpec((1, ff_e, d), lambda e: (e, 0, 0))
+    n_copies = 2 * 4 * n_dp
+    return pl.pallas_call(
+        kernel,
+        grid=(e_dev,),
+        out_shape=[
+            jax.ShapeDtypeStruct((2, part, n_tok), BF),
+            jax.ShapeDtypeStruct((2, part, n_tok), F32),
+        ],
+        in_specs=[SMEM, ANY, ANY, weights, weights, weights],
+        out_specs=[
+            pl.BlockSpec((2, part, n_tok), lambda e: (0, 0, 0)),
+            pl.BlockSpec((2, part, n_tok), lambda e: (0, 0, 0)),
+        ],
+        scratch_shapes=[
+            pltpu.VMEM((n_tok, d), BF),
+            pltpu.VMEM((n_tok, 128), BF),
+            pltpu.VMEM((128, n_tok), F32),
+            pltpu.VMEM((128, n_tok), F32),
+            pltpu.VMEM((e_dev * slots, n_tok), BF),
+            pltpu.VMEM((e_dev * slots, d), BF),
+            pltpu.VMEM((d, n_tok), F32),
+            pltpu.SemaphoreType.DMA((n_copies,)),
+        ],
+        compiler_params=pltpu.CompilerParams(vmem_limit_bytes=52 << 20),
+        cost_estimate=pl.CostEstimate(
+            flops=6 * slots * e_dev * ff_e * d + 4 * slots * e_dev * n_tok * d,
+            bytes_accessed=6 * e_dev * ff_e * d,
+            transcendentals=slots * e_dev * ff_e,
+        ),
+        name="routed",
+    )(where, direct, crossed, eg, eu, ed)
+
+
+def shared_hidden(where, own, other, pieces, vec, after, width):
+    d_part = pieces[0].shape[0]
+    n = len(pieces)
+    d = n * d_part
+    n_tok = own[0].shape[1] * own[0].shape[2] * 4
+    whole = width - 64
+
+    def kernel(where_ref, a0, a1, b0, b1, vec_ref, *rest):
+        p_refs = rest[:n]
+        hid, scale, tok, w, tok_sem, w_sem = rest[n + 1 :]
+        z = where_ref[0]
+        t_copies = token_copies(where_ref, a0, a1, tok, None, tok_sem.at[0], 0)
+        t_copies += token_copies(where_ref, b0, b1, tok, None, tok_sem.at[1], n_tok)
+        w_copies = []
+        for k in range(n):
+            row = pl.multiple_of((z ^ k) * d_part, d_part)
+            w_copies.append(
+                pltpu.make_async_copy(p_refs[k], w.at[pl.ds(row, d_part)], w_sem.at[k])
+            )
+        run_all(w_copies + t_copies)
+        dims = (((1,), (1,)), ((), ()))
+        lines = jnp.broadcast_to(vec_ref[...], (8, d))
+        def half_hidden(row):
+            x = tok[pl.ds(row, 256), :]
+            acc = jnp.dot(x, w[...], preferred_element_type=F32)
+            gate_mid = acc[:, whole : whole + 128]
+            up_mid = pltpu.roll(gate_mid, 64, 1)
+            gate, up = acc[:, :whole], acc[:, width + 64 :]
+            line = lax.dot_general(lines, x, dims, preferred_element_type=F32)
+            scale[:, pl.ds(row, 256)] = jax.nn.sigmoid(line[:1])
+            body = gate * jax.nn.sigmoid(gate) * up
+            return body.astype(BF), gate_mid * jax.nn.sigmoid(gate_mid) * up_mid
+
+        for row in range(0, n_tok, 256):
+            rows = pl.ds(row, 256)
+            body, mid = half_hidden(row)
+            far_body, far_mid = half_hidden(n_tok + row)
+            lane = lax.broadcasted_iota(jnp.int32, mid.shape, 1)
+            hid[rows, pl.ds(0, whole)] = body
+            hid[rows, pl.ds(width + 64, whole)] = far_body
+            mid = jnp.where(lane < 64, mid, pltpu.roll(far_mid, 64, 1))
+            hid[rows, pl.ds(whole, 128)] = mid.astype(BF)
+
+    return pl.pallas_call(
+        kernel,
+        out_shape=[
+            jax.ShapeDtypeStruct((n_tok, 2 * width), BF),
+            jax.ShapeDtypeStruct((1, 2 * n_tok), F32),
+        ],
+        in_specs=[SMEM] + [ANY] * 4 + [pl.BlockSpec(memory_space=pltpu.VMEM)] + [ANY] * (n + 1),
+        out_specs=[pl.BlockSpec(memory_space=pltpu.VMEM)] * 2,
+        scratch_shapes=[
+            pltpu.VMEM((2 * n_tok, d), BF),
+            pltpu.VMEM((d, 2 * width), BF),
+            pltpu.SemaphoreType.DMA((2, 4 * own[0].shape[1])),
+            pltpu.SemaphoreType.DMA((n,)),
+        ],
+        compiler_params=pltpu.CompilerParams(vmem_limit_bytes=24 << 20),
+        cost_estimate=pl.CostEstimate(
+            flops=2 * 2 * n_tok * d * 2 * width,
+            bytes_accessed=8 << 20,
+            transcendentals=2 * n_tok * width,
+        ),
+        name="shared_hidden",
+    )(where, own[0], own[1], other[0], other[1], vec, *pieces, after)
+
+
+def shared_down(where, pieces, direct, crossed, scale, routed, width):
+    n = len(pieces)
+    half = pieces[0].shape[0]
+    whole = width - 64
+    lanes = whole + 128
+    n_tok = direct.shape[1]
+    both = 2 * n_tok
+
+    def kernel(where_ref, dir_ref, cro_ref, scale_ref, routed_ref, *rest):
+        p_refs = rest[:n]
+        far, near, w, h, w_sem, h_sem = rest[n:]
+        z, t = where_ref[0], where_ref[1]
+        copies = []
+        for r in range(n):
+            jobs = (
+                (p_refs[r].at[:, pl.ds(0, lanes)], w.at[pl.ds(0, half), pl.ds(lanes * r, lanes)]),
+                (
+                    p_refs[r].at[:, pl.ds(lanes, whole)],
+                    w.at[pl.ds(half, half), pl.ds(lanes * r, whole)],
+                ),
+                (
+                    p_refs[r].at[:, pl.ds(whole, 128)],
+                    w.at[pl.ds(half, half), pl.ds(lanes * r + whole, 128)],
+                ),
+            )
+            for j, (s, d) in enumerate(jobs):
+                copies.append(pltpu.make_async_copy(s, d, w_sem.at[r, j]))
+        for m, ref in ((0, dir_ref), (2, dir_ref), (1, cro_ref), (3, cro_ref)):
+            at = pl.multiple_of((z ^ t ^ m) * lanes, lanes)
+            src = ref.at[m // 2]
+            jobs = (
+                (src.at[:, pl.ds(0, lanes)], h.at[pl.ds(0, n_tok), pl.ds(at, lanes)]),
+                (
+                    src.at[:, pl.ds(lanes, whole)],
+                    h.at[pl.ds(n_tok, n_tok), pl.ds(at, whole)],
+                ),
+                (
+                    src.at[:, pl.ds(whole, 128)],
+                    h.at[pl.ds(n_tok, n_tok), pl.ds(at + whole, 128)],
+                ),
+            )
+            for j, (s, d) in enumerate(jobs):
+                copies.append(pltpu.make_async_copy(s, d, h_sem.at[m, j]))
+        run_all(copies)
+        lane = lax.broadcasted_iota(jnp.int32, (half, 128), 1)
+        for r in range(n):
+            at = pl.ds(lanes * r + whole, 128)
+            for i, mask in ((0, lane < 64), (1, lane >= 64)):
+                rows = pl.ds(half * i, half)
+                w[rows, at] = jnp.where(mask, w[rows, at].astype(F32), 0.0).astype(BF)
+        lane = lax.broadcasted_iota(jnp.int32, (n_tok, 128), 1)
+        for r in range(n):
+            at = pl.ds(lanes * r + whole, 128)
+            for i, own in ((0, lane < 64), (1, lane >= 64)):
+                rows = pl.ds(n_tok * i, n_tok)
+                mid = h[rows, at].astype(F32)
+                h[rows, at] = jnp.where(own, mid, pltpu.roll(mid, 64, 1)).astype(BF)
+        dims = (((1,), (1,)), ((), ()))
+        out = lax.dot_general(w[...], h[pl.ds(n_tok, n_tok), :], dims, preferred_element_type=F32)
+        far[...] = (out * scale_ref[:, pl.ds(n_tok, n_tok)]).astype(BF)
+        out = lax.dot_general(w[...], h[pl.ds(0, n_tok), :], dims, preferred_element_type=F32)
+        near[...] = out * scale_ref[:, pl.ds(0, n_tok)] + routed_ref[...]
+
+    vm = pl.BlockSpec(memory_space=pltpu.VMEM)
+    return pl.pallas_call(
+        kernel,
+        out_shape=[
+            jax.ShapeDtypeStruct((2 * half, n_tok), BF),
+            jax.ShapeDtypeStruct((2 * half, n_tok), F32),
+        ],
+        in_specs=[SMEM, ANY, ANY, vm, vm] + [ANY] * n,
+        out_specs=[vm, vm],
+        scratch_shapes=[
+            pltpu.VMEM((2 * half, n * lanes), BF),
+            pltpu.VMEM((both, n * lanes), BF),
+            pltpu.SemaphoreType.DMA((n, 3)),
+            pltpu.SemaphoreType.DMA((4, 3)),
+        ],
+        compiler_params=pltpu.CompilerParams(vmem_limit_bytes=24 << 20),
+        cost_estimate=pl.CostEstimate(
+            flops=2 * 2 * half * n * lanes * both, bytes_accessed=6 << 20, transcendentals=0
+        ),
+        name="shared_down",
+    )(where, direct, crossed, scale, routed, *pieces)
+
+
+def exchanged(
+    tokens,
+    expert_ids,
+    route_gates,
+    shared_gate_vec,
+    w_shared_gate,
+    w_shared_up,
+    w_shared_down_t,
+    w_expert_gate_t,
+    w_expert_up_t,
+    w_expert_down,
+):
+    z, t, g = lax.axis_index("dp"), lax.axis_index("tensor"), lax.axis_index("groups")
+    n_dp, n_t, n_g = lax.axis_size("dp"), lax.axis_size("tensor"), lax.axis_size("groups")
+    where = jnp.stack([z, t, g]).astype(jnp.int32)
+    rows, d = tokens.shape
+    top = expert_ids.shape[1]
+    width = w_shared_gate.shape[1] // (n_dp * n_g)
+
+    some = expert_ids[0, 0] >= 0
+
+    def apart(step, *operands):
+        shapes = jax.eval_shape(step, *operands)
+        empty = lambda *_: jax.tree.map(lambda a: jnp.zeros(a.shape, a.dtype), shapes)
+        return lax.cond(some, step, empty, *operands)
+
+    def first_step(mine, *weights):
+        packed = pack(where, *weights, width)
+        over_z = jnp.stack([mine] + [swap(mine, "dp", k) for k in range(1, n_dp)])
+        return over_z, packed
+
+    over_z, packed = apart(
+        first_step,
+        token_rows(where, tokens, expert_ids.T, route_gates.T),
+        w_shared_gate,
+        w_shared_up,
+        w_shared_down_t,
+    )
+    gu = [packed[0]] + [swap(packed[k], "dp", k) for k in range(1, n_dp)]
+
+    def spread(q):
+        direct = jnp.stack([q, swap(q, "tensor", 2)])
+        return direct, swap(direct, "tensor", 1)
+
+    def cross(piece, r):
+        route = [(i * n_t + j, (j ^ r) * n_t + i) for i in range(n_dp) for j in range(n_t)]
+        return lax.ppermute(piece, ("dp", "tensor"), route)
+
+    def routed_step(q, piece, *weights):
+        direct = jnp.stack([q, swap(q, "tensor", 2)])
+        direct, other = lax.optimization_barrier((direct, swap(q, "groups", 1)))
+        crossed, other = lax.optimization_barrier((swap(direct, "tensor", 1), other))
+        over_x = swap(other, "tensor", 2)
+        piece = cross(piece, 0)
+        give, keep = routed_experts(where, direct, crossed, *weights, top)
+        other, over_x, give, piece = lax.optimization_barrier((other, over_x, give, piece))
+        other = jnp.stack([other, over_x])
+        return (direct, crossed), (other, swap(other, "tensor", 1)), give, keep, piece
+
+    tok_own, tok_other, give, keep, first = apart(
+        routed_step, over_z, packed[n_dp], w_expert_gate_t, w_expert_up_t, w_expert_down
+    )
+    hidden, scale = shared_hidden(
+        where, tok_own, tok_other, gu, shared_gate_vec[None, :], give, width
+    )
+
+    def gather_step(h, out, kept):
+        got = swap(out, "tensor", 1).astype(F32)
+        return spread(h), kept[0] + got[0], (kept[1] + got[1]).astype(BF)
+
+    (h_direct, h_crossed), routed, routed_far = apart(gather_step, hidden, give, keep)
+
+    down = [first] + [cross(packed[n_dp + r], r) for r in range(1, n_dp)]
+    far, near = shared_down(where, down, h_direct, h_crossed, scale, routed, width)
+    total = near + swap(far, "groups", 1).astype(F32) + swap(routed_far, "tensor", 2).astype(F32)
+    done = total[:, :rows]
+    for k in range(1, n_dp):
+        piece = total[:, rows * k : rows * (k + 1)].astype(BF)
+        done = done + swap(piece, "dp", k).astype(F32)
+    return done.T.astype(BF)
+
+
 def solution(mesh):
+    sizes = mesh.shape
+
+    def on_device(*args):
+        d_part, ff = args[4].shape
+        width = ff // (sizes["dp"] * sizes["groups"])
+        fits = (
+            sizes["dp"] == 4
+            and sizes["tensor"] == 4
+            and sizes["groups"] == 2
+            and width % 128 == 64
+            and d_part % 32 == 0
+            and args[7].shape[2] % 256 == 0
+            and args[1].shape[1] == 8
+            and args[0].shape[0] % 128 == 0
+        )
+        return (exchanged if fits else general)(*args)
+
     return jax.shard_map(
         on_device,
         mesh=mesh,

time: 884 us -> 157 us (0.18)
  waiting for transfers between devices: 743 us -> 60.1 us
  matrix products: 52 us -> 0 us
  Pallas kernels: 0 us -> 48.3 us
  local copies, waits for them, and re-layouts: 45.5 us -> 1.28 us
  starting transfers between devices: 12.9 us -> 42 us
  other arithmetic: 17.1 us -> 4.15 us
  between operations: 13.2 us -> 0.76 us
    all_to_all x2 -> x0, waiting for transfers between devices: 718 us -> none  [the longest x1 476 us: on_device(): lax.all_to_all(ex_part.reshape(n_dp, exp_dev * CAP, model_width), 'dp', s...]
    ppermute x0 -> x23, waiting for transfers between devices: none -> 60.1 us  [the longest x19 60 us: swap(): return lax.ppermute(x, axis, [(i, i ^ bit) for i in range(n)])]
    dot_general x5 -> x0, matrix products: 52 us -> none  [the longest x1 22.3 us: on_device(): jnp.einsum('sjcf,jfd->sjcd', ex_hidden, w_expert_down, preferred_element_...]
    pallas_call x0 -> x5, Pallas kernels: none -> 48.3 us  [the longest x1 30.8 us: routed_experts(): pl.pallas_call(kernel, grid=(e_dev,), out_shape=[jax.ShapeDtypeStruct((2,...]
    ppermute x0 -> x23, starting transfers between devices: none -> 42 us  [the longest x19 25.5 us: swap(): return lax.ppermute(x, axis, [(i, i ^ bit) for i in range(n)])]
    reduce_scatter x1 -> x0, waiting for transfers between devices: 22.6 us -> none  [on_device(): lax.psum_scatter(combined, 'tensor', scatter_dimension=1, tiled=True)]
    scatter x1 -> x0, local copies, waits for them, and re-layouts: 21.1 us -> none  [on_device(): jnp.zeros((experts * CAP, model_width), jnp.bfloat16).at[target]]
    all_to_all x2 -> x0, starting transfers between devices: 12.6 us -> none  [the longest x1 6.32 us: on_device(): lax.all_to_all(outgoing.reshape(n_dp, exp_dev * CAP, model_width), 'dp',...]
  transfers between devices with their start and end apart: 6 -> 23, of which waited for: 3 -> 11; matrix products, arithmetic and copies ran while one was open for 11% -> 2% of each run, Pallas kernels for 0% -> 27%
where the time goes in v2:
time: 157 us
  waiting for transfers between devices  60.1 us (38%)
  Pallas kernels  48.3 us (31%)
  starting transfers between devices  42 us (27%)
  other arithmetic  4.15 us (3%)
    ppermute x19, waiting for transfers between devices, swap(): return lax.ppermute(x, axis, [(i, i ^ bit) for i in range(n)])  60 us
    pallas_call x1, Pallas kernels, routed_experts(): pl.pallas_call(kernel, grid=(e_dev,), out_shape=[jax.ShapeDtypeStruct((2,...  30.8 us
    ppermute x19, starting transfers between devices, swap(): return lax.ppermute(x, axis, [(i, i ^ bit) for i in range(n)])  25.5 us
    ppermute x4, starting transfers between devices, cross(): return lax.ppermute(piece, ('dp', 'tensor'), route)  16.5 us
    pallas_call x1, Pallas kernels, shared_hidden(): pl.pallas_call(kernel, out_shape=[jax.ShapeDtypeStruct((n_tok, 2 * width)...  7.22 us
    pallas_call x1, Pallas kernels, shared_down(): pl.pallas_call(kernel, out_shape=[jax.ShapeDtypeStruct((2 * half, n_tok),...  4.47 us
    pallas_call x1, Pallas kernels, pack(): pl.pallas_call(kernel, out_shape=[jax.ShapeDtypeStruct((d_part, 2 * width...  4.18 us
  transfers between devices with their start and end apart: 23, of which 11 were waited for; matrix products, arithmetic and copies ran while one was open for 2% of the time, Pallas kernels for 27%

profile of v2, /device:TPU:0, one launch (start us, length us, event | category | flops | bytes accessed | tf_op | source)
XLA Modules:
  0.0 156.8 jit_solution(4213646036596242156)
XLA Ops:
  0.0 1.2 slice.30
  1.9 1.6 %token_rows.1 = bf16[32,1920]{1,0:T(8,128)(2,1)S(1)} custom-call(s32[3]{0:T(128)S(1)} %pad_add_fusion.where_ref, bf16[128,1792]{1,0:T(8,128)(2,1)} %tok_ref.1, s32[8,128]{1,0:T(8,128)} %bitcast.32, f32[8,128]{1,0:T(8,128)} %bitcast.33), custom_call_target="tpu_custom_call" | custom-call | tf_op jit(solution)/shard_map/token_rows/pallas_call | solution.py:129
  3.6 15.5 %conditional.3 = (bf16[4,32,1920]{2,1,0:T(8,128)(2,1)S(1)}, bf16[448,640]{1,0:T(8,128)(2,1)}, bf16[448,640]{1,0:T(8,128)(2,1)}, bf16[448,640]{1,0:T(8,128)(2,1)}...) conditional(s32[]{:T(128)} %bitcast.15, () %tuple.34, ...), branch_computations={%region_0.0_spmd, %region_1.0_spmd} | conditional | flops 737280 | bytes 10846400 | solution.py:516
  3.6 3.1 %collective-permute-start = (bf16[32,1920]{1,0:T(8,128)(2,1)S(1)}, bf16[32,1920]{1,0:T(8,128)(2,1)S(1)}, u32[]{:S(2)}, u32[]{:S(2)}) collective-permute-start(bf16[32,1920]{1,0:T(8,128)(2,1)S(1)} %get-tuple-element.33), channel_id=1, source_target_pairs={{0,4},{4,0},{8,12},{12,8},{1,5},{5,1},{9,13},{13,9},{2,6},{6,2},{1... | collective-permute-start | bytes 368648 | tf_op jit(solution)/shard_map/cond/branch_1_fun/ppermute | solution.py:90
  6.7 2.6 %collective-permute-start.1 = (bf16[32,1920]{1,0:T(8,128)(2,1)S(1)}, bf16[32,1920]{1,0:T(8,128)(2,1)S(1)}, u32[]{:S(2)}, u32[]{:S(2)}) collective-permute-start(bf16[32,1920]{1,0:T(8,128)(2,1)S(1)} %get-tuple-element.33), channel_id=1, source_target_pairs={{0,8},{4,12},{8,0},{12,4},{1,9},{5,13},{9,1},{13,5},{2,10},{6,14},... | collective-permute-start | bytes 368648 | tf_op jit(solution)/shard_map/cond/branch_1_fun/ppermute | solution.py:90
  9.3 4.2 %pack.1 = (bf16[448,640]{1,0:T(8,128)(2,1)}, bf16[448,640]{1,0:T(8,128)(2,1)}, bf16[448,640]{1,0:T(8,128)(2,1)}, bf16[448,640]{1,0:T(8,128)(2,1)}, bf16[224,640]...) custom-call(s32[3]{0:T(128)S(1)} %get-tuple-element.34.where_ref, ...), custom_call_target="tpu_custom_call" | custom-call | bytes 8388608 | tf_op jit(solution)/shard_map/cond/branch_1_fun/pack/pallas_call | solution.py:196
  13.5 5.5 %collective-permute-done.1 = bf16[32,1920]{1,0:T(8,128)(2,1)S(1)} collective-permute-done((bf16[32,1920]{1,0:T(8,128)(2,1)S(1)}, bf16[32,1920]{1,0:T(8,128)(2,1)S(1)}, u32[]{:S(2)}, u32[]{:S(2)}) %collective-permute-start.1) | collective-permute-done | bytes 122912 | tf_op jit(solution)/shard_map/cond/branch_1_fun/ppermute | solution.py:90
  19.1 1.9 %collective-permute-start.12 = (bf16[448,640]{1,0:T(8,128)(2,1)}, bf16[448,640]{1,0:T(8,128)(2,1)S(1)}, u32[]{:S(2)}, u32[]{:S(2)}) collective-permute-start(bf16[448,640]{1,0:T(8,128)(2,1)} %get-tuple-element.96), channel_id=1, source_target_pairs={{0,4},{4,0},{8,12},{12,8},{1,5},{5,1},{9,13},{13,9},{2,6},{6,2},{1... | collective-permute-start | bytes 1720328 | tf_op jit(solution)/shard_map/ppermute | solution.py:90
  22.1 1.4 collective-permute-start.14
  23.5 52.9 %conditional.4 = (bf16[2,4,32,1920]{3,2,1,0:T(8,128)(2,1)S(1)}, bf16[2,4,32,1920]{3,2,1,0:T(8,128)(2,1)S(1)}, bf16[2,4,32,1920]{3,2,1,0:T(8,128)(2,1)}, bf16[2,4...) conditional(s32[]{:T(128)} %bitcast.15, () %tuple.33, ...), branch_computations={%region_2.0_spmd, %region_3.0_spmd} | conditional | flops 16207773696 | bytes 89620888 | solution.py:516
  23.5 1.5 collective-permute-start.3
  25.0 1.5 collective-permute-start.4
  26.5 8.4 %collective-permute-done.3 = bf16[4,32,1920]{2,1,0:T(8,128)(2,1)S(1)} collective-permute-done((bf16[4,32,1920]{2,1,0:T(8,128)(2,1)S(1)}, bf16[4,32,1920]{2,1,0:T(8,128)(2,1)S(1)}, u32[]{:S(2)}, u32[]{:S(2)}) %collective-permute-start.3) | collective-permute-done | bytes 491552 | tf_op jit(solution)/shard_map/cond/branch_1_fun/ppermute | solution.py:90
  36.2 1.4 collective-permute-start.7
  37.5 1.2 collective-permute-done.5.cro_ref
  38.7 2.6 %collective-permute-start.6 = (bf16[4,32,1920]{2,1,0:T(8,128)(2,1)S(1)}, bf16[4,32,1920]{2,1,0:T(8,128)(2,1)S(1)}, u32[]{:S(2)}, u32[]{:S(2)}) collective-permute-start(bf16[4,32,1920]{2,1,0:T(8,128)(2,1)S(1)} %collective-permute-done.4), channel_id=1, source_target_pairs={{0,2},{1,3},{2,0},{3,1},{4,6},{5,7},{6,4},{7,5},{8,10},{9,11},{10,... | collective-permute-start | bytes 1474568 | tf_op jit(solution)/shard_map/cond/branch_1_fun/ppermute | solution.py:90
  41.4 30.8 %routed.1 = (bf16[2,448,512]{2,1,0:T(8,128)(2,1)S(1)}, f32[2,448,512]{2,1,0:T(8,128)S(1)}) custom-call(s32[3]{0:T(128)S(1)} %get-tuple-element.51.where_ref, bf16[2,4,32,1920]{3,2,1,0:T(8,128)(2,1)S(1)} %pad_maximum_fusion.1.dir_ref, bf16[2,4,32,1920]{3,2,1,0:T(8,128)(2,1)S(1)} %collective-permute-done.5.cro_ref, ...), custom_call_target="tpu_custom_call" | custom-call | flops 16206790656 | bytes 55050240 | tf_op jit(solution)/shard_map/cond/branch_1_fun/routed/pallas_call | solution.py:307
  73.9 2.5 %collective-permute-done.8 = bf16[2,4,32,1920]{3,2,1,0:T(8,128)(2,1)} collective-permute-done((bf16[2,4,32,1920]{3,2,1,0:T(8,128)(2,1)}, bf16[2,4,32,1920]{3,2,1,0:T(8,128)(2,1)}, u32[]{:S(2)}, u32[]{:S(2)}) %collective-permute-start.8) | collective-permute-done | bytes 983072 | tf_op jit(solution)/shard_map/cond/branch_1_fun/ppermute | solution.py:90
  77.1 13.9 %collective-permute-start.16 = (bf16[224,640]{1,0:T(8,128)(2,1)}, bf16[224,640]{1,0:T(8,128)(2,1)S(1)}, u32[]{:S(2)}, u32[]{:S(2)}) collective-permute-start(bf16[224,640]{1,0:T(8,128)(2,1)} %get-tuple-element.108), channel_id=1, source_target_pairs={{0,8},{1,12},{2,0},{3,4},{4,9},{5,13},{6,1},{7,5},{8,10},{9,14},{1... | collective-permute-start | bytes 860168 | tf_op jit(solution)/shard_map/ppermute | solution.py:538
  91.6 7.2 %shared_hidden.1 = (bf16[512,640]{1,0:T(8,128)(2,1)S(1)}, f32[1,1024]{1,0:T(1,128)S(1)}) custom-call(s32[3]{0:T(128)S(1)} %pad_add_fusion.where_ref, bf16[2,4,32,1920]{3,2,1,0:T(8,128)(2,1)S(1)} %get-tuple-element.91.a0, bf16[2,4,32,1920]{3,2,1,0:T(8,128)(2,1)S(1)} %get-tuple-element.92.a1, bf16[2,4,32,1920]{3,2,1,0:T(8,128)(2,1)} %get-tuple-element.93.b0, ...), custom_call_target="tpu_custom_call" | custom-call | flops 2348810240 | bytes 8388608 | tf_op jit(solution)/shard_map/shared_hidden/pallas_call | solution.py:382
  98.8 26.3 %conditional.5 = (bf16[2,512,640]{2,1,0:T(8,128)(2,1)}, bf16[2,512,640]{2,1,0:T(8,128)(2,1)}, f32[448,512]{1,0:T(8,128)S(1)}, bf16[448,512]{1,0:T(8,128)(2,1)S(1)}) conditional(s32[]{:T(128)} %bitcast.15, () %tuple.32, (bf16[512,640]{1,0:T(8,128)(2,1)S(1)}, f32[2,448,512]{2,1,0:T(8,128)S(1)}, bf16[2,448,512]{2,1,0:T(8,128)(2,1)S(1)}) %tuple.37), branch_computations={%region_4.0_spmd, %region_5.0_spmd} | conditional | flops 1802240 | bytes 21954712 | solution.py:516
  98.8 2.7 %collective-permute-start.9 = (bf16[512,640]{1,0:T(8,128)(2,1)S(1)}, bf16[512,640]{1,0:T(8,128)(2,1)S(1)}, u32[]{:S(2)}, u32[]{:S(2)}) collective-permute-start(bf16[512,640]{1,0:T(8,128)(2,1)S(1)} %get-tuple-element.62), channel_id=1, source_target_pairs={{0,2},{1,3},{2,0},{3,1},{4,6},{5,7},{6,4},{7,5},{8,10},{9,11},{10,... | collective-permute-start | bytes 1966088 | tf_op jit(solution)/shard_map/cond/branch_1_fun/ppermute | solution.py:90
  101.5 17.3 %collective-permute-done.9 = bf16[512,640]{1,0:T(8,128)(2,1)S(1)} collective-permute-done((bf16[512,640]{1,0:T(8,128)(2,1)S(1)}, bf16[512,640]{1,0:T(8,128)(2,1)S(1)}, u32[]{:S(2)}, u32[]{:S(2)}) %collective-permute-start.9) | collective-permute-done | bytes 655392 | tf_op jit(solution)/shard_map/cond/branch_1_fun/ppermute | solution.py:90
  118.8 1.2 pad_maximum_fusion.3
  120.6 3.8 %collective-permute-done.11 = bf16[2,448,512]{2,1,0:T(8,128)(2,1)S(1)} collective-permute-done((bf16[2,448,512]{2,1,0:T(8,128)(2,1)S(1)}, bf16[2,448,512]{2,1,0:T(8,128)(2,1)S(1)}, u32[]{:S(2)}, u32[]{:S(2)}) %collective-permute-start.11) | collective-permute-done | bytes 917536 | tf_op jit(solution)/shard_map/cond/branch_1_fun/ppermute | solution.py:90
  125.2 4.5 %shared_down.1 = (bf16[448,512]{1,0:T(8,128)(2,1)S(1)}, f32[448,512]{1,0:T(8,128)S(1)}) custom-call(s32[3]{0:T(128)S(1)} %pad_add_fusion.where_ref, bf16[2,512,640]{2,1,0:T(8,128)(2,1)} %get-tuple-element.102.dir_ref, bf16[2,512,640]{2,1,0:T(8,128)(2,1)} %get-tuple-element.103.cro_ref, f32[1,1024]{1,0:T(1,128)S(1)} %get-tuple-element.104.scale_ref, ...), custom_call_target="tpu_custom_call" | custom-call | flops 1409286144 | bytes 6291456 | tf_op jit(solution)/shard_map/shared_down/pallas_call | solution.py:470
  129.6 1.6 %collective-permute-start.18 = (bf16[448,512]{1,0:T(8,128)(2,1)S(1)}, bf16[448,512]{1,0:T(8,128)(2,1)S(1)}, u32[]{:S(2)}, u32[]{:S(2)}) collective-permute-start(bf16[448,512]{1,0:T(8,128)(2,1)S(1)} %get-tuple-element.111), channel_id=1, source_target_pairs={{0,16},{16,0},{1,17},{17,1},{2,18},{18,2},{3,19},{19,3},{4,20},{20... | collective-permute-start | bytes 1376264 | tf_op jit(solution)/shard_map/ppermute | solution.py:90
  131.2 11.0 %collective-permute-done.18 = bf16[448,512]{1,0:T(8,128)(2,1)S(1)} collective-permute-done((bf16[448,512]{1,0:T(8,128)(2,1)S(1)}, bf16[448,512]{1,0:T(8,128)(2,1)S(1)}, u32[]{:S(2)}, u32[]{:S(2)}) %collective-permute-start.18) | collective-permute-done | bytes 458784 | tf_op jit(solution)/shard_map/ppermute | solution.py:90
  142.3 1.2 collective-permute-done.19
  143.8 1.6 %collective-permute-start.20 = (bf16[448,128]{1,0:T(8,128)(2,1)S(1)}, bf16[448,128]{1,0:T(8,128)(2,1)S(1)}, u32[]{:S(2)}, u32[]{:S(2)}) collective-permute-start(bf16[448,128]{1,0:T(8,128)(2,1)S(1)} %get-tuple-element.129), channel_id=1, source_target_pairs={{0,4},{4,0},{8,12},{12,8},{1,5},{5,1},{9,13},{13,9},{2,6},{6,2},{1... | collective-permute-start | bytes 344072 | tf_op jit(solution)/shard_map/ppermute | solution.py:90
  146.3 2.0 %collective-permute-start.22 = (bf16[448,128]{1,0:T(8,128)(2,1)S(1)}, bf16[448,128]{1,0:T(8,128)(2,1)S(1)}, u32[]{:S(2)}, u32[]{:S(2)}) collective-permute-start(bf16[448,128]{1,0:T(8,128)(2,1)S(1)} %get-tuple-element.130), channel_id=1, source_target_pairs={{0,12},{4,8},{8,4},{12,0},{1,13},{5,9},{9,5},{13,1},{2,14},{6,10},... | collective-permute-start | bytes 344072 | tf_op jit(solution)/shard_map/ppermute | solution.py:90
  149.4 6.7 %collective-permute-done.21 = bf16[448,128]{1,0:T(8,128)(2,1)S(1)} collective-permute-done((bf16[448,128]{1,0:T(8,128)(2,1)S(1)}, bf16[448,128]{1,0:T(8,128)(2,1)S(1)}, u32[]{:S(2)}, u32[]{:S(2)}) %collective-permute-start.21) | collective-permute-done | bytes 114720 | tf_op jit(solution)/shard_map/ppermute | solution.py:90
  (44 shorter events, 9.6 us)
Async XLA Ops:
  3.6 9.9 %collective-permute-start = (bf16[32,1920]{1,0:T(8,128)(2,1)S(1)}, bf16[32,1920]{1,0:T(8,128)(2,1)S(1)}, u32[]{:S(2)}, u32[]{:S(2)}) collective-permute-start(bf16[32,1920]{1,0:T(8,128)(2,1)S(1)} %get-tuple-element.33), channel_id=1, source_target_pairs={{0,4},{4,0},{8,12},{12,8},{1,5},{5,1},{9,13},{13,9},{2,6},{6,2},{1... | collective-permute-start | bytes 368648 | tf_op jit(solution)/shard_map/cond/branch_1_fun/ppermute | solution.py:90
  6.7 12.3 %collective-permute-start.1 = (bf16[32,1920]{1,0:T(8,128)(2,1)S(1)}, bf16[32,1920]{1,0:T(8,128)(2,1)S(1)}, u32[]{:S(2)}, u32[]{:S(2)}) collective-permute-start(bf16[32,1920]{1,0:T(8,128)(2,1)S(1)} %get-tuple-element.33), channel_id=1, source_target_pairs={{0,8},{4,12},{8,0},{12,4},{1,9},{5,13},{9,1},{13,5},{2,10},{6,14},... | collective-permute-start | bytes 368648 | tf_op jit(solution)/shard_map/cond/branch_1_fun/ppermute | solution.py:90
  9.3 9.7 %collective-permute-start.2 = (bf16[32,1920]{1,0:T(8,128)(2,1)S(1)}, bf16[32,1920]{1,0:T(8,128)(2,1)S(1)}, u32[]{:S(2)}, u32[]{:S(2)}) collective-permute-start(bf16[32,1920]{1,0:T(8,128)(2,1)S(1)} %get-tuple-element.33), channel_id=1, source_target_pairs={{0,12},{4,8},{8,4},{12,0},{1,13},{5,9},{9,5},{13,1},{2,14},{6,10},... | collective-permute-start | bytes 368648 | tf_op jit(solution)/shard_map/cond/branch_1_fun/ppermute | solution.py:90
  19.1 71.9 %collective-permute-start.12 = (bf16[448,640]{1,0:T(8,128)(2,1)}, bf16[448,640]{1,0:T(8,128)(2,1)S(1)}, u32[]{:S(2)}, u32[]{:S(2)}) collective-permute-start(bf16[448,640]{1,0:T(8,128)(2,1)} %get-tuple-element.96), channel_id=1, source_target_pairs={{0,4},{4,0},{8,12},{12,8},{1,5},{5,1},{9,13},{13,9},{2,6},{6,2},{1... | collective-permute-start | bytes 1720328 | tf_op jit(solution)/shard_map/ppermute | solution.py:90
  21.0 70.6 %collective-permute-start.13 = (bf16[448,640]{1,0:T(8,128)(2,1)}, bf16[448,640]{1,0:T(8,128)(2,1)S(1)}, u32[]{:S(2)}, u32[]{:S(2)}) collective-permute-start(bf16[448,640]{1,0:T(8,128)(2,1)} %get-tuple-element.97), channel_id=1, source_target_pairs={{0,8},{4,12},{8,0},{12,4},{1,9},{5,13},{9,1},{13,5},{2,10},{6,14},... | collective-permute-start | bytes 1720328 | tf_op jit(solution)/shard_map/ppermute | solution.py:90
  22.1 69.5 %collective-permute-start.14 = (bf16[448,640]{1,0:T(8,128)(2,1)}, bf16[448,640]{1,0:T(8,128)(2,1)S(1)}, u32[]{:S(2)}, u32[]{:S(2)}) collective-permute-start(bf16[448,640]{1,0:T(8,128)(2,1)} %get-tuple-element.98), channel_id=1, source_target_pairs={{0,12},{4,8},{8,4},{12,0},{1,13},{5,9},{9,5},{13,1},{2,14},{6,10},... | collective-permute-start | bytes 1720328 | tf_op jit(solution)/shard_map/ppermute | solution.py:90
  23.5 68.0 %copy-start.4 = (bf16[1792]{0:T(1024)(128)(2,1)S(1)}, bf16[1792]{0:T(1024)(128)(2,1)}, u32[]{:S(2)}) copy-start(bf16[1792]{0:T(1024)(128)(2,1)} %param.19) | copy-start | bytes 10756
  23.5 11.4 %collective-permute-start.3 = (bf16[4,32,1920]{2,1,0:T(8,128)(2,1)S(1)}, bf16[4,32,1920]{2,1,0:T(8,128)(2,1)S(1)}, u32[]{:S(2)}, u32[]{:S(2)}) collective-permute-start(bf16[4,32,1920]{2,1,0:T(8,128)(2,1)S(1)} %get-tuple-element.46), channel_id=1, source_target_pairs={{0,2},{1,3},{2,0},{3,1},{4,6},{5,7},{6,4},{7,5},{8,10},{9,11},{10,... | collective-permute-start | bytes 1474568 | tf_op jit(solution)/shard_map/cond/branch_1_fun/ppermute | solution.py:90
  25.0 11.1 %collective-permute-start.4 = (bf16[4,32,1920]{2,1,0:T(8,128)(2,1)S(1)}, bf16[4,32,1920]{2,1,0:T(8,128)(2,1)S(1)}, u32[]{:S(2)}, u32[]{:S(2)}) collective-permute-start(bf16[4,32,1920]{2,1,0:T(8,128)(2,1)S(1)} %get-tuple-element.46), channel_id=1, source_target_pairs={{0,16},{16,0},{1,17},{17,1},{2,18},{18,2},{3,19},{19,3},{4,20},{20... | collective-permute-start | bytes 1474568 | tf_op jit(solution)/shard_map/cond/branch_1_fun/ppermute | solution.py:90
  35.0 37.2 %copy-start = (bf16[2,4,32,1920]{3,2,1,0:T(8,128)(2,1)}, bf16[2,4,32,1920]{3,2,1,0:T(8,128)(2,1)S(1)}, u32[]{:S(2)}) copy-start(bf16[2,4,32,1920]{3,2,1,0:T(8,128)(2,1)S(1)} %pad_maximum_fusion.1.dir_ref) | copy-start | bytes 2949124 | tf_op jit(solution)/shard_map/cond
  36.1 2.6 %collective-permute-start.5 = (bf16[2,4,32,1920]{3,2,1,0:T(8,128)(2,1)S(1)}, bf16[2,4,32,1920]{3,2,1,0:T(8,128)(2,1)S(1)}, u32[]{:S(2)}, u32[]{:S(2)}) collective-permute-start(bf16[2,4,32,1920]{3,2,1,0:T(8,128)(2,1)S(1)} %pad_maximum_fusion.1.dir_ref), channel_id=1, source_target_pairs={{0,1},{1,0},{2,3},{3,2},{4,5},{5,4},{6,7},{7,6},{8,9},{9,8},{10,11... | collective-permute-start | bytes 2949128 | tf_op jit(solution)/shard_map/cond/branch_1_fun/ppermute | solution.py:90
  36.2 36.1 %collective-permute-start.7 = (bf16[224,640]{1,0:T(8,128)(2,1)S(1)}, bf16[224,640]{1,0:T(8,128)(2,1)}, u32[]{:S(2)}, u32[]{:S(2)}) collective-permute-start(bf16[224,640]{1,0:T(8,128)(2,1)S(1)} %get-tuple-element.56), channel_id=1, source_target_pairs={{0,0},{1,4},{2,8},{3,12},{4,1},{5,5},{6,9},{7,13},{8,2},{9,6},{10,... | collective-permute-start | bytes 860168 | tf_op jit(solution)/shard_map/cond/branch_1_fun/ppermute | solution.py:538
  38.7 33.5 %copy-start.2 = (bf16[2,4,32,1920]{3,2,1,0:T(8,128)(2,1)}, bf16[2,4,32,1920]{3,2,1,0:T(8,128)(2,1)S(1)}, u32[]{:S(2)}) copy-start(bf16[2,4,32,1920]{3,2,1,0:T(8,128)(2,1)S(1)} %collective-permute-done.5.cro_ref) | copy-start | bytes 2949124 | tf_op jit(solution)/shard_map/cond
  38.7 33.5 %collective-permute-start.6 = (bf16[4,32,1920]{2,1,0:T(8,128)(2,1)S(1)}, bf16[4,32,1920]{2,1,0:T(8,128)(2,1)S(1)}, u32[]{:S(2)}, u32[]{:S(2)}) collective-permute-start(bf16[4,32,1920]{2,1,0:T(8,128)(2,1)S(1)} %collective-permute-done.4), channel_id=1, source_target_pairs={{0,2},{1,3},{2,0},{3,1},{4,6},{5,7},{6,4},{7,5},{8,10},{9,11},{10,... | collective-permute-start | bytes 1474568 | tf_op jit(solution)/shard_map/cond/branch_1_fun/ppermute | solution.py:90
  72.2 4.2 %copy-start.1 = (bf16[2,4,32,1920]{3,2,1,0:T(8,128)(2,1)S(1)}, bf16[2,4,32,1920]{3,2,1,0:T(8,128)(2,1)}, u32[]{:S(2)}) copy-start(bf16[2,4,32,1920]{3,2,1,0:T(8,128)(2,1)} %copy-done) | copy-start | bytes 2949124 | tf_op jit(solution)/shard_map/cond
  72.2 4.2 %copy-start.3 = (bf16[2,4,32,1920]{3,2,1,0:T(8,128)(2,1)S(1)}, bf16[2,4,32,1920]{3,2,1,0:T(8,128)(2,1)}, u32[]{:S(2)}) copy-start(bf16[2,4,32,1920]{3,2,1,0:T(8,128)(2,1)} %copy-done.2) | copy-start | bytes 2949124 | tf_op jit(solution)/shard_map/cond
  73.3 3.1 %collective-permute-start.8 = (bf16[2,4,32,1920]{3,2,1,0:T(8,128)(2,1)}, bf16[2,4,32,1920]{3,2,1,0:T(8,128)(2,1)}, u32[]{:S(2)}, u32[]{:S(2)}) collective-permute-start(bf16[2,4,32,1920]{3,2,1,0:T(8,128)(2,1)} %pad_maximum_fusion.2), channel_id=1, source_target_pairs={{0,1},{1,0},{2,3},{3,2},{4,5},{5,4},{6,7},{7,6},{8,9},{9,8},{10,11... | collective-permute-start | bytes 2949128 | tf_op jit(solution)/shard_map/cond/branch_1_fun/ppermute | solution.py:90
  76.4 48.7 %collective-permute-start.15 = (bf16[224,640]{1,0:T(8,128)(2,1)}, bf16[224,640]{1,0:T(8,128)(2,1)S(1)}, u32[]{:S(2)}, u32[]{:S(2)}) collective-permute-start(bf16[224,640]{1,0:T(8,128)(2,1)} %get-tuple-element.107), channel_id=1, source_target_pairs={{0,4},{1,0},{2,12},{3,8},{4,5},{5,1},{6,13},{7,9},{8,6},{9,2},{10,... | collective-permute-start | bytes 860168 | tf_op jit(solution)/shard_map/ppermute | solution.py:538
  77.1 48.0 %collective-permute-start.16 = (bf16[224,640]{1,0:T(8,128)(2,1)}, bf16[224,640]{1,0:T(8,128)(2,1)S(1)}, u32[]{:S(2)}, u32[]{:S(2)}) collective-permute-start(bf16[224,640]{1,0:T(8,128)(2,1)} %get-tuple-element.108), channel_id=1, source_target_pairs={{0,8},{1,12},{2,0},{3,4},{4,9},{5,13},{6,1},{7,5},{8,10},{9,14},{1... | collective-permute-start | bytes 860168 | tf_op jit(solution)/shard_map/ppermute | solution.py:538
  91.0 34.2 %collective-permute-start.17 = (bf16[224,640]{1,0:T(8,128)(2,1)}, bf16[224,640]{1,0:T(8,128)(2,1)S(1)}, u32[]{:S(2)}, u32[]{:S(2)}) collective-permute-start(bf16[224,640]{1,0:T(8,128)(2,1)} %get-tuple-element.109), channel_id=1, source_target_pairs={{0,12},{1,8},{2,4},{3,0},{4,13},{5,9},{6,5},{7,1},{8,14},{9,10},{1... | collective-permute-start | bytes 860168 | tf_op jit(solution)/shard_map/ppermute | solution.py:538
  98.8 20.0 %collective-permute-start.9 = (bf16[512,640]{1,0:T(8,128)(2,1)S(1)}, bf16[512,640]{1,0:T(8,128)(2,1)S(1)}, u32[]{:S(2)}, u32[]{:S(2)}) collective-permute-start(bf16[512,640]{1,0:T(8,128)(2,1)S(1)} %get-tuple-element.62), channel_id=1, source_target_pairs={{0,2},{1,3},{2,0},{3,1},{4,6},{5,7},{6,4},{7,5},{8,10},{9,11},{10,... | collective-permute-start | bytes 1966088 | tf_op jit(solution)/shard_map/cond/branch_1_fun/ppermute | solution.py:90
  120.1 5.1 %collective-permute-start.10 = (bf16[2,512,640]{2,1,0:T(8,128)(2,1)}, bf16[2,512,640]{2,1,0:T(8,128)(2,1)}, u32[]{:S(2)}, u32[]{:S(2)}) collective-permute-start(bf16[2,512,640]{2,1,0:T(8,128)(2,1)} %pad_maximum_fusion.3), channel_id=1, source_target_pairs={{0,1},{1,0},{2,3},{3,2},{4,5},{5,4},{6,7},{7,6},{8,9},{9,8},{10,11... | collective-permute-start | bytes 3932168 | tf_op jit(solution)/shard_map/cond/branch_1_fun/ppermute | solution.py:90
  120.2 4.2 %collective-permute-start.11 = (bf16[2,448,512]{2,1,0:T(8,128)(2,1)S(1)}, bf16[2,448,512]{2,1,0:T(8,128)(2,1)S(1)}, u32[]{:S(2)}, u32[]{:S(2)}) collective-permute-start(bf16[2,448,512]{2,1,0:T(8,128)(2,1)S(1)} %get-tuple-element.64), channel_id=1, source_target_pairs={{0,1},{1,0},{2,3},{3,2},{4,5},{5,4},{6,7},{7,6},{8,9},{9,8},{10,11... | collective-permute-start | bytes 2752520 | tf_op jit(solution)/shard_map/cond/branch_1_fun/ppermute | solution.py:90
  129.6 12.6 %collective-permute-start.18 = (bf16[448,512]{1,0:T(8,128)(2,1)S(1)}, bf16[448,512]{1,0:T(8,128)(2,1)S(1)}, u32[]{:S(2)}, u32[]{:S(2)}) collective-permute-start(bf16[448,512]{1,0:T(8,128)(2,1)S(1)} %get-tuple-element.111), channel_id=1, source_target_pairs={{0,16},{16,0},{1,17},{17,1},{2,18},{18,2},{3,19},{19,3},{4,20},{20... | collective-permute-start | bytes 1376264 | tf_op jit(solution)/shard_map/ppermute | solution.py:90
  131.2 12.3 %collective-permute-start.19 = (bf16[448,512]{1,0:T(8,128)(2,1)S(1)}, bf16[448,512]{1,0:T(8,128)(2,1)S(1)}, u32[]{:S(2)}, u32[]{:S(2)}) collective-permute-start(bf16[448,512]{1,0:T(8,128)(2,1)S(1)} %get-tuple-element.112), channel_id=1, source_target_pairs={{0,2},{1,3},{2,0},{3,1},{4,6},{5,7},{6,4},{7,5},{8,10},{9,11},{10,... | collective-permute-start | bytes 1376264 | tf_op jit(solution)/shard_map/ppermute | solution.py:90
  143.8 5.6 %collective-permute-start.20 = (bf16[448,128]{1,0:T(8,128)(2,1)S(1)}, bf16[448,128]{1,0:T(8,128)(2,1)S(1)}, u32[]{:S(2)}, u32[]{:S(2)}) collective-permute-start(bf16[448,128]{1,0:T(8,128)(2,1)S(1)} %get-tuple-element.129), channel_id=1, source_target_pairs={{0,4},{4,0},{8,12},{12,8},{1,5},{5,1},{9,13},{13,9},{2,6},{6,2},{1... | collective-permute-start | bytes 344072 | tf_op jit(solution)/shard_map/ppermute | solution.py:90
  145.4 10.7 %collective-permute-start.21 = (bf16[448,128]{1,0:T(8,128)(2,1)S(1)}, bf16[448,128]{1,0:T(8,128)(2,1)S(1)}, u32[]{:S(2)}, u32[]{:S(2)}) collective-permute-start(bf16[448,128]{1,0:T(8,128)(2,1)S(1)} %get-tuple-element.131), channel_id=1, source_target_pairs={{0,8},{4,12},{8,0},{12,4},{1,9},{5,13},{9,1},{13,5},{2,10},{6,14},... | collective-permute-start | bytes 344072 | tf_op jit(solution)/shard_map/ppermute | solution.py:90
  146.3 9.8 %collective-permute-start.22 = (bf16[448,128]{1,0:T(8,128)(2,1)S(1)}, bf16[448,128]{1,0:T(8,128)(2,1)S(1)}, u32[]{:S(2)}, u32[]{:S(2)}) collective-permute-start(bf16[448,128]{1,0:T(8,128)(2,1)S(1)} %get-tuple-element.130), channel_id=1, source_target_pairs={{0,12},{4,8},{8,4},{12,0},{1,13},{5,9},{9,5},{13,1},{2,14},{6,10},... | collective-permute-start | bytes 344072 | tf_op jit(solution)/shard_map/ppermute | solution.py:90

commit v3 on v2

--- a/solution.py
+++ b/solution.py
@@ -213,48 +213,44 @@
     )(where, wg, wu, wd)
 
 
-def token_copies(where_ref, direct, crossed, rows_ref, info_ref, sem, base):
+def token_copies(where_ref, refs, rows_ref, info_ref, sem, base):
     t = where_ref[1]
-    _, n_dp, quarter, _ = direct.shape
+    n_dp, quarter, _ = refs[0].shape
     d = rows_ref.shape[1]
     copies = []
-    for b, ref in ((0, direct), (2, direct), (1, crossed), (3, crossed)):
-        for k in range(n_dp):
+    for k in range(n_dp):
+        jobs = []
+        for b, ref in enumerate(refs):
             row = pl.multiple_of(base + k * 4 * quarter + (t ^ b) * quarter, quarter)
-            src = ref.at[b // 2, k]
-            copies.append(
-                pltpu.make_async_copy(
-                    src.at[:, pl.ds(0, d)], rows_ref.at[pl.ds(row, quarter)], sem.at[len(copies)]
-                )
-            )
+            src = ref.at[k]
+            jobs.append((src.at[:, pl.ds(0, d)], rows_ref.at[pl.ds(row, quarter)]))
             if info_ref is not None:
-                copies.append(
-                    pltpu.make_async_copy(
-                        src.at[:, pl.ds(d, 128)],
-                        info_ref.at[pl.ds(row, quarter)],
-                        sem.at[len(copies)],
-                    )
-                )
+                jobs.append((src.at[:, pl.ds(d, 128)], info_ref.at[pl.ds(row, quarter)]))
+        copies.append(
+            [pltpu.make_async_copy(x, y, sem.at[k, j]) for j, (x, y) in enumerate(jobs)]
+        )
     return copies
 
 
-def routed_experts(where, direct, crossed, eg, eu, ed, top):
+def routed_experts(where, spread_tokens, eg, eu, ed, top):
     e_dev, ff_e, d = eg.shape
-    n_dp = direct.shape[1]
-    n_tok = n_dp * direct.shape[2] * 4
-    slots = n_dp * CAP
+    n_dp, quarter, _ = spread_tokens[0].shape
+    block = 4 * quarter
+    n_tok = n_dp * block
     part = d // 4
-
-    def kernel(
-        where_ref, dir_ref, cro_ref, g_ref, u_ref, w_ref, give, keep,
-        tok, info, place_t, gate_t, back, outs, acc_t, sem,
-    ):
+    pairs = n_dp // 2
+    seg = 2 * CAP
+    side = e_dev * seg
+
+    def kernel(where_ref, *rest):
+        refs = rest[:4]
+        g_ref, u_ref, w_ref, give, keep, tok, info, back, moved, gate_of, acc_t, sem = rest[4:]
         e = pl.program_id(0)
         z, t = where_ref[0], where_ref[1]
 
         @pl.when(e == 0)
         def _():
-            run_all(token_copies(where_ref, dir_ref, cro_ref, tok, info, sem, 0))
+            run_all(sum(token_copies(where_ref, refs, tok, info, sem, 0), []))
             tags = info[...].astype(F32)
             lane = lax.broadcasted_iota(jnp.int32, tags.shape, 1)
             weight = pltpu.roll(tags, 128 - top, 1) + pltpu.roll(tags, 128 - 2 * top, 1)
@@ -266,36 +262,53 @@
                 gate = jnp.sum(jnp.where(hit, weight, 0.0), axis=1, keepdims=True)
                 chosen = jnp.where(lane == i, has, chosen)
                 gates = jnp.where(lane == i, gate, gates)
-            row = lax.broadcasted_iota(jnp.int32, (n_tok, n_tok), 0)
-            col = lax.broadcasted_iota(jnp.int32, (n_tok, n_tok), 1)
+            row = lax.broadcasted_iota(jnp.int32, (block, block), 0)
+            col = lax.broadcasted_iota(jnp.int32, (block, block), 1)
             earlier = jnp.where(col < row, 1.0, 0.0).astype(BF)
-            before = jnp.dot(earlier, chosen.astype(BF), preferred_element_type=F32)
-            where_to = jnp.where(chosen > 0.5, before, -1.0)
-            place_t[...] = where_to.T
-            gate_t[...] = gates.T
-
-        line = place_t[pl.ds(e, 1), :]
-        slot = lax.broadcasted_iota(jnp.int32, (slots, n_tok), 0).astype(F32)
-        hit = slot == line
-        pick = jnp.where(hit, 1.0, 0.0).astype(BF)
-        gate_of = jnp.sum(jnp.where(hit, gate_t[pl.ds(e, 1), :], 0.0), axis=1, keepdims=True)
-        x = jnp.dot(pick, tok[...], preferred_element_type=F32).astype(BF)
+            for p in range(pairs):
+                slots = []
+                for b in range(2):
+                    lo = (2 * p + b) * block
+                    mine = chosen[lo : lo + block]
+                    before = jnp.dot(earlier, mine.astype(BF), preferred_element_type=F32)
+                    slots.append(jnp.where(mine > 0.5, before + b * CAP, -1.0))
+                slot_t = jnp.concatenate(slots, axis=0).T
+                gate_t = gates[2 * p * block : 2 * (p + 1) * block].T
+                picks = []
+                for i in range(e_dev):
+                    spot = lax.broadcasted_iota(jnp.int32, (seg, 2 * block), 0).astype(F32)
+                    hit = spot == slot_t[i : i + 1, :]
+                    g = jnp.sum(jnp.where(hit, gate_t[i : i + 1, :], 0.0), axis=1, keepdims=True)
+                    gate_of[pl.ds(p * side + i * seg, seg), :] = jnp.broadcast_to(g, (seg, 128))
+                    picks.append(jnp.where(hit, 1.0, 0.0))
+                pick = jnp.concatenate(picks, axis=0)
+                back[p] = pick.T.astype(BF)
+                moved[pl.ds(p * side, side), :] = jnp.dot(
+                    pick.astype(BF),
+                    tok[pl.ds(2 * p * block, 2 * block), :],
+                    preferred_element_type=F32,
+                ).astype(BF)
+
+        spots = [pl.ds(pl.multiple_of(p * side + e * seg, seg), seg) for p in range(pairs)]
+        x = jnp.concatenate([moved[s, :] for s in spots], axis=0)
         dims = (((1,), (1,)), ((), ()))
         gate = lax.dot_general(x, g_ref[0], dims, preferred_element_type=F32)
         up = lax.dot_general(x, u_ref[0], dims, preferred_element_type=F32)
         hidden = (gate * jax.nn.sigmoid(gate) * up).astype(BF)
         out = jnp.dot(hidden, w_ref[0], preferred_element_type=F32)
-        at = pl.multiple_of(e * slots, slots)
-        outs[pl.ds(at, slots), :] = (gate_of * out).astype(BF)
-        back[pl.ds(at, slots), :] = pick
+        for p, s in enumerate(spots):
+            moved[s, :] = (gate_of[s, :1] * out[p * seg : (p + 1) * seg]).astype(BF)
 
         @pl.when(e == e_dev - 1)
         def _():
-            dims = (((0,), (0,)), ((), ()))
-            for i in range(d // 256):
-                acc_t[pl.ds(256 * i, 256), :] = lax.dot_general(
-                    outs[:, pl.ds(256 * i, 256)], back[...], dims, preferred_element_type=F32
-                )
+            for p in range(pairs):
+                for i in range(d // 256):
+                    sums = jnp.dot(
+                        back[p],
+                        moved[pl.ds(p * side, side), pl.ds(256 * i, 256)],
+                        preferred_element_type=F32,
+                    )
+                    acc_t[pl.ds(256 * i, 256), pl.ds(2 * p * block, 2 * block)] = sums.T
             for b in range(2):
                 mine = pl.multiple_of((t ^ (2 * b)) * part, part)
                 theirs = pl.multiple_of((t ^ (2 * b + 1)) * part, part)
@@ -303,7 +316,6 @@
                 give[b] = acc_t[pl.ds(theirs, part), :].astype(BF)
 
     weights = pl.BlockSpec((1, ff_e, d), lambda e: (e, 0, 0))
-    n_copies = 2 * 4 * n_dp
     return pl.pallas_call(
         kernel,
         grid=(e_dev,),
@@ -311,7 +323,7 @@
             jax.ShapeDtypeStruct((2, part, n_tok), BF),
             jax.ShapeDtypeStruct((2, part, n_tok), F32),
         ],
-        in_specs=[SMEM, ANY, ANY, weights, weights, weights],
+        in_specs=[SMEM] + [ANY] * 4 + [weights, weights, weights],
         out_specs=[
             pl.BlockSpec((2, part, n_tok), lambda e: (0, 0, 0)),
             pl.BlockSpec((2, part, n_tok), lambda e: (0, 0, 0)),
@@ -319,101 +331,108 @@
         scratch_shapes=[
             pltpu.VMEM((n_tok, d), BF),
             pltpu.VMEM((n_tok, 128), BF),
-            pltpu.VMEM((128, n_tok), F32),
-            pltpu.VMEM((128, n_tok), F32),
-            pltpu.VMEM((e_dev * slots, n_tok), BF),
-            pltpu.VMEM((e_dev * slots, d), BF),
+            pltpu.VMEM((pairs, 2 * block, side), BF),
+            pltpu.VMEM((pairs * side, d), BF),
+            pltpu.VMEM((pairs * side, 128), F32),
             pltpu.VMEM((d, n_tok), F32),
-            pltpu.SemaphoreType.DMA((n_copies,)),
+            pltpu.SemaphoreType.DMA((n_dp, 8)),
         ],
         compiler_params=pltpu.CompilerParams(vmem_limit_bytes=52 << 20),
         cost_estimate=pl.CostEstimate(
-            flops=6 * slots * e_dev * ff_e * d + 4 * slots * e_dev * n_tok * d,
+            flops=6 * pairs * side * ff_e * d,
             bytes_accessed=6 * e_dev * ff_e * d,
-            transcendentals=slots * e_dev * ff_e,
+            transcendentals=pairs * side * ff_e,
         ),
         name="routed",
-    )(where, direct, crossed, eg, eu, ed)
-
-
-def shared_hidden(where, own, other, pieces, vec, after, width):
+    )(where, *spread_tokens, eg, eu, ed)
+
+
+def shared_hidden(where, tokens, pieces, vec, after, width):
     d_part = pieces[0].shape[0]
     n = len(pieces)
     d = n * d_part
-    n_tok = own[0].shape[1] * own[0].shape[2] * 4
+    n_dp, quarter, _ = tokens[0].shape
+    n_tok = n_dp * quarter * 4
+    half = n_tok // 2
     whole = width - 64
 
-    def kernel(where_ref, a0, a1, b0, b1, vec_ref, *rest):
-        p_refs = rest[:n]
-        hid, scale, tok, w, tok_sem, w_sem = rest[n + 1 :]
+    def kernel(where_ref, *rest):
+        refs, vec_ref, p_refs = rest[:4], rest[4], rest[5 : 5 + n]
+        hid, scale, tok, w, tok_sem, w_sem = rest[6 + n :]
         z = where_ref[0]
-        t_copies = token_copies(where_ref, a0, a1, tok, None, tok_sem.at[0], 0)
-        t_copies += token_copies(where_ref, b0, b1, tok, None, tok_sem.at[1], n_tok)
         w_copies = []
         for k in range(n):
             row = pl.multiple_of((z ^ k) * d_part, d_part)
             w_copies.append(
                 pltpu.make_async_copy(p_refs[k], w.at[pl.ds(row, d_part)], w_sem.at[k])
             )
-        run_all(w_copies + t_copies)
+        copies = token_copies(where_ref, refs, tok, None, tok_sem, 0)
+        for batch in [w_copies] + copies:
+            for c in batch:
+                c.start()
         dims = (((1,), (1,)), ((), ()))
         lines = jnp.broadcast_to(vec_ref[...], (8, d))
-        def half_hidden(row):
-            x = tok[pl.ds(row, 256), :]
+        for c in w_copies:
+            c.wait()
+        mids = []
+        for side in range(2):
+            for k in range(side * n_dp // 2, (side + 1) * n_dp // 2):
+                for c in copies[k]:
+                    c.wait()
+            rows = pl.ds(side * half, half)
+            x = tok[rows, :]
             acc = jnp.dot(x, w[...], preferred_element_type=F32)
             gate_mid = acc[:, whole : whole + 128]
             up_mid = pltpu.roll(gate_mid, 64, 1)
             gate, up = acc[:, :whole], acc[:, width + 64 :]
             line = lax.dot_general(lines, x, dims, preferred_element_type=F32)
-            scale[:, pl.ds(row, 256)] = jax.nn.sigmoid(line[:1])
-            body = gate * jax.nn.sigmoid(gate) * up
-            return body.astype(BF), gate_mid * jax.nn.sigmoid(gate_mid) * up_mid
-
-        for row in range(0, n_tok, 256):
-            rows = pl.ds(row, 256)
-            body, mid = half_hidden(row)
-            far_body, far_mid = half_hidden(n_tok + row)
-            lane = lax.broadcasted_iota(jnp.int32, mid.shape, 1)
-            hid[rows, pl.ds(0, whole)] = body
-            hid[rows, pl.ds(width + 64, whole)] = far_body
-            mid = jnp.where(lane < 64, mid, pltpu.roll(far_mid, 64, 1))
-            hid[rows, pl.ds(whole, 128)] = mid.astype(BF)
-
+            scale[:, rows] = jax.nn.sigmoid(line[:1])
+            at = pl.ds(side * (width + 64), whole)
+            hid[:, at] = (gate * jax.nn.sigmoid(gate) * up).astype(BF)
+            mids.append(gate_mid * jax.nn.sigmoid(gate_mid) * up_mid)
+        lane = lax.broadcasted_iota(jnp.int32, mids[0].shape, 1)
+        mid = jnp.where(lane < 64, mids[0], pltpu.roll(mids[1], 64, 1))
+        hid[:, pl.ds(whole, 128)] = mid.astype(BF)
+
+    vm = pl.BlockSpec(memory_space=pltpu.VMEM)
     return pl.pallas_call(
         kernel,
         out_shape=[
-            jax.ShapeDtypeStruct((n_tok, 2 * width), BF),
-            jax.ShapeDtypeStruct((1, 2 * n_tok), F32),
+            jax.ShapeDtypeStruct((half, 2 * width), BF),
+            jax.ShapeDtypeStruct((1, n_tok), F32),
         ],
-        in_specs=[SMEM] + [ANY] * 4 + [pl.BlockSpec(memory_space=pltpu.VMEM)] + [ANY] * (n + 1),
-        out_specs=[pl.BlockSpec(memory_space=pltpu.VMEM)] * 2,
+        in_specs=[SMEM] + [ANY] * 4 + [vm] + [ANY] * (n + 1),
+        out_specs=[vm] * 2,
         scratch_shapes=[
-            pltpu.VMEM((2 * n_tok, d), BF),
+            pltpu.VMEM((n_tok, d), BF),
             pltpu.VMEM((d, 2 * width), BF),
-            pltpu.SemaphoreType.DMA((2, 4 * own[0].shape[1])),
+            pltpu.SemaphoreType.DMA((n_dp, 4)),
             pltpu.SemaphoreType.DMA((n,)),
         ],
         compiler_params=pltpu.CompilerParams(vmem_limit_bytes=24 << 20),
         cost_estimate=pl.CostEstimate(
-            flops=2 * 2 * n_tok * d * 2 * width,
-            bytes_accessed=8 << 20,
-            transcendentals=2 * n_tok * width,
+            flops=2 * n_tok * d * 2 * width,
+            bytes_accessed=4 << 20,
+            transcendentals=n_tok * width,
         ),
         name="shared_hidden",
-    )(where, own[0], own[1], other[0], other[1], vec, *pieces, after)
-
-
-def shared_down(where, pieces, direct, crossed, scale, routed, width):
+    )(where, *tokens, vec, *pieces, after)
+
+
+def shared_down(where, pieces, hidden, scale, width, far, routed):
     n = len(pieces)
     half = pieces[0].shape[0]
     whole = width - 64
     lanes = whole + 128
-    n_tok = direct.shape[1]
-    both = 2 * n_tok
-
-    def kernel(where_ref, dir_ref, cro_ref, scale_ref, routed_ref, *rest):
-        p_refs = rest[:n]
-        far, near, w, h, w_sem, h_sem = rest[n:]
+    rows_h = hidden[0].shape[0]
+    n_tok = 2 * rows_h
+
+    def kernel(where_ref, scale_ref, *rest):
+        h_refs, p_refs = rest[:4], rest[4 : 4 + n]
+        if far:
+            out_ref, w, h, w_sem, h_sem = rest[4 + n :]
+        else:
+            routed_ref, out_ref, w, h, w_sem, h_sem = rest[4 + n :]
         z, t = where_ref[0], where_ref[1]
         copies = []
         for r in range(n):
@@ -430,63 +449,55 @@
             )
             for j, (s, d) in enumerate(jobs):
                 copies.append(pltpu.make_async_copy(s, d, w_sem.at[r, j]))
-        for m, ref in ((0, dir_ref), (2, dir_ref), (1, cro_ref), (3, cro_ref)):
+        for m in range(4):
             at = pl.multiple_of((z ^ t ^ m) * lanes, lanes)
-            src = ref.at[m // 2]
+            top, bottom = h.at[pl.ds(0, rows_h)], h.at[pl.ds(rows_h, rows_h)]
             jobs = (
-                (src.at[:, pl.ds(0, lanes)], h.at[pl.ds(0, n_tok), pl.ds(at, lanes)]),
-                (
-                    src.at[:, pl.ds(lanes, whole)],
-                    h.at[pl.ds(n_tok, n_tok), pl.ds(at, whole)],
-                ),
-                (
-                    src.at[:, pl.ds(whole, 128)],
-                    h.at[pl.ds(n_tok, n_tok), pl.ds(at + whole, 128)],
-                ),
+                (h_refs[m].at[:, pl.ds(0, lanes)], top.at[:, pl.ds(at, lanes)]),
+                (h_refs[m].at[:, pl.ds(lanes, whole)], bottom.at[:, pl.ds(at, whole)]),
+                (h_refs[m].at[:, pl.ds(whole, 128)], bottom.at[:, pl.ds(at + whole, 128)]),
             )
             for j, (s, d) in enumerate(jobs):
                 copies.append(pltpu.make_async_copy(s, d, h_sem.at[m, j]))
         run_all(copies)
-        lane = lax.broadcasted_iota(jnp.int32, (half, 128), 1)
+        low = lax.broadcasted_iota(jnp.int32, (half, 128), 1) < 64
+        low_h = lax.broadcasted_iota(jnp.int32, (rows_h, 128), 1) < 64
         for r in range(n):
             at = pl.ds(lanes * r + whole, 128)
-            for i, mask in ((0, lane < 64), (1, lane >= 64)):
+            for i in range(2):
                 rows = pl.ds(half * i, half)
+                mask = low if i == 0 else ~low
                 w[rows, at] = jnp.where(mask, w[rows, at].astype(F32), 0.0).astype(BF)
-        lane = lax.broadcasted_iota(jnp.int32, (n_tok, 128), 1)
-        for r in range(n):
-            at = pl.ds(lanes * r + whole, 128)
-            for i, own in ((0, lane < 64), (1, lane >= 64)):
-                rows = pl.ds(n_tok * i, n_tok)
+            for i in range(2):
+                rows = pl.ds(rows_h * i, rows_h)
                 mid = h[rows, at].astype(F32)
-                h[rows, at] = jnp.where(own, mid, pltpu.roll(mid, 64, 1)).astype(BF)
+                mask = low_h if i == 0 else ~low_h
+                h[rows, at] = jnp.where(mask, mid, pltpu.roll(mid, 64, 1)).astype(BF)
         dims = (((1,), (1,)), ((), ()))
-        out = lax.dot_general(w[...], h[pl.ds(n_tok, n_tok), :], dims, preferred_element_type=F32)
-        far[...] = (out * scale_ref[:, pl.ds(n_tok, n_tok)]).astype(BF)
-        out = lax.dot_general(w[...], h[pl.ds(0, n_tok), :], dims, preferred_element_type=F32)
-        near[...] = out * scale_ref[:, pl.ds(0, n_tok)] + routed_ref[...]
+        out = lax.dot_general(w[...], h[...], dims, preferred_element_type=F32)
+        if far:
+            out_ref[...] = (out * scale_ref[...]).astype(BF)
+        else:
+            out_ref[...] = out * scale_ref[...] + routed_ref[...]
 
     vm = pl.BlockSpec(memory_space=pltpu.VMEM)
     return pl.pallas_call(
         kernel,
-        out_shape=[
-            jax.ShapeDtypeStruct((2 * half, n_tok), BF),
-            jax.ShapeDtypeStruct((2 * half, n_tok), F32),
-        ],
-        in_specs=[SMEM, ANY, ANY, vm, vm] + [ANY] * n,
-        out_specs=[vm, vm],
+        out_shape=jax.ShapeDtypeStruct((2 * half, n_tok), BF if far else F32),
+        in_specs=[SMEM, vm] + [ANY] * (4 + n) + ([] if far else [vm]),
+        out_specs=vm,
         scratch_shapes=[
             pltpu.VMEM((2 * half, n * lanes), BF),
-            pltpu.VMEM((both, n * lanes), BF),
+            pltpu.VMEM((n_tok, n * lanes), BF),
             pltpu.SemaphoreType.DMA((n, 3)),
             pltpu.SemaphoreType.DMA((4, 3)),
         ],
         compiler_params=pltpu.CompilerParams(vmem_limit_bytes=24 << 20),
         cost_estimate=pl.CostEstimate(
-            flops=2 * 2 * half * n * lanes * both, bytes_accessed=6 << 20, transcendentals=0
+            flops=2 * 2 * half * n * lanes * n_tok, bytes_accessed=4 << 20, transcendentals=0
         ),
-        name="shared_down",
-    )(where, direct, crossed, scale, routed, *pieces)
+        name="down_far" if far else "down_near",
+    )(where, scale, *hidden, *pieces, *([] if far else [routed]))
 
 
 def exchanged(
@@ -508,7 +519,7 @@
     top = expert_ids.shape[1]
     width = w_shared_gate.shape[1] // (n_dp * n_g)
 
-    some = expert_ids[0, 0] >= 0
+    some = where[0] >= 0
 
     def apart(step, *operands):
         shapes = jax.eval_shape(step, *operands)
@@ -529,40 +540,45 @@
     )
     gu = [packed[0]] + [swap(packed[k], "dp", k) for k in range(1, n_dp)]
 
-    def spread(q):
-        direct = jnp.stack([q, swap(q, "tensor", 2)])
-        return direct, swap(direct, "tensor", 1)
-
     def cross(piece, r):
         route = [(i * n_t + j, (j ^ r) * n_t + i) for i in range(n_dp) for j in range(n_t)]
         return lax.ppermute(piece, ("dp", "tensor"), route)
 
-    def routed_step(q, piece, *weights):
-        direct = jnp.stack([q, swap(q, "tensor", 2)])
-        direct, other = lax.optimization_barrier((direct, swap(q, "groups", 1)))
-        crossed, other = lax.optimization_barrier((swap(direct, "tensor", 1), other))
-        over_x = swap(other, "tensor", 2)
-        piece = cross(piece, 0)
-        give, keep = routed_experts(where, direct, crossed, *weights, top)
-        other, over_x, give, piece = lax.optimization_barrier((other, over_x, give, piece))
-        other = jnp.stack([other, over_x])
-        return (direct, crossed), (other, swap(other, "tensor", 1)), give, keep, piece
-
-    tok_own, tok_other, give, keep, first = apart(
-        routed_step, over_z, packed[n_dp], w_expert_gate_t, w_expert_up_t, w_expert_down
-    )
-    hidden, scale = shared_hidden(
-        where, tok_own, tok_other, gu, shared_gate_vec[None, :], give, width
-    )
-
-    def gather_step(h, out, kept):
-        got = swap(out, "tensor", 1).astype(F32)
-        return spread(h), kept[0] + got[0], (kept[1] + got[1]).astype(BF)
-
-    (h_direct, h_crossed), routed, routed_far = apart(gather_step, hidden, give, keep)
-
+    def routed_step(q, *weights):
+        over_x, other = swap(q, "tensor", 2), swap(q, "groups", 1)
+        over_core = swap(q, "tensor", 1)
+        over_x, other = lax.optimization_barrier((over_x, other))
+        over_both, other = lax.optimization_barrier((swap(over_x, "tensor", 1), other))
+        other_x = swap(other, "tensor", 2)
+        own = (q, over_core, over_x, over_both)
+        give, keep = routed_experts(where, own, *weights, top)
+        other, other_x, give = lax.optimization_barrier((other, other_x, give))
+        others = (other, swap(other, "tensor", 1), other_x, swap(other_x, "tensor", 1))
+        others, give = lax.optimization_barrier((others, give))
+        return own, others, swap(give, "tensor", 1), keep
+
+    tok_own, tok_other, got, keep = apart(
+        routed_step, over_z, w_expert_gate_t, w_expert_up_t, w_expert_down
+    )
+    vec = shared_gate_vec[None, :]
+    far_hidden, far_scale = shared_hidden(where, tok_other, gu, vec, got, width)
+
+    def gather_step(h, tokens_here, pieces):
+        over_x = swap(h, "tensor", 2)
+        near = shared_hidden(where, tokens_here, pieces, vec, h, width)
+        over_x, near = lax.optimization_barrier((over_x, near))
+        return [h, swap(h, "tensor", 1), over_x, swap(over_x, "tensor", 1)], near
+
+    far_hidden, first = lax.optimization_barrier((far_hidden, cross(packed[n_dp], 0)))
+    gathered, (near_hidden, near_scale) = apart(gather_step, far_hidden, tok_own, gu)
+    near_x, near_core = swap(near_hidden, "tensor", 2), swap(near_hidden, "tensor", 1)
     down = [first] + [cross(packed[n_dp + r], r) for r in range(1, n_dp)]
-    far, near = shared_down(where, down, h_direct, h_crossed, scale, routed, width)
+    far = shared_down(where, down, gathered, far_scale, width, True, None)
+    got = got.astype(F32)
+    routed = keep[0] + got[0]
+    routed_far = (keep[1] + got[1]).astype(BF)
+    gathered = [near_hidden, near_core, near_x, swap(near_x, "tensor", 1)]
+    near = shared_down(where, down, gathered, near_scale, width, False, routed)
     total = near + swap(far, "groups", 1).astype(F32) + swap(routed_far, "tensor", 2).astype(F32)
     done = total[:, :rows]
     for k in range(1, n_dp):

time: 157 us -> 147 us (0.936)
  waiting for transfers between devices: 60.1 us -> 40.7 us
  Pallas kernels: 48.3 us -> 55.2 us
  starting transfers between devices: 42 us -> 44.8 us
    ppermute x19 -> x25, waiting for transfers between devices: 60 us -> 40.7 us  [swap(): return lax.ppermute(x, axis, [(i, i ^ bit) for i in range(n)])]
    ppermute x19 -> x25, starting transfers between devices: 25.5 us -> 36.7 us  [swap(): return lax.ppermute(x, axis, [(i, i ^ bit) for i in range(n)])]
    ppermute x4, starting transfers between devices: 16.5 us -> 8.06 us  [cross(): return lax.ppermute(piece, ('dp', 'tensor'), route)]
    pallas_call x2 -> x4, Pallas kernels: 11.7 us -> 17 us  [the longest x2 10.9 us: shared_hidden(): pl.pallas_call(kernel, out_shape=[jax.ShapeDtypeStruct((half, 2 * width),...]
    another operation x4 -> x1, other arithmetic: 2.59 us -> 0.19 us  [the longest x1 1.22 us: spread(): direct = jnp.stack([q, swap(q, 'tensor', 2)])]
    add x0 -> x1, other arithmetic: none -> 1.78 us  [exchanged(): routed = keep[0] + got[0]]
  transfers between devices with their start and end apart: 23 -> 29, of which waited for: 11 -> 13; matrix products, arithmetic and copies ran while one was open for 2% -> 2% of each run, Pallas kernels for 27% -> 37%
where the time goes in v3:
time: 147 us; the launch traced here: 146 us
  Pallas kernels  55.2 us (38%)
  starting transfers between devices  44.8 us (30%)
  waiting for transfers between devices  40.7 us (28%)
  other arithmetic  4.26 us (3%)
    ppermute x25, waiting for transfers between devices, swap(): return lax.ppermute(x, axis, [(i, i ^ bit) for i in range(n)])  40.7 us
    ppermute x25, starting transfers between devices, swap(): return lax.ppermute(x, axis, [(i, i ^ bit) for i in range(n)])  36.7 us
    pallas_call x1, Pallas kernels, routed_experts(): pl.pallas_call(kernel, grid=(e_dev,), out_shape=[jax.ShapeDtypeStruct((2,...  32.3 us
    pallas_call x2, Pallas kernels, shared_hidden(): pl.pallas_call(kernel, out_shape=[jax.ShapeDtypeStruct((half, 2 * width),...  10.9 us
    ppermute x4, starting transfers between devices, cross(): return lax.ppermute(piece, ('dp', 'tensor'), route)  8.06 us
    pallas_call x2, Pallas kernels, shared_down(): pl.pallas_call(kernel, out_shape=jax.ShapeDtypeStruct((2 * half, n_tok),...  6.12 us
    pallas_call x1, Pallas kernels, pack(): pl.pallas_call(kernel, out_shape=[jax.ShapeDtypeStruct((d_part, 2 * width...  4.2 us
  transfers between devices with their start and end apart: 29, of which 13 were waited for; matrix products, arithmetic and copies ran while one was open for 2% of the time, Pallas kernels for 37%

profile of v3, /device:TPU:0, one launch (start us, length us, event | category | flops | bytes accessed | tf_op | source)
XLA Modules:
  0.0 146.2 jit_solution(3381555557620203162)
XLA Ops:
  0.1 1.6 %token_rows.1 = bf16[32,1920]{1,0:T(8,128)(2,1)S(1)} custom-call(s32[3]{0:T(128)S(1)} %pad_add_fusion.where_ref, bf16[128,1792]{1,0:T(8,128)(2,1)} %tok_ref.1, s32[8,128]{1,0:T(8,128)} %bitcast.19, f32[8,128]{1,0:T(8,128)} %bitcast.20), custom_call_target="tpu_custom_call" | custom-call | tf_op jit(solution)/shard_map/token_rows/pallas_call | solution.py:129
  1.7 15.5 %conditional.3 = (bf16[4,32,1920]{2,1,0:T(8,128)(2,1)S(1)}, bf16[448,640]{1,0:T(8,128)(2,1)}, bf16[448,640]{1,0:T(8,128)(2,1)}, bf16[448,640]{1,0:T(8,128)(2,1)}...) conditional(s32[]{:T(128)} %convert_element_type.38, () %tuple.37, ...), branch_computations={%region_0.0_spmd, %region_1.0_spmd} | conditional | flops 737280 | bytes 10846400 | solution.py:527
  1.7 3.1 %collective-permute-start.11 = (bf16[32,1920]{1,0:T(8,128)(2,1)S(1)}, bf16[32,1920]{1,0:T(8,128)(2,1)S(1)}, u32[]{:S(2)}, u32[]{:S(2)}) collective-permute-start(bf16[32,1920]{1,0:T(8,128)(2,1)S(1)} %get-tuple-element.47), channel_id=1, source_target_pairs={{0,4},{4,0},{8,12},{12,8},{1,5},{5,1},{9,13},{13,9},{2,6},{6,2},{1... | collective-permute-start | bytes 368648 | tf_op jit(solution)/shard_map/cond/branch_1_fun/ppermute | solution.py:90
  4.8 2.6 %collective-permute-start.12 = (bf16[32,1920]{1,0:T(8,128)(2,1)S(1)}, bf16[32,1920]{1,0:T(8,128)(2,1)S(1)}, u32[]{:S(2)}, u32[]{:S(2)}) collective-permute-start(bf16[32,1920]{1,0:T(8,128)(2,1)S(1)} %get-tuple-element.47), channel_id=1, source_target_pairs={{0,8},{4,12},{8,0},{12,4},{1,9},{5,13},{9,1},{13,5},{2,10},{6,14},... | collective-permute-start | bytes 368648 | tf_op jit(solution)/shard_map/cond/branch_1_fun/ppermute | solution.py:90
  7.4 4.2 %pack.1 = (bf16[448,640]{1,0:T(8,128)(2,1)}, bf16[448,640]{1,0:T(8,128)(2,1)}, bf16[448,640]{1,0:T(8,128)(2,1)}, bf16[448,640]{1,0:T(8,128)(2,1)}, bf16[224,640]...) custom-call(s32[3]{0:T(128)S(1)} %get-tuple-element.48.where_ref, ...), custom_call_target="tpu_custom_call" | custom-call | bytes 8388608 | tf_op jit(solution)/shard_map/cond/branch_1_fun/pack/pallas_call | solution.py:196
  11.6 5.5 %collective-permute-done.12 = bf16[32,1920]{1,0:T(8,128)(2,1)S(1)} collective-permute-done((bf16[32,1920]{1,0:T(8,128)(2,1)S(1)}, bf16[32,1920]{1,0:T(8,128)(2,1)S(1)}, u32[]{:S(2)}, u32[]{:S(2)}) %collective-permute-start.12) | collective-permute-done | bytes 122912 | tf_op jit(solution)/shard_map/cond/branch_1_fun/ppermute | solution.py:90
  17.2 1.9 %collective-permute-start.14 = (bf16[448,640]{1,0:T(8,128)(2,1)}, bf16[448,640]{1,0:T(8,128)(2,1)S(1)}, u32[]{:S(2)}, u32[]{:S(2)}) collective-permute-start(bf16[448,640]{1,0:T(8,128)(2,1)} %get-tuple-element.130), channel_id=1, source_target_pairs={{0,4},{4,0},{8,12},{12,8},{1,5},{5,1},{9,13},{13,9},{2,6},{6,2},{1... | collective-permute-start | bytes 1720328 | tf_op jit(solution)/shard_map/ppermute | solution.py:90
  21.7 54.1 %conditional.4 = (bf16[4,32,1920]{2,1,0:T(8,128)(2,1)S(1)}, bf16[4,32,1920]{2,1,0:T(8,128)(2,1)}, bf16[4,32,1920]{2,1,0:T(8,128)(2,1)}, bf16[4,32,1920]{2,1,0:T(...) conditional(s32[]{:T(128)} %convert_element_type.38, () %tuple.36, ...), branch_computations={%region_2.0_spmd, %region_3.0_spmd} | conditional | flops 10569646080 | bytes 73466256 | solution.py:527
  24.7 8.5 %collective-permute-done.1.rest_2_ = bf16[4,32,1920]{2,1,0:T(8,128)(2,1)} collective-permute-done((bf16[4,32,1920]{2,1,0:T(8,128)(2,1)S(1)}, bf16[4,32,1920]{2,1,0:T(8,128)(2,1)}, u32[]{:S(2)}, u32[]{:S(2)}) %collective-permute-start.1) | collective-permute-done | bytes 491552 | tf_op jit(solution)/shard_map/cond/branch_1_fun/ppermute | solution.py:90
  34.9 2.4 %collective-permute-done.3.rest_3_ = bf16[4,32,1920]{2,1,0:T(8,128)(2,1)} collective-permute-done((bf16[4,32,1920]{2,1,0:T(8,128)(2,1)}, bf16[4,32,1920]{2,1,0:T(8,128)(2,1)}, u32[]{:S(2)}, u32[]{:S(2)}) %collective-permute-start.3) | collective-permute-done | bytes 491552 | tf_op jit(solution)/shard_map/cond/branch_1_fun/ppermute | solution.py:90
  37.8 32.3 %routed.1 = (bf16[2,448,512]{2,1,0:T(8,128)(2,1)S(1)}, f32[2,448,512]{2,1,0:T(8,128)}) custom-call(s32[3]{0:T(128)S(1)} %get-tuple-element.65.where_ref, bf16[4,32,1920]{2,1,0:T(8,128)(2,1)S(1)} %get-tuple-element.200.rest_0_, bf16[4,32,1920]{2,1,0:T(8,128)(2,1)} %collective-permute-done.rest_1_, bf16[4,32,1920]{2,1,0:T(8,128)(2,1)} %collective-permute-done.1.rest_2_, ...), custom_call_target="tpu_custom_call" | custom-call | flops 10569646080 | bytes 55050240 | tf_op jit(solution)/shard_map/cond/branch_1_fun/routed/pallas_call | solution.py:319
  70.7 1.7 %collective-permute-done.5 = bf16[4,32,1920]{2,1,0:T(8,128)(2,1)} collective-permute-done((bf16[4,32,1920]{2,1,0:T(8,128)(2,1)}, bf16[4,32,1920]{2,1,0:T(8,128)(2,1)}, u32[]{:S(2)}, u32[]{:S(2)}) %collective-permute-start.5) | collective-permute-done | bytes 491552 | tf_op jit(solution)/shard_map/cond/branch_1_fun/ppermute | solution.py:90
  73.3 2.4 %collective-permute-done.7 = bf16[2,448,512]{2,1,0:T(8,128)(2,1)} collective-permute-done((bf16[2,448,512]{2,1,0:T(8,128)(2,1)S(1)}, bf16[2,448,512]{2,1,0:T(8,128)(2,1)}, u32[]{:S(2)}, u32[]{:S(2)}) %collective-permute-start.7) | collective-permute-done | bytes 917536 | tf_op jit(solution)/shard_map/cond/branch_1_fun/ppermute | solution.py:90
  75.7 1.7 %collective-permute-start.17 = (bf16[224,640]{1,0:T(8,128)(2,1)}, bf16[224,640]{1,0:T(8,128)(2,1)S(1)}, u32[]{:S(2)}, u32[]{:S(2)}) collective-permute-start(bf16[224,640]{1,0:T(8,128)(2,1)} %get-tuple-element.135), channel_id=1, source_target_pairs={{0,0},{1,4},{2,8},{3,12},{4,1},{5,5},{6,9},{7,13},{8,2},{9,6},{10,... | collective-permute-start | bytes 860168 | tf_op jit(solution)/shard_map/ppermute | solution.py:545
  77.5 2.1 %collective-permute-start.21 = (bf16[224,640]{1,0:T(8,128)(2,1)}, bf16[224,640]{1,0:T(8,128)(2,1)S(1)}, u32[]{:S(2)}, u32[]{:S(2)}) collective-permute-start(bf16[224,640]{1,0:T(8,128)(2,1)} %get-tuple-element.144), channel_id=1, source_target_pairs={{0,4},{1,0},{2,12},{3,8},{4,5},{5,1},{6,13},{7,9},{8,6},{9,2},{10,... | collective-permute-start | bytes 860168 | tf_op jit(solution)/shard_map/ppermute | solution.py:545
  81.9 2.6 %collective-permute-start.22 = (bf16[224,640]{1,0:T(8,128)(2,1)}, bf16[224,640]{1,0:T(8,128)(2,1)S(1)}, u32[]{:S(2)}, u32[]{:S(2)}) collective-permute-start(bf16[224,640]{1,0:T(8,128)(2,1)} %get-tuple-element.145), channel_id=1, source_target_pairs={{0,8},{1,12},{2,0},{3,4},{4,9},{5,13},{6,1},{7,5},{8,10},{9,14},{1... | collective-permute-start | bytes 860168 | tf_op jit(solution)/shard_map/ppermute | solution.py:545
  84.5 1.6 %collective-permute-start.23 = (bf16[224,640]{1,0:T(8,128)(2,1)}, bf16[224,640]{1,0:T(8,128)(2,1)S(1)}, u32[]{:S(2)}, u32[]{:S(2)}) collective-permute-start(bf16[224,640]{1,0:T(8,128)(2,1)} %get-tuple-element.146), channel_id=1, source_target_pairs={{0,12},{1,8},{2,4},{3,0},{4,13},{5,9},{6,5},{7,1},{8,14},{9,10},{1... | collective-permute-start | bytes 860168 | tf_op jit(solution)/shard_map/ppermute | solution.py:545
  86.2 5.8 %shared_hidden.3 = (bf16[256,640]{1,0:T(8,128)(2,1)S(1)}, f32[1,512]{1,0:T(1,128)S(1)}) custom-call(s32[3]{0:T(128)S(1)} %copy-done.9, bf16[4,32,1920]{2,1,0:T(8,128)(2,1)} %get-tuple-element.125.rest_0_, bf16[4,32,1920]{2,1,0:T(8,128)(2,1)} %get-tuple-element.126.rest_1_, bf16[4,32,1920]{2,1,0:T(8,128)(2,1)} %get-tuple-element.127.rest_2_, ...), custom_call_target="tpu_custom_call" | custom-call | flops 1174405120 | bytes 4194304 | tf_op jit(solution)/shard_map/shared_hidden/pallas_call | solution.py:398
  92.0 18.2 %conditional.5 = (bf16[256,640]{1,0:T(8,128)(2,1)S(1)}, bf16[256,640]{1,0:T(8,128)(2,1)}, bf16[256,640]{1,0:T(8,128)(2,1)}, bf16[256,640]{1,0:T(8,128)(2,1)}, bf...) conditional(s32[]{:T(128)} %convert_element_type.38, () %tuple.35, (bf16[256,640]{1,0:T(8,128)(2,1)S(1)}, ...), branch_computations={%region_4.0_spmd, %region_5.0_spmd} | conditional | flops 1174405120 | bytes 8781992 | solution.py:527
  92.0 10.9 %collective-permute-start.9 = (bf16[256,640]{1,0:T(8,128)(2,1)S(1)}, bf16[256,640]{1,0:T(8,128)(2,1)}, u32[]{:S(2)}, u32[]{:S(2)}) collective-permute-start(bf16[256,640]{1,0:T(8,128)(2,1)S(1)} %get-tuple-element.216.rest_9_), channel_id=1, source_target_pairs={{0,2},{1,3},{2,0},{3,1},{4,6},{5,7},{6,4},{7,5},{8,10},{9,11},{10,... | collective-permute-start | bytes 983048 | tf_op jit(solution)/shard_map/cond/branch_1_fun/ppermute | solution.py:90
  102.8 5.1 %shared_hidden.2 = (bf16[256,640]{1,0:T(8,128)(2,1)S(1)}, f32[1,512]{1,0:T(1,128)S(1)}) custom-call(s32[3]{0:T(128)S(1)} %get-tuple-element.80.where_ref, bf16[4,32,1920]{2,1,0:T(8,128)(2,1)S(1)} %get-tuple-element.81.rest_0_, bf16[4,32,1920]{2,1,0:T(8,128)(2,1)} %get-tuple-element.82.rest_1_, bf16[4,32,1920]{2,1,0:T(8,128)(2,1)} %get-tuple-element.83.rest_2_, ...), custom_call_target="tpu_custom_call" | custom-call | flops 1174405120 | bytes 4194304 | tf_op jit(solution)/shard_map/cond/branch_1_fun/shared_hidden/pallas_call | solution.py:398
  108.6 1.6 %collective-permute-done.10 = bf16[256,640]{1,0:T(8,128)(2,1)} collective-permute-done((bf16[256,640]{1,0:T(8,128)(2,1)}, bf16[256,640]{1,0:T(8,128)(2,1)}, u32[]{:S(2)}, u32[]{:S(2)}) %collective-permute-start.10) | collective-permute-done | bytes 327712 | tf_op jit(solution)/shard_map/cond/branch_1_fun/ppermute | solution.py:90
  110.2 2.2 %collective-permute-start.19 = (bf16[256,640]{1,0:T(8,128)(2,1)S(1)}, bf16[256,640]{1,0:T(8,128)(2,1)S(1)}, u32[]{:S(2)}, u32[]{:S(2)}) collective-permute-start(bf16[256,640]{1,0:T(8,128)(2,1)S(1)} %get-tuple-element.142.rest_0_), channel_id=1, source_target_pairs={{0,2},{1,3},{2,0},{3,1},{4,6},{5,7},{6,4},{7,5},{8,10},{9,11},{10,... | collective-permute-start | bytes 983048 | tf_op jit(solution)/shard_map/ppermute | solution.py:90
  112.4 1.8 %fusion.1 = (f32[448,512]{1,0:T(8,128)S(1)}, bf16[448,512]{1,0:T(8,128)(2,1)S(1)}) fusion(f32[2,448,512]{2,1,0:T(8,128)S(1)} %convert_element_type.39, f32[2,448,512]{2,1,0:T(8,128)} %get-tuple-element.147), kind=kLoop, calls=%fused_computation.4 | loop fusion | flops 688128 | bytes 5046272 | tf_op jit(solution)/shard_map/add | solution.py:578
  114.4 3.2 %down_far.1 = bf16[448,512]{1,0:T(8,128)(2,1)S(1)} custom-call(s32[3]{0:T(128)S(1)} %copy-done.10, f32[1,512]{1,0:T(1,128)S(1)} %get-tuple-element.148.scale_ref, bf16[256,640]{1,0:T(8,128)(2,1)S(1)} %get-tuple-element.149.rest_0_, bf16[256,640]{1,0:T(8,128)(2,1)} %get-tuple-element.150.rest_1_, bf16[256,640]{1,0:T(8,128)(2,1)} %get-tuple-element.151.rest_2_, ...), custom_call_target="tpu_custom_call" | custom-call | flops 704643072 | bytes 4194304 | tf_op jit(solution)/shard_map/down_far/pallas_call | solution.py:484
  117.6 1.6 %collective-permute-start.24 = (bf16[448,512]{1,0:T(8,128)(2,1)S(1)}, bf16[448,512]{1,0:T(8,128)(2,1)S(1)}, u32[]{:S(2)}, u32[]{:S(2)}) collective-permute-start(bf16[448,512]{1,0:T(8,128)(2,1)S(1)} %down_far.1), channel_id=1, source_target_pairs={{0,16},{16,0},{1,17},{17,1},{2,18},{18,2},{3,19},{19,3},{4,20},{20... | collective-permute-start | bytes 1376264 | tf_op jit(solution)/shard_map/ppermute | solution.py:90
  119.2 1.7 %collective-permute-done.19.rest_2_ = bf16[256,640]{1,0:T(8,128)(2,1)S(1)} collective-permute-done((bf16[256,640]{1,0:T(8,128)(2,1)S(1)}, bf16[256,640]{1,0:T(8,128)(2,1)S(1)}, u32[]{:S(2)}, u32[]{:S(2)}) %collective-permute-start.19) | collective-permute-done | bytes 327712 | tf_op jit(solution)/shard_map/ppermute | solution.py:90
  120.9 1.6 %collective-permute-done.20.rest_3_ = bf16[256,640]{1,0:T(8,128)(2,1)S(1)} collective-permute-done((bf16[256,640]{1,0:T(8,128)(2,1)S(1)}, bf16[256,640]{1,0:T(8,128)(2,1)S(1)}, u32[]{:S(2)}, u32[]{:S(2)}) %collective-permute-start.20) | collective-permute-done | bytes 327712 | tf_op jit(solution)/shard_map/ppermute | solution.py:90
  122.5 2.9 %down_near.1 = f32[448,512]{1,0:T(8,128)S(1)} custom-call(s32[3]{0:T(128)S(1)} %copy-done.10, f32[1,512]{1,0:T(1,128)S(1)} %get-tuple-element.141.scale_ref, bf16[256,640]{1,0:T(8,128)(2,1)} %copy-done.7, bf16[256,640]{1,0:T(8,128)(2,1)S(1)} %collective-permute-done.18.rest_1_, bf16[256,640]{1,0:T(8,128)(2,1)S(1)} %collective-permute-done.19.rest_2_, ...), custom_call_target="tpu_custom_call" | custom-call | flops 704643072 | bytes 4194304 | tf_op jit(solution)/shard_map/down_near/pallas_call | solution.py:484
  125.4 4.8 %collective-permute-done.25 = bf16[448,512]{1,0:T(8,128)(2,1)S(1)} collective-permute-done((bf16[448,512]{1,0:T(8,128)(2,1)S(1)}, bf16[448,512]{1,0:T(8,128)(2,1)S(1)}, u32[]{:S(2)}, u32[]{:S(2)}) %collective-permute-start.25) | collective-permute-done | bytes 458784 | tf_op jit(solution)/shard_map/ppermute | solution.py:90
  130.5 3.5 %collective-permute-start.26 = (bf16[448,128]{1,0:T(8,128)(2,1)S(1)}, bf16[448,128]{1,0:T(8,128)(2,1)S(1)}, u32[]{:S(2)}, u32[]{:S(2)}) collective-permute-start(bf16[448,128]{1,0:T(8,128)(2,1)S(1)} %get-tuple-element.169), channel_id=1, source_target_pairs={{0,4},{4,0},{8,12},{12,8},{1,5},{5,1},{9,13},{13,9},{2,6},{6,2},{1... | collective-permute-start | bytes 344072 | tf_op jit(solution)/shard_map/ppermute | solution.py:90
  137.5 7.9 %collective-permute-done.27 = bf16[448,128]{1,0:T(8,128)(2,1)S(1)} collective-permute-done((bf16[448,128]{1,0:T(8,128)(2,1)S(1)}, bf16[448,128]{1,0:T(8,128)(2,1)S(1)}, u32[]{:S(2)}, u32[]{:S(2)}) %collective-permute-start.27) | collective-permute-done | bytes 114720 | tf_op jit(solution)/shard_map/ppermute | solution.py:90
  (70 shorter events, 17.0 us)
Async XLA Ops:
  0.1 21.6 %copy-start.8 = (s32[3]{0:T(128)}, s32[3]{0:T(128)S(1)}, u32[]{:S(2)}) copy-start(s32[3]{0:T(128)S(1)} %pad_add_fusion.where_ref) | copy-start | bytes 40
  1.7 9.9 %collective-permute-start.11 = (bf16[32,1920]{1,0:T(8,128)(2,1)S(1)}, bf16[32,1920]{1,0:T(8,128)(2,1)S(1)}, u32[]{:S(2)}, u32[]{:S(2)}) collective-permute-start(bf16[32,1920]{1,0:T(8,128)(2,1)S(1)} %get-tuple-element.47), channel_id=1, source_target_pairs={{0,4},{4,0},{8,12},{12,8},{1,5},{5,1},{9,13},{13,9},{2,6},{6,2},{1... | collective-permute-start | bytes 368648 | tf_op jit(solution)/shard_map/cond/branch_1_fun/ppermute | solution.py:90
  4.8 12.3 %collective-permute-start.12 = (bf16[32,1920]{1,0:T(8,128)(2,1)S(1)}, bf16[32,1920]{1,0:T(8,128)(2,1)S(1)}, u32[]{:S(2)}, u32[]{:S(2)}) collective-permute-start(bf16[32,1920]{1,0:T(8,128)(2,1)S(1)} %get-tuple-element.47), channel_id=1, source_target_pairs={{0,8},{4,12},{8,0},{12,4},{1,9},{5,13},{9,1},{13,5},{2,10},{6,14},... | collective-permute-start | bytes 368648 | tf_op jit(solution)/shard_map/cond/branch_1_fun/ppermute | solution.py:90
  7.4 9.7 %collective-permute-start.13 = (bf16[32,1920]{1,0:T(8,128)(2,1)S(1)}, bf16[32,1920]{1,0:T(8,128)(2,1)S(1)}, u32[]{:S(2)}, u32[]{:S(2)}) collective-permute-start(bf16[32,1920]{1,0:T(8,128)(2,1)S(1)} %get-tuple-element.47), channel_id=1, source_target_pairs={{0,12},{4,8},{8,4},{12,0},{1,13},{5,9},{9,5},{13,1},{2,14},{6,10},... | collective-permute-start | bytes 368648 | tf_op jit(solution)/shard_map/cond/branch_1_fun/ppermute | solution.py:90
  17.2 63.9 %collective-permute-start.14 = (bf16[448,640]{1,0:T(8,128)(2,1)}, bf16[448,640]{1,0:T(8,128)(2,1)S(1)}, u32[]{:S(2)}, u32[]{:S(2)}) collective-permute-start(bf16[448,640]{1,0:T(8,128)(2,1)} %get-tuple-element.130), channel_id=1, source_target_pairs={{0,4},{4,0},{8,12},{12,8},{1,5},{5,1},{9,13},{13,9},{2,6},{6,2},{1... | collective-permute-start | bytes 1720328 | tf_op jit(solution)/shard_map/ppermute | solution.py:90
  19.1 65.4 %collective-permute-start.15 = (bf16[448,640]{1,0:T(8,128)(2,1)}, bf16[448,640]{1,0:T(8,128)(2,1)S(1)}, u32[]{:S(2)}, u32[]{:S(2)}) collective-permute-start(bf16[448,640]{1,0:T(8,128)(2,1)} %get-tuple-element.131), channel_id=1, source_target_pairs={{0,8},{4,12},{8,0},{12,4},{1,9},{5,13},{9,1},{13,5},{2,10},{6,14},... | collective-permute-start | bytes 1720328 | tf_op jit(solution)/shard_map/ppermute | solution.py:90
  20.2 65.9 %collective-permute-start.16 = (bf16[448,640]{1,0:T(8,128)(2,1)}, bf16[448,640]{1,0:T(8,128)(2,1)}, u32[]{:S(2)}, u32[]{:S(2)}) collective-permute-start(bf16[448,640]{1,0:T(8,128)(2,1)} %get-tuple-element.132), channel_id=1, source_target_pairs={{0,12},{4,8},{8,4},{12,0},{1,13},{5,9},{9,5},{13,1},{2,14},{6,10},... | collective-permute-start | bytes 1720328 | tf_op jit(solution)/shard_map/ppermute | solution.py:90
  21.7 58.0 %copy-start.11 = (bf16[1792]{0:T(1024)(128)(2,1)S(1)}, bf16[1792]{0:T(1024)(128)(2,1)}, u32[]{:S(2)}) copy-start(bf16[1792]{0:T(1024)(128)(2,1)} %param.19) | copy-start | bytes 10756
  21.7 11.5 %collective-permute-start.1 = (bf16[4,32,1920]{2,1,0:T(8,128)(2,1)S(1)}, bf16[4,32,1920]{2,1,0:T(8,128)(2,1)}, u32[]{:S(2)}, u32[]{:S(2)}) collective-permute-start(bf16[4,32,1920]{2,1,0:T(8,128)(2,1)S(1)} %get-tuple-element.200.rest_0_), channel_id=1, source_target_pairs={{0,2},{1,3},{2,0},{3,1},{4,6},{5,7},{6,4},{7,5},{8,10},{9,11},{10,... | collective-permute-start | bytes 1474568 | tf_op jit(solution)/shard_map/cond/branch_1_fun/ppermute | solution.py:90
  23.2 11.2 %collective-permute-start.2 = (bf16[4,32,1920]{2,1,0:T(8,128)(2,1)S(1)}, bf16[4,32,1920]{2,1,0:T(8,128)(2,1)}, u32[]{:S(2)}, u32[]{:S(2)}) collective-permute-start(bf16[4,32,1920]{2,1,0:T(8,128)(2,1)S(1)} %get-tuple-element.200.rest_0_), channel_id=1, source_target_pairs={{0,16},{16,0},{1,17},{17,1},{2,18},{18,2},{3,19},{19,3},{4,20},{20... | collective-permute-start | bytes 1474568 | tf_op jit(solution)/shard_map/cond/branch_1_fun/ppermute | solution.py:90
  34.4 2.9 %collective-permute-start.3 = (bf16[4,32,1920]{2,1,0:T(8,128)(2,1)}, bf16[4,32,1920]{2,1,0:T(8,128)(2,1)}, u32[]{:S(2)}, u32[]{:S(2)}) collective-permute-start(bf16[4,32,1920]{2,1,0:T(8,128)(2,1)} %collective-permute-done.1.rest_2_), channel_id=1, source_target_pairs={{0,1},{1,0},{2,3},{3,2},{4,5},{5,4},{6,7},{7,6},{8,9},{9,8},{10,11... | collective-permute-start | bytes 1474568 | tf_op jit(solution)/shard_map/cond/branch_1_fun/ppermute | solution.py:90
  34.4 3.4 %collective-permute-start = (bf16[4,32,1920]{2,1,0:T(8,128)(2,1)S(1)}, bf16[4,32,1920]{2,1,0:T(8,128)(2,1)}, u32[]{:S(2)}, u32[]{:S(2)}) collective-permute-start(bf16[4,32,1920]{2,1,0:T(8,128)(2,1)S(1)} %get-tuple-element.200.rest_0_), channel_id=1, source_target_pairs={{0,1},{1,0},{2,3},{3,2},{4,5},{5,4},{6,7},{7,6},{8,9},{9,8},{10,11... | collective-permute-start | bytes 1474568 | tf_op jit(solution)/shard_map/cond/branch_1_fun/ppermute | solution.py:90
  37.3 32.9 %collective-permute-start.4 = (bf16[4,32,1920]{2,1,0:T(8,128)(2,1)}, bf16[4,32,1920]{2,1,0:T(8,128)(2,1)}, u32[]{:S(2)}, u32[]{:S(2)}) collective-permute-start(bf16[4,32,1920]{2,1,0:T(8,128)(2,1)} %collective-permute-done.2), channel_id=1, source_target_pairs={{0,2},{1,3},{2,0},{3,1},{4,6},{5,7},{6,4},{7,5},{8,10},{9,11},{10,... | collective-permute-start | bytes 1474568 | tf_op jit(solution)/shard_map/cond/branch_1_fun/ppermute | solution.py:90
  70.2 2.3 %collective-permute-start.5 = (bf16[4,32,1920]{2,1,0:T(8,128)(2,1)}, bf16[4,32,1920]{2,1,0:T(8,128)(2,1)}, u32[]{:S(2)}, u32[]{:S(2)}) collective-permute-start(bf16[4,32,1920]{2,1,0:T(8,128)(2,1)} %collective-permute-done.2), channel_id=1, source_target_pairs={{0,1},{1,0},{2,3},{3,2},{4,5},{5,4},{6,7},{7,6},{8,9},{9,8},{10,11... | collective-permute-start | bytes 1474568 | tf_op jit(solution)/shard_map/cond/branch_1_fun/ppermute | solution.py:90
  70.2 2.9 %collective-permute-start.6 = (bf16[4,32,1920]{2,1,0:T(8,128)(2,1)}, bf16[4,32,1920]{2,1,0:T(8,128)(2,1)}, u32[]{:S(2)}, u32[]{:S(2)}) collective-permute-start(bf16[4,32,1920]{2,1,0:T(8,128)(2,1)} %collective-permute-done.4), channel_id=1, source_target_pairs={{0,1},{1,0},{2,3},{3,2},{4,5},{5,4},{6,7},{7,6},{8,9},{9,8},{10,11... | collective-permute-start | bytes 1474568 | tf_op jit(solution)/shard_map/cond/branch_1_fun/ppermute | solution.py:90
  73.1 2.6 %collective-permute-start.7 = (bf16[2,448,512]{2,1,0:T(8,128)(2,1)S(1)}, bf16[2,448,512]{2,1,0:T(8,128)(2,1)}, u32[]{:S(2)}, u32[]{:S(2)}) collective-permute-start(bf16[2,448,512]{2,1,0:T(8,128)(2,1)S(1)} %get-tuple-element.77), channel_id=1, source_target_pairs={{0,1},{1,0},{2,3},{3,2},{4,5},{5,4},{6,7},{7,6},{8,9},{9,8},{10,11... | collective-permute-start | bytes 2752520 | tf_op jit(solution)/shard_map/cond/branch_1_fun/ppermute | solution.py:90
  75.7 10.4 %copy-start.9 = (s32[3]{0:T(128)S(1)}, s32[3]{0:T(128)}, u32[]{:S(2)}) copy-start(s32[3]{0:T(128)} %copy-done.8) | copy-start | bytes 40
  75.7 16.2 %collective-permute-start.17 = (bf16[224,640]{1,0:T(8,128)(2,1)}, bf16[224,640]{1,0:T(8,128)(2,1)S(1)}, u32[]{:S(2)}, u32[]{:S(2)}) collective-permute-start(bf16[224,640]{1,0:T(8,128)(2,1)} %get-tuple-element.135), channel_id=1, source_target_pairs={{0,0},{1,4},{2,8},{3,12},{4,1},{5,5},{6,9},{7,13},{8,2},{9,6},{10,... | collective-permute-start | bytes 860168 | tf_op jit(solution)/shard_map/ppermute | solution.py:545
  77.5 36.9 %collective-permute-start.21 = (bf16[224,640]{1,0:T(8,128)(2,1)}, bf16[224,640]{1,0:T(8,128)(2,1)S(1)}, u32[]{:S(2)}, u32[]{:S(2)}) collective-permute-start(bf16[224,640]{1,0:T(8,128)(2,1)} %get-tuple-element.144), channel_id=1, source_target_pairs={{0,4},{1,0},{2,12},{3,8},{4,5},{5,1},{6,13},{7,9},{8,6},{9,2},{10,... | collective-permute-start | bytes 860168 | tf_op jit(solution)/shard_map/ppermute | solution.py:545
  81.9 32.5 %collective-permute-start.22 = (bf16[224,640]{1,0:T(8,128)(2,1)}, bf16[224,640]{1,0:T(8,128)(2,1)S(1)}, u32[]{:S(2)}, u32[]{:S(2)}) collective-permute-start(bf16[224,640]{1,0:T(8,128)(2,1)} %get-tuple-element.145), channel_id=1, source_target_pairs={{0,8},{1,12},{2,0},{3,4},{4,9},{5,13},{6,1},{7,5},{8,10},{9,14},{1... | collective-permute-start | bytes 860168 | tf_op jit(solution)/shard_map/ppermute | solution.py:545
  84.5 29.8 %collective-permute-start.23 = (bf16[224,640]{1,0:T(8,128)(2,1)}, bf16[224,640]{1,0:T(8,128)(2,1)S(1)}, u32[]{:S(2)}, u32[]{:S(2)}) collective-permute-start(bf16[224,640]{1,0:T(8,128)(2,1)} %get-tuple-element.146), channel_id=1, source_target_pairs={{0,12},{1,8},{2,4},{3,0},{4,13},{5,9},{6,5},{7,1},{8,14},{9,10},{1... | collective-permute-start | bytes 860168 | tf_op jit(solution)/shard_map/ppermute | solution.py:545
  92.0 16.0 %collective-permute-start.9 = (bf16[256,640]{1,0:T(8,128)(2,1)S(1)}, bf16[256,640]{1,0:T(8,128)(2,1)}, u32[]{:S(2)}, u32[]{:S(2)}) collective-permute-start(bf16[256,640]{1,0:T(8,128)(2,1)S(1)} %get-tuple-element.216.rest_9_), channel_id=1, source_target_pairs={{0,2},{1,3},{2,0},{3,1},{4,6},{5,7},{6,4},{7,5},{8,10},{9,11},{10,... | collective-permute-start | bytes 983048 | tf_op jit(solution)/shard_map/cond/branch_1_fun/ppermute | solution.py:90
  102.8 5.8 %collective-permute-start.8 = (bf16[256,640]{1,0:T(8,128)(2,1)S(1)}, bf16[256,640]{1,0:T(8,128)(2,1)}, u32[]{:S(2)}, u32[]{:S(2)}) collective-permute-start(bf16[256,640]{1,0:T(8,128)(2,1)S(1)} %get-tuple-element.216.rest_9_), channel_id=1, source_target_pairs={{0,1},{1,0},{2,3},{3,2},{4,5},{5,4},{6,7},{7,6},{8,9},{9,8},{10,11... | collective-permute-start | bytes 983048 | tf_op jit(solution)/shard_map/cond/branch_1_fun/ppermute | solution.py:90
  108.0 2.2 %collective-permute-start.10 = (bf16[256,640]{1,0:T(8,128)(2,1)}, bf16[256,640]{1,0:T(8,128)(2,1)}, u32[]{:S(2)}, u32[]{:S(2)}) collective-permute-start(bf16[256,640]{1,0:T(8,128)(2,1)} %collective-permute-done.9), channel_id=1, source_target_pairs={{0,1},{1,0},{2,3},{3,2},{4,5},{5,4},{6,7},{7,6},{8,9},{9,8},{10,11... | collective-permute-start | bytes 983048 | tf_op jit(solution)/shard_map/cond/branch_1_fun/ppermute | solution.py:90
  110.2 10.7 %collective-permute-start.19 = (bf16[256,640]{1,0:T(8,128)(2,1)S(1)}, bf16[256,640]{1,0:T(8,128)(2,1)S(1)}, u32[]{:S(2)}, u32[]{:S(2)}) collective-permute-start(bf16[256,640]{1,0:T(8,128)(2,1)S(1)} %get-tuple-element.142.rest_0_), channel_id=1, source_target_pairs={{0,2},{1,3},{2,0},{3,1},{4,6},{5,7},{6,4},{7,5},{8,10},{9,11},{10,... | collective-permute-start | bytes 983048 | tf_op jit(solution)/shard_map/ppermute | solution.py:90
  114.2 16.0 %collective-permute-start.25 = (bf16[448,512]{1,0:T(8,128)(2,1)S(1)}, bf16[448,512]{1,0:T(8,128)(2,1)S(1)}, u32[]{:S(2)}, u32[]{:S(2)}) collective-permute-start(bf16[448,512]{1,0:T(8,128)(2,1)S(1)} %get-tuple-element.168), channel_id=1, source_target_pairs={{0,2},{1,3},{2,0},{3,1},{4,6},{5,7},{6,4},{7,5},{8,10},{9,11},{10,... | collective-permute-start | bytes 1376264 | tf_op jit(solution)/shard_map/ppermute | solution.py:90
  117.6 12.6 %collective-permute-start.24 = (bf16[448,512]{1,0:T(8,128)(2,1)S(1)}, bf16[448,512]{1,0:T(8,128)(2,1)S(1)}, u32[]{:S(2)}, u32[]{:S(2)}) collective-permute-start(bf16[448,512]{1,0:T(8,128)(2,1)S(1)} %down_far.1), channel_id=1, source_target_pairs={{0,16},{16,0},{1,17},{17,1},{2,18},{18,2},{3,19},{19,3},{4,20},{20... | collective-permute-start | bytes 1376264 | tf_op jit(solution)/shard_map/ppermute | solution.py:90
  119.2 1.7 %collective-permute-start.18 = (bf16[256,640]{1,0:T(8,128)(2,1)S(1)}, bf16[256,640]{1,0:T(8,128)(2,1)S(1)}, u32[]{:S(2)}, u32[]{:S(2)}) collective-permute-start(bf16[256,640]{1,0:T(8,128)(2,1)S(1)} %get-tuple-element.142.rest_0_), channel_id=1, source_target_pairs={{0,1},{1,0},{2,3},{3,2},{4,5},{5,4},{6,7},{7,6},{8,9},{9,8},{10,11... | collective-permute-start | bytes 983048 | tf_op jit(solution)/shard_map/ppermute | solution.py:90
  120.9 1.6 %collective-permute-start.20 = (bf16[256,640]{1,0:T(8,128)(2,1)S(1)}, bf16[256,640]{1,0:T(8,128)(2,1)S(1)}, u32[]{:S(2)}, u32[]{:S(2)}) collective-permute-start(bf16[256,640]{1,0:T(8,128)(2,1)S(1)} %collective-permute-done.19.rest_2_), channel_id=1, source_target_pairs={{0,1},{1,0},{2,3},{3,2},{4,5},{5,4},{6,7},{7,6},{8,9},{9,8},{10,11... | collective-permute-start | bytes 983048 | tf_op jit(solution)/shard_map/ppermute | solution.py:90
  130.5 7.0 %collective-permute-start.26 = (bf16[448,128]{1,0:T(8,128)(2,1)S(1)}, bf16[448,128]{1,0:T(8,128)(2,1)S(1)}, u32[]{:S(2)}, u32[]{:S(2)}) collective-permute-start(bf16[448,128]{1,0:T(8,128)(2,1)S(1)} %get-tuple-element.169), channel_id=1, source_target_pairs={{0,4},{4,0},{8,12},{12,8},{1,5},{5,1},{9,13},{13,9},{2,6},{6,2},{1... | collective-permute-start | bytes 344072 | tf_op jit(solution)/shard_map/ppermute | solution.py:90
  134.0 11.5 %collective-permute-start.27 = (bf16[448,128]{1,0:T(8,128)(2,1)S(1)}, bf16[448,128]{1,0:T(8,128)(2,1)S(1)}, u32[]{:S(2)}, u32[]{:S(2)}) collective-permute-start(bf16[448,128]{1,0:T(8,128)(2,1)S(1)} %get-tuple-element.171), channel_id=1, source_target_pairs={{0,8},{4,12},{8,0},{12,4},{1,9},{5,13},{9,1},{13,5},{2,10},{6,14},... | collective-permute-start | bytes 344072 | tf_op jit(solution)/shard_map/ppermute | solution.py:90
  135.5 9.9 %collective-permute-start.28 = (bf16[448,128]{1,0:T(8,128)(2,1)S(1)}, bf16[448,128]{1,0:T(8,128)(2,1)S(1)}, u32[]{:S(2)}, u32[]{:S(2)}) collective-permute-start(bf16[448,128]{1,0:T(8,128)(2,1)S(1)} %get-tuple-element.170), channel_id=1, source_target_pairs={{0,12},{4,8},{8,4},{12,0},{1,13},{5,9},{9,5},{13,1},{2,14},{6,10},... | collective-permute-start | bytes 344072 | tf_op jit(solution)/shard_map/ppermute | solution.py:90
  (9 other events, 45.2 us)

commit v4 on v3

--- a/solution.py
+++ b/solution.py
@@ -554,29 +554,29 @@
         give, keep = routed_experts(where, own, *weights, top)
         other, other_x, give = lax.optimization_barrier((other, other_x, give))
         others = (other, swap(other, "tensor", 1), other_x, swap(other_x, "tensor", 1))
-        others, give = lax.optimization_barrier((others, give))
-        return own, others, swap(give, "tensor", 1), keep
-
-    tok_own, tok_other, got, keep = apart(
+        return own, others, give, keep
+
+    tok_own, tok_other, give, keep = apart(
         routed_step, over_z, w_expert_gate_t, w_expert_up_t, w_expert_down
     )
     vec = shared_gate_vec[None, :]
-    far_hidden, far_scale = shared_hidden(where, tok_other, gu, vec, got, width)
-
-    def gather_step(h, tokens_here, pieces):
-        over_x = swap(h, "tensor", 2)
+    far_hidden, far_scale = shared_hidden(where, tok_other, gu, vec, give, width)
+
+    def gather_step(h, tokens_here, pieces, out, kept):
+        over_x, over_core = swap(h, "tensor", 2), swap(h, "tensor", 1)
         near = shared_hidden(where, tokens_here, pieces, vec, h, width)
-        over_x, near = lax.optimization_barrier((over_x, near))
-        return [h, swap(h, "tensor", 1), over_x, swap(over_x, "tensor", 1)], near
+        over_x, over_core, out, near = lax.optimization_barrier((over_x, over_core, out, near))
+        got = swap(out, "tensor", 1).astype(F32)
+        sums = kept[0] + got[0], (kept[1] + got[1]).astype(BF)
+        return [h, over_core, over_x, swap(over_x, "tensor", 1)], near, sums
 
     far_hidden, first = lax.optimization_barrier((far_hidden, cross(packed[n_dp], 0)))
-    gathered, (near_hidden, near_scale) = apart(gather_step, far_hidden, tok_own, gu)
+    gathered, (near_hidden, near_scale), (routed, routed_far) = apart(
+        gather_step, far_hidden, tok_own, gu, give, keep
+    )
     near_x, near_core = swap(near_hidden, "tensor", 2), swap(near_hidden, "tensor", 1)
     down = [first] + [cross(packed[n_dp + r], r) for r in range(1, n_dp)]
     far = shared_down(where, down, gathered, far_scale, width, True, None)
-    got = got.astype(F32)
-    routed = keep[0] + got[0]
-    routed_far = (keep[1] + got[1]).astype(BF)
     gathered = [near_hidden, near_core, near_x, swap(near_x, "tensor", 1)]
     near = shared_down(where, down, gathered, near_scale, width, False, routed)
     total = near + swap(far, "groups", 1).astype(F32) + swap(routed_far, "tensor", 2).astype(F32)

time: 147 us -> 144 us (0.980)
  other arithmetic: 4.26 us -> 1.75 us
  Pallas kernels: 55.2 us -> 53.4 us
    add x1 -> x0, other arithmetic: 1.78 us -> none  [exchanged(): routed = keep[0] + got[0]]
  transfers between devices with their start and end apart: 29 -> 29, of which waited for: 13 -> 13; matrix products, arithmetic and copies ran while one was open for 2% -> 1% of each run, Pallas kernels for 37% -> 36%
where the time goes in v4:
time: 144 us
  Pallas kernels  53.4 us (37%)
  starting transfers between devices  44.6 us (31%)
  waiting for transfers between devices  42 us (29%)
  other arithmetic  1.75 us (1%)
  local copies, waits for them, and re-layouts  1.66 us (1%)
    ppermute x25, waiting for transfers between devices, swap(): return lax.ppermute(x, axis, [(i, i ^ bit) for i in range(n)])  42 us
    ppermute x25, starting transfers between devices, swap(): return lax.ppermute(x, axis, [(i, i ^ bit) for i in range(n)])  36.7 us
    pallas_call x1, Pallas kernels, routed_experts(): pl.pallas_call(kernel, grid=(e_dev,), out_shape=[jax.ShapeDtypeStruct((2,...  31.1 us
    pallas_call x2, Pallas kernels, shared_hidden(): pl.pallas_call(kernel, out_shape=[jax.ShapeDtypeStruct((half, 2 * width),...  11.2 us
    ppermute x4, starting transfers between devices, cross(): return lax.ppermute(piece, ('dp', 'tensor'), route)  7.94 us
    pallas_call x2, Pallas kernels, shared_down(): pl.pallas_call(kernel, out_shape=jax.ShapeDtypeStruct((2 * half, n_tok),...  5.31 us
    pallas_call x1, Pallas kernels, pack(): pl.pallas_call(kernel, out_shape=[jax.ShapeDtypeStruct((d_part, 2 * width...  4.19 us
  transfers between devices with their start and end apart: 29, of which 13 were waited for; matrix products, arithmetic and copies ran while one was open for 1% of the time, Pallas kernels for 36%

profile of v4, /device:TPU:0, one launch (start us, length us, event | category | flops | bytes accessed | tf_op | source)
XLA Modules:
  0.0 143.7 jit_solution(17081006303445502568)
XLA Ops:
  0.1 1.6 %token_rows.1 = bf16[32,1920]{1,0:T(8,128)(2,1)S(1)} custom-call(s32[3]{0:T(128)S(1)} %pad_add_fusion.where_ref, bf16[128,1792]{1,0:T(8,128)(2,1)} %tok_ref.1, s32[8,128]{1,0:T(8,128)} %bitcast.19, f32[8,128]{1,0:T(8,128)} %bitcast.20), custom_call_target="tpu_custom_call" | custom-call | tf_op jit(solution)/shard_map/token_rows/pallas_call | solution.py:129
  1.7 15.5 %conditional.3 = (bf16[4,32,1920]{2,1,0:T(8,128)(2,1)S(1)}, bf16[448,640]{1,0:T(8,128)(2,1)}, bf16[448,640]{1,0:T(8,128)(2,1)}, bf16[448,640]{1,0:T(8,128)(2,1)}...) conditional(s32[]{:T(128)} %convert_element_type.38, () %tuple.36, ...), branch_computations={%region_0.0_spmd, %region_1.0_spmd} | conditional | flops 737280 | bytes 10846400 | solution.py:527
  1.7 3.1 %collective-permute-start.7 = (bf16[32,1920]{1,0:T(8,128)(2,1)S(1)}, bf16[32,1920]{1,0:T(8,128)(2,1)S(1)}, u32[]{:S(2)}, u32[]{:S(2)}) collective-permute-start(bf16[32,1920]{1,0:T(8,128)(2,1)S(1)} %get-tuple-element.51), channel_id=1, source_target_pairs={{0,4},{4,0},{8,12},{12,8},{1,5},{5,1},{9,13},{13,9},{2,6},{6,2},{1... | collective-permute-start | bytes 368648 | tf_op jit(solution)/shard_map/cond/branch_1_fun/ppermute | solution.py:90
  4.8 2.6 %collective-permute-start.8 = (bf16[32,1920]{1,0:T(8,128)(2,1)S(1)}, bf16[32,1920]{1,0:T(8,128)(2,1)S(1)}, u32[]{:S(2)}, u32[]{:S(2)}) collective-permute-start(bf16[32,1920]{1,0:T(8,128)(2,1)S(1)} %get-tuple-element.51), channel_id=1, source_target_pairs={{0,8},{4,12},{8,0},{12,4},{1,9},{5,13},{9,1},{13,5},{2,10},{6,14},... | collective-permute-start | bytes 368648 | tf_op jit(solution)/shard_map/cond/branch_1_fun/ppermute | solution.py:90
  7.4 4.2 %pack.1 = (bf16[448,640]{1,0:T(8,128)(2,1)}, bf16[448,640]{1,0:T(8,128)(2,1)}, bf16[448,640]{1,0:T(8,128)(2,1)}, bf16[448,640]{1,0:T(8,128)(2,1)}, bf16[224,640]...) custom-call(s32[3]{0:T(128)S(1)} %get-tuple-element.52.where_ref, ...), custom_call_target="tpu_custom_call" | custom-call | bytes 8388608 | tf_op jit(solution)/shard_map/cond/branch_1_fun/pack/pallas_call | solution.py:196
  11.6 5.5 %collective-permute-done.8 = bf16[32,1920]{1,0:T(8,128)(2,1)S(1)} collective-permute-done((bf16[32,1920]{1,0:T(8,128)(2,1)S(1)}, bf16[32,1920]{1,0:T(8,128)(2,1)S(1)}, u32[]{:S(2)}, u32[]{:S(2)}) %collective-permute-start.8) | collective-permute-done | bytes 122912 | tf_op jit(solution)/shard_map/cond/branch_1_fun/ppermute | solution.py:90
  17.2 1.9 %collective-permute-start.14 = (bf16[448,640]{1,0:T(8,128)(2,1)}, bf16[448,640]{1,0:T(8,128)(2,1)S(1)}, u32[]{:S(2)}, u32[]{:S(2)}) collective-permute-start(bf16[448,640]{1,0:T(8,128)(2,1)} %get-tuple-element.135), channel_id=1, source_target_pairs={{0,4},{4,0},{8,12},{12,8},{1,5},{5,1},{9,13},{13,9},{2,6},{6,2},{1... | collective-permute-start | bytes 1720328 | tf_op jit(solution)/shard_map/ppermute | solution.py:90
  21.7 50.2 %conditional.4 = (bf16[4,32,1920]{2,1,0:T(8,128)(2,1)S(1)}, bf16[4,32,1920]{2,1,0:T(8,128)(2,1)}, bf16[4,32,1920]{2,1,0:T(8,128)(2,1)}, bf16[4,32,1920]{2,1,0:T(...) conditional(s32[]{:T(128)} %convert_element_type.38, () %tuple.35, ...), branch_computations={%region_2.0_spmd, %region_3.0_spmd} | conditional | flops 10569646080 | bytes 69796200 | solution.py:527
  23.2 1.5 %collective-permute-start.2 = (bf16[4,32,1920]{2,1,0:T(8,128)(2,1)S(1)}, bf16[4,32,1920]{2,1,0:T(8,128)(2,1)}, u32[]{:S(2)}, u32[]{:S(2)}) collective-permute-start(bf16[4,32,1920]{2,1,0:T(8,128)(2,1)S(1)} %get-tuple-element.207.rest_0_), channel_id=1, source_target_pairs={{0,16},{16,0},{1,17},{17,1},{2,18},{18,2},{3,19},{19,3},{4,20},{20... | collective-permute-start | bytes 1474568 | tf_op jit(solution)/shard_map/cond/branch_1_fun/ppermute | solution.py:90
  24.7 8.5 %collective-permute-done.1.rest_2_ = bf16[4,32,1920]{2,1,0:T(8,128)(2,1)} collective-permute-done((bf16[4,32,1920]{2,1,0:T(8,128)(2,1)S(1)}, bf16[4,32,1920]{2,1,0:T(8,128)(2,1)}, u32[]{:S(2)}, u32[]{:S(2)}) %collective-permute-start.1) | collective-permute-done | bytes 491552 | tf_op jit(solution)/shard_map/cond/branch_1_fun/ppermute | solution.py:90
  34.9 2.4 %collective-permute-done.3.rest_3_ = bf16[4,32,1920]{2,1,0:T(8,128)(2,1)} collective-permute-done((bf16[4,32,1920]{2,1,0:T(8,128)(2,1)}, bf16[4,32,1920]{2,1,0:T(8,128)(2,1)}, u32[]{:S(2)}, u32[]{:S(2)}) %collective-permute-start.3) | collective-permute-done | bytes 491552 | tf_op jit(solution)/shard_map/cond/branch_1_fun/ppermute | solution.py:90
  37.8 31.1 %routed.1 = (bf16[2,448,512]{2,1,0:T(8,128)(2,1)S(1)}, f32[2,448,512]{2,1,0:T(8,128)S(1)}) custom-call(s32[3]{0:T(128)S(1)} %get-tuple-element.69.where_ref, bf16[4,32,1920]{2,1,0:T(8,128)(2,1)S(1)} %get-tuple-element.207.rest_0_, bf16[4,32,1920]{2,1,0:T(8,128)(2,1)} %collective-permute-done.rest_1_, bf16[4,32,1920]{2,1,0:T(8,128)(2,1)} %collective-permute-done.1.rest_2_, ...), custom_call_target="tpu_custom_call" | custom-call | flops 10569646080 | bytes 55050240 | tf_op jit(solution)/shard_map/cond/branch_1_fun/routed/pallas_call | solution.py:319
  69.5 1.7 %collective-permute-done.5 = bf16[4,32,1920]{2,1,0:T(8,128)(2,1)} collective-permute-done((bf16[4,32,1920]{2,1,0:T(8,128)(2,1)}, bf16[4,32,1920]{2,1,0:T(8,128)(2,1)}, u32[]{:S(2)}, u32[]{:S(2)}) %collective-permute-start.5) | collective-permute-done | bytes 491552 | tf_op jit(solution)/shard_map/cond/branch_1_fun/ppermute | solution.py:90
  71.9 1.6 %collective-permute-start.17 = (bf16[224,640]{1,0:T(8,128)(2,1)}, bf16[224,640]{1,0:T(8,128)(2,1)S(1)}, u32[]{:S(2)}, u32[]{:S(2)}) collective-permute-start(bf16[224,640]{1,0:T(8,128)(2,1)} %get-tuple-element.140), channel_id=1, source_target_pairs={{0,0},{1,4},{2,8},{3,12},{4,1},{5,5},{6,9},{7,13},{8,2},{9,6},{10,... | collective-permute-start | bytes 860168 | tf_op jit(solution)/shard_map/ppermute | solution.py:545
  73.5 2.1 %collective-permute-start.21 = (bf16[224,640]{1,0:T(8,128)(2,1)}, bf16[224,640]{1,0:T(8,128)(2,1)S(1)}, u32[]{:S(2)}, u32[]{:S(2)}) collective-permute-start(bf16[224,640]{1,0:T(8,128)(2,1)} %get-tuple-element.150), channel_id=1, source_target_pairs={{0,4},{1,0},{2,12},{3,8},{4,5},{5,1},{6,13},{7,9},{8,6},{9,2},{10,... | collective-permute-start | bytes 860168 | tf_op jit(solution)/shard_map/ppermute | solution.py:545
  77.1 2.6 %collective-permute-start.22 = (bf16[224,640]{1,0:T(8,128)(2,1)}, bf16[224,640]{1,0:T(8,128)(2,1)S(1)}, u32[]{:S(2)}, u32[]{:S(2)}) collective-permute-start(bf16[224,640]{1,0:T(8,128)(2,1)} %get-tuple-element.151), channel_id=1, source_target_pairs={{0,8},{1,12},{2,0},{3,4},{4,9},{5,13},{6,1},{7,5},{8,10},{9,14},{1... | collective-permute-start | bytes 860168 | tf_op jit(solution)/shard_map/ppermute | solution.py:545
  79.8 1.6 %collective-permute-start.23 = (bf16[224,640]{1,0:T(8,128)(2,1)}, bf16[224,640]{1,0:T(8,128)(2,1)S(1)}, u32[]{:S(2)}, u32[]{:S(2)}) collective-permute-start(bf16[224,640]{1,0:T(8,128)(2,1)} %get-tuple-element.152), channel_id=1, source_target_pairs={{0,12},{1,8},{2,4},{3,0},{4,13},{5,9},{6,5},{7,1},{8,14},{9,10},{1... | collective-permute-start | bytes 860168 | tf_op jit(solution)/shard_map/ppermute | solution.py:545
  81.4 6.1 %shared_hidden.3 = (bf16[256,640]{1,0:T(8,128)(2,1)S(1)}, f32[1,512]{1,0:T(1,128)S(1)}) custom-call(s32[3]{0:T(128)} %copy-done.5, bf16[4,32,1920]{2,1,0:T(8,128)(2,1)} %get-tuple-element.130.rest_0_, bf16[4,32,1920]{2,1,0:T(8,128)(2,1)} %get-tuple-element.131.rest_1_, bf16[4,32,1920]{2,1,0:T(8,128)(2,1)} %get-tuple-element.132.rest_2_, ...), custom_call_target="tpu_custom_call" | custom-call | flops 1174405120 | bytes 4194304 | tf_op jit(solution)/shard_map/shared_hidden/pallas_call | solution.py:398
  87.5 20.3 %conditional.5 = (bf16[256,640]{1,0:T(8,128)(2,1)S(1)}, bf16[256,640]{1,0:T(8,128)(2,1)}, bf16[256,640]{1,0:T(8,128)(2,1)}, bf16[256,640]{1,0:T(8,128)(2,1)}, bf...) conditional(s32[]{:T(128)} %convert_element_type.38, () %tuple.34, ...), branch_computations={%region_4.0_spmd, %region_5.0_spmd} | conditional | flops 1175552000 | bytes 20250848 | solution.py:527
  87.5 11.3 %collective-permute-start.10 = (bf16[256,640]{1,0:T(8,128)(2,1)S(1)}, bf16[256,640]{1,0:T(8,128)(2,1)}, u32[]{:S(2)}, u32[]{:S(2)}) collective-permute-start(bf16[256,640]{1,0:T(8,128)(2,1)S(1)} %get-tuple-element.225.rest_9_), channel_id=1, source_target_pairs={{0,2},{1,3},{2,0},{3,1},{4,6},{5,7},{6,4},{7,5},{8,10},{9,11},{10,... | collective-permute-start | bytes 983048 | tf_op jit(solution)/shard_map/cond/branch_1_fun/ppermute | solution.py:90
  98.8 5.1 %shared_hidden.2 = (bf16[256,640]{1,0:T(8,128)(2,1)S(1)}, f32[1,512]{1,0:T(1,128)S(1)}) custom-call(s32[3]{0:T(128)S(1)} %get-tuple-element.80.where_ref, bf16[4,32,1920]{2,1,0:T(8,128)(2,1)S(1)} %get-tuple-element.81.rest_0_, bf16[4,32,1920]{2,1,0:T(8,128)(2,1)} %get-tuple-element.82.rest_1_, bf16[4,32,1920]{2,1,0:T(8,128)(2,1)} %get-tuple-element.83.rest_2_, ...), custom_call_target="tpu_custom_call" | custom-call | flops 1174405120 | bytes 4194304 | tf_op jit(solution)/shard_map/cond/branch_1_fun/shared_hidden/pallas_call | solution.py:398
  104.6 2.5 %collective-permute-done.13 = bf16[2,448,512]{2,1,0:T(8,128)(2,1)S(1)} collective-permute-done((bf16[2,448,512]{2,1,0:T(8,128)(2,1)S(1)}, bf16[2,448,512]{2,1,0:T(8,128)(2,1)S(1)}, u32[]{:S(2)}, u32[]{:S(2)}) %collective-permute-start.13) | collective-permute-done | bytes 917536 | tf_op jit(solution)/shard_map/cond/branch_1_fun/ppermute | solution.py:90
  107.8 2.3 %collective-permute-start.19 = (bf16[256,640]{1,0:T(8,128)(2,1)S(1)}, bf16[256,640]{1,0:T(8,128)(2,1)S(1)}, u32[]{:S(2)}, u32[]{:S(2)}) collective-permute-start(bf16[256,640]{1,0:T(8,128)(2,1)S(1)} %get-tuple-element.148.rest_0_), channel_id=1, source_target_pairs={{0,2},{1,3},{2,0},{3,1},{4,6},{5,7},{6,4},{7,5},{8,10},{9,11},{10,... | collective-permute-start | bytes 983048 | tf_op jit(solution)/shard_map/ppermute | solution.py:90
  110.1 3.2 %down_far.1 = bf16[448,512]{1,0:T(8,128)(2,1)S(1)} custom-call(s32[3]{0:T(128)S(1)} %copy-done.6, f32[1,512]{1,0:T(1,128)S(1)} %get-tuple-element.154.scale_ref, bf16[256,640]{1,0:T(8,128)(2,1)S(1)} %get-tuple-element.155.rest_0_, bf16[256,640]{1,0:T(8,128)(2,1)} %get-tuple-element.156.rest_1_, bf16[256,640]{1,0:T(8,128)(2,1)} %get-tuple-element.157.rest_2_, ...), custom_call_target="tpu_custom_call" | custom-call | flops 704643072 | bytes 4194304 | tf_op jit(solution)/shard_map/down_far/pallas_call | solution.py:484
  113.3 1.6 %collective-permute-start.24 = (bf16[448,512]{1,0:T(8,128)(2,1)S(1)}, bf16[448,512]{1,0:T(8,128)(2,1)S(1)}, u32[]{:S(2)}, u32[]{:S(2)}) collective-permute-start(bf16[448,512]{1,0:T(8,128)(2,1)S(1)} %down_far.1), channel_id=1, source_target_pairs={{0,16},{16,0},{1,17},{17,1},{2,18},{18,2},{3,19},{19,3},{4,20},{20... | collective-permute-start | bytes 1376264 | tf_op jit(solution)/shard_map/ppermute | solution.py:90
  115.0 3.6 %collective-permute-done.19.rest_2_ = bf16[256,640]{1,0:T(8,128)(2,1)S(1)} collective-permute-done((bf16[256,640]{1,0:T(8,128)(2,1)S(1)}, bf16[256,640]{1,0:T(8,128)(2,1)S(1)}, u32[]{:S(2)}, u32[]{:S(2)}) %collective-permute-start.19) | collective-permute-done | bytes 327712 | tf_op jit(solution)/shard_map/ppermute | solution.py:90
  118.6 1.6 %collective-permute-done.20.rest_3_ = bf16[256,640]{1,0:T(8,128)(2,1)S(1)} collective-permute-done((bf16[256,640]{1,0:T(8,128)(2,1)S(1)}, bf16[256,640]{1,0:T(8,128)(2,1)S(1)}, u32[]{:S(2)}, u32[]{:S(2)}) %collective-permute-start.20) | collective-permute-done | bytes 327712 | tf_op jit(solution)/shard_map/ppermute | solution.py:90
  120.2 2.1 %down_near.1 = f32[448,512]{1,0:T(8,128)S(1)} custom-call(s32[3]{0:T(128)S(1)} %copy-done.6, f32[1,512]{1,0:T(1,128)S(1)} %get-tuple-element.147.scale_ref, bf16[256,640]{1,0:T(8,128)(2,1)S(1)} %get-tuple-element.148.rest_0_, bf16[256,640]{1,0:T(8,128)(2,1)S(1)} %collective-permute-done.18.rest_1_, bf16[256,640]{1,0:T(8,128)(2,1)S(1)} %collective-permute-done.19.rest_2_, ...), custom_call_target="tpu_custom_call" | custom-call | flops 704643072 | bytes 4194304 | tf_op jit(solution)/shard_map/down_near/pallas_call | solution.py:484
  122.3 3.4 %collective-permute-done.24 = bf16[448,512]{1,0:T(8,128)(2,1)S(1)} collective-permute-done((bf16[448,512]{1,0:T(8,128)(2,1)S(1)}, bf16[448,512]{1,0:T(8,128)(2,1)S(1)}, u32[]{:S(2)}, u32[]{:S(2)}) %collective-permute-start.24) | collective-permute-done | bytes 458784 | tf_op jit(solution)/shard_map/ppermute | solution.py:90
  125.7 2.2 %collective-permute-done.25 = bf16[448,512]{1,0:T(8,128)(2,1)S(1)} collective-permute-done((bf16[448,512]{1,0:T(8,128)(2,1)S(1)}, bf16[448,512]{1,0:T(8,128)(2,1)S(1)}, u32[]{:S(2)}, u32[]{:S(2)}) %collective-permute-start.25) | collective-permute-done | bytes 458784 | tf_op jit(solution)/shard_map/ppermute | solution.py:90
  128.2 3.5 %collective-permute-start.26 = (bf16[448,128]{1,0:T(8,128)(2,1)S(1)}, bf16[448,128]{1,0:T(8,128)(2,1)S(1)}, u32[]{:S(2)}, u32[]{:S(2)}) collective-permute-start(bf16[448,128]{1,0:T(8,128)(2,1)S(1)} %get-tuple-element.176), channel_id=1, source_target_pairs={{0,4},{4,0},{8,12},{12,8},{1,5},{5,1},{9,13},{13,9},{2,6},{6,2},{1... | collective-permute-start | bytes 344072 | tf_op jit(solution)/shard_map/ppermute | solution.py:90
  135.3 7.7 %collective-permute-done.27 = bf16[448,128]{1,0:T(8,128)(2,1)S(1)} collective-permute-done((bf16[448,128]{1,0:T(8,128)(2,1)S(1)}, bf16[448,128]{1,0:T(8,128)(2,1)S(1)}, u32[]{:S(2)}, u32[]{:S(2)}) %collective-permute-start.27) | collective-permute-done | bytes 114720 | tf_op jit(solution)/shard_map/ppermute | solution.py:90
  (60 shorter events, 15.3 us)
Async XLA Ops:
  0.1 21.6 %copy-start.5 = (s32[3]{0:T(128)}, s32[3]{0:T(128)S(1)}, u32[]{:S(2)}) copy-start(s32[3]{0:T(128)S(1)} %pad_add_fusion.where_ref) | copy-start | bytes 40
  1.7 9.9 %collective-permute-start.7 = (bf16[32,1920]{1,0:T(8,128)(2,1)S(1)}, bf16[32,1920]{1,0:T(8,128)(2,1)S(1)}, u32[]{:S(2)}, u32[]{:S(2)}) collective-permute-start(bf16[32,1920]{1,0:T(8,128)(2,1)S(1)} %get-tuple-element.51), channel_id=1, source_target_pairs={{0,4},{4,0},{8,12},{12,8},{1,5},{5,1},{9,13},{13,9},{2,6},{6,2},{1... | collective-permute-start | bytes 368648 | tf_op jit(solution)/shard_map/cond/branch_1_fun/ppermute | solution.py:90
  4.8 12.3 %collective-permute-start.8 = (bf16[32,1920]{1,0:T(8,128)(2,1)S(1)}, bf16[32,1920]{1,0:T(8,128)(2,1)S(1)}, u32[]{:S(2)}, u32[]{:S(2)}) collective-permute-start(bf16[32,1920]{1,0:T(8,128)(2,1)S(1)} %get-tuple-element.51), channel_id=1, source_target_pairs={{0,8},{4,12},{8,0},{12,4},{1,9},{5,13},{9,1},{13,5},{2,10},{6,14},... | collective-permute-start | bytes 368648 | tf_op jit(solution)/shard_map/cond/branch_1_fun/ppermute | solution.py:90
  7.4 9.7 %collective-permute-start.9 = (bf16[32,1920]{1,0:T(8,128)(2,1)S(1)}, bf16[32,1920]{1,0:T(8,128)(2,1)S(1)}, u32[]{:S(2)}, u32[]{:S(2)}) collective-permute-start(bf16[32,1920]{1,0:T(8,128)(2,1)S(1)} %get-tuple-element.51), channel_id=1, source_target_pairs={{0,12},{4,8},{8,4},{12,0},{1,13},{5,9},{9,5},{13,1},{2,14},{6,10},... | collective-permute-start | bytes 368648 | tf_op jit(solution)/shard_map/cond/branch_1_fun/ppermute | solution.py:90
  17.2 59.1 %collective-permute-start.14 = (bf16[448,640]{1,0:T(8,128)(2,1)}, bf16[448,640]{1,0:T(8,128)(2,1)S(1)}, u32[]{:S(2)}, u32[]{:S(2)}) collective-permute-start(bf16[448,640]{1,0:T(8,128)(2,1)} %get-tuple-element.135), channel_id=1, source_target_pairs={{0,4},{4,0},{8,12},{12,8},{1,5},{5,1},{9,13},{13,9},{2,6},{6,2},{1... | collective-permute-start | bytes 1720328 | tf_op jit(solution)/shard_map/ppermute | solution.py:90
  19.1 60.6 %collective-permute-start.15 = (bf16[448,640]{1,0:T(8,128)(2,1)}, bf16[448,640]{1,0:T(8,128)(2,1)S(1)}, u32[]{:S(2)}, u32[]{:S(2)}) collective-permute-start(bf16[448,640]{1,0:T(8,128)(2,1)} %get-tuple-element.136), channel_id=1, source_target_pairs={{0,8},{4,12},{8,0},{12,4},{1,9},{5,13},{9,1},{13,5},{2,10},{6,14},... | collective-permute-start | bytes 1720328 | tf_op jit(solution)/shard_map/ppermute | solution.py:90
  20.2 61.1 %collective-permute-start.16 = (bf16[448,640]{1,0:T(8,128)(2,1)}, bf16[448,640]{1,0:T(8,128)(2,1)}, u32[]{:S(2)}, u32[]{:S(2)}) collective-permute-start(bf16[448,640]{1,0:T(8,128)(2,1)} %get-tuple-element.137), channel_id=1, source_target_pairs={{0,12},{4,8},{8,4},{12,0},{1,13},{5,9},{9,5},{13,1},{2,14},{6,10},... | collective-permute-start | bytes 1720328 | tf_op jit(solution)/shard_map/ppermute | solution.py:90
  21.7 11.5 %collective-permute-start.1 = (bf16[4,32,1920]{2,1,0:T(8,128)(2,1)S(1)}, bf16[4,32,1920]{2,1,0:T(8,128)(2,1)}, u32[]{:S(2)}, u32[]{:S(2)}) collective-permute-start(bf16[4,32,1920]{2,1,0:T(8,128)(2,1)S(1)} %get-tuple-element.207.rest_0_), channel_id=1, source_target_pairs={{0,2},{1,3},{2,0},{3,1},{4,6},{5,7},{6,4},{7,5},{8,10},{9,11},{10,... | collective-permute-start | bytes 1474568 | tf_op jit(solution)/shard_map/cond/branch_1_fun/ppermute | solution.py:90
  23.2 11.2 %collective-permute-start.2 = (bf16[4,32,1920]{2,1,0:T(8,128)(2,1)S(1)}, bf16[4,32,1920]{2,1,0:T(8,128)(2,1)}, u32[]{:S(2)}, u32[]{:S(2)}) collective-permute-start(bf16[4,32,1920]{2,1,0:T(8,128)(2,1)S(1)} %get-tuple-element.207.rest_0_), channel_id=1, source_target_pairs={{0,16},{16,0},{1,17},{17,1},{2,18},{18,2},{3,19},{19,3},{4,20},{20... | collective-permute-start | bytes 1474568 | tf_op jit(solution)/shard_map/cond/branch_1_fun/ppermute | solution.py:90
  34.4 2.9 %collective-permute-start.3 = (bf16[4,32,1920]{2,1,0:T(8,128)(2,1)}, bf16[4,32,1920]{2,1,0:T(8,128)(2,1)}, u32[]{:S(2)}, u32[]{:S(2)}) collective-permute-start(bf16[4,32,1920]{2,1,0:T(8,128)(2,1)} %collective-permute-done.1.rest_2_), channel_id=1, source_target_pairs={{0,1},{1,0},{2,3},{3,2},{4,5},{5,4},{6,7},{7,6},{8,9},{9,8},{10,11... | collective-permute-start | bytes 1474568 | tf_op jit(solution)/shard_map/cond/branch_1_fun/ppermute | solution.py:90
  34.4 3.4 %collective-permute-start = (bf16[4,32,1920]{2,1,0:T(8,128)(2,1)S(1)}, bf16[4,32,1920]{2,1,0:T(8,128)(2,1)}, u32[]{:S(2)}, u32[]{:S(2)}) collective-permute-start(bf16[4,32,1920]{2,1,0:T(8,128)(2,1)S(1)} %get-tuple-element.207.rest_0_), channel_id=1, source_target_pairs={{0,1},{1,0},{2,3},{3,2},{4,5},{5,4},{6,7},{7,6},{8,9},{9,8},{10,11... | collective-permute-start | bytes 1474568 | tf_op jit(solution)/shard_map/cond/branch_1_fun/ppermute | solution.py:90
  37.3 31.6 %collective-permute-start.4 = (bf16[4,32,1920]{2,1,0:T(8,128)(2,1)}, bf16[4,32,1920]{2,1,0:T(8,128)(2,1)}, u32[]{:S(2)}, u32[]{:S(2)}) collective-permute-start(bf16[4,32,1920]{2,1,0:T(8,128)(2,1)} %collective-permute-done.2), channel_id=1, source_target_pairs={{0,2},{1,3},{2,0},{3,1},{4,6},{5,7},{6,4},{7,5},{8,10},{9,11},{10,... | collective-permute-start | bytes 1474568 | tf_op jit(solution)/shard_map/cond/branch_1_fun/ppermute | solution.py:90
  68.9 2.3 %collective-permute-start.5 = (bf16[4,32,1920]{2,1,0:T(8,128)(2,1)}, bf16[4,32,1920]{2,1,0:T(8,128)(2,1)}, u32[]{:S(2)}, u32[]{:S(2)}) collective-permute-start(bf16[4,32,1920]{2,1,0:T(8,128)(2,1)} %collective-permute-done.2), channel_id=1, source_target_pairs={{0,1},{1,0},{2,3},{3,2},{4,5},{5,4},{6,7},{7,6},{8,9},{9,8},{10,11... | collective-permute-start | bytes 1474568 | tf_op jit(solution)/shard_map/cond/branch_1_fun/ppermute | solution.py:90
  69.0 2.9 %collective-permute-start.6 = (bf16[4,32,1920]{2,1,0:T(8,128)(2,1)}, bf16[4,32,1920]{2,1,0:T(8,128)(2,1)}, u32[]{:S(2)}, u32[]{:S(2)}) collective-permute-start(bf16[4,32,1920]{2,1,0:T(8,128)(2,1)} %collective-permute-done.4), channel_id=1, source_target_pairs={{0,1},{1,0},{2,3},{3,2},{4,5},{5,4},{6,7},{7,6},{8,9},{9,8},{10,11... | collective-permute-start | bytes 1474568 | tf_op jit(solution)/shard_map/cond/branch_1_fun/ppermute | solution.py:90
  71.9 15.6 %collective-permute-start.17 = (bf16[224,640]{1,0:T(8,128)(2,1)}, bf16[224,640]{1,0:T(8,128)(2,1)S(1)}, u32[]{:S(2)}, u32[]{:S(2)}) collective-permute-start(bf16[224,640]{1,0:T(8,128)(2,1)} %get-tuple-element.140), channel_id=1, source_target_pairs={{0,0},{1,4},{2,8},{3,12},{4,1},{5,5},{6,9},{7,13},{8,2},{9,6},{10,... | collective-permute-start | bytes 860168 | tf_op jit(solution)/shard_map/ppermute | solution.py:545
  73.5 36.6 %collective-permute-start.21 = (bf16[224,640]{1,0:T(8,128)(2,1)}, bf16[224,640]{1,0:T(8,128)(2,1)S(1)}, u32[]{:S(2)}, u32[]{:S(2)}) collective-permute-start(bf16[224,640]{1,0:T(8,128)(2,1)} %get-tuple-element.150), channel_id=1, source_target_pairs={{0,4},{1,0},{2,12},{3,8},{4,5},{5,1},{6,13},{7,9},{8,6},{9,2},{10,... | collective-permute-start | bytes 860168 | tf_op jit(solution)/shard_map/ppermute | solution.py:545
  77.1 33.0 %collective-permute-start.22 = (bf16[224,640]{1,0:T(8,128)(2,1)}, bf16[224,640]{1,0:T(8,128)(2,1)S(1)}, u32[]{:S(2)}, u32[]{:S(2)}) collective-permute-start(bf16[224,640]{1,0:T(8,128)(2,1)} %get-tuple-element.151), channel_id=1, source_target_pairs={{0,8},{1,12},{2,0},{3,4},{4,9},{5,13},{6,1},{7,5},{8,10},{9,14},{1... | collective-permute-start | bytes 860168 | tf_op jit(solution)/shard_map/ppermute | solution.py:545
  79.8 30.3 %collective-permute-start.23 = (bf16[224,640]{1,0:T(8,128)(2,1)}, bf16[224,640]{1,0:T(8,128)(2,1)S(1)}, u32[]{:S(2)}, u32[]{:S(2)}) collective-permute-start(bf16[224,640]{1,0:T(8,128)(2,1)} %get-tuple-element.152), channel_id=1, source_target_pairs={{0,12},{1,8},{2,4},{3,0},{4,13},{5,9},{6,5},{7,1},{8,14},{9,10},{1... | collective-permute-start | bytes 860168 | tf_op jit(solution)/shard_map/ppermute | solution.py:545
  81.4 6.1 %copy-start.4 = (bf16[448,640]{1,0:T(8,128)(2,1)S(1)}, bf16[448,640]{1,0:T(8,128)(2,1)}, u32[]{:S(2)}) copy-start(bf16[448,640]{1,0:T(8,128)(2,1)} %copy-done.3) | copy-start | bytes 1720324
  81.4 6.1 %copy-start.6 = (s32[3]{0:T(128)S(1)}, s32[3]{0:T(128)}, u32[]{:S(2)}) copy-start(s32[3]{0:T(128)} %copy-done.5) | copy-start | bytes 40
  87.5 16.4 %collective-permute-start.10 = (bf16[256,640]{1,0:T(8,128)(2,1)S(1)}, bf16[256,640]{1,0:T(8,128)(2,1)}, u32[]{:S(2)}, u32[]{:S(2)}) collective-permute-start(bf16[256,640]{1,0:T(8,128)(2,1)S(1)} %get-tuple-element.225.rest_9_), channel_id=1, source_target_pairs={{0,2},{1,3},{2,0},{3,1},{4,6},{5,7},{6,4},{7,5},{8,10},{9,11},{10,... | collective-permute-start | bytes 983048 | tf_op jit(solution)/shard_map/cond/branch_1_fun/ppermute | solution.py:90
  98.8 5.2 %collective-permute-start.11 = (bf16[256,640]{1,0:T(8,128)(2,1)S(1)}, bf16[256,640]{1,0:T(8,128)(2,1)}, u32[]{:S(2)}, u32[]{:S(2)}) collective-permute-start(bf16[256,640]{1,0:T(8,128)(2,1)S(1)} %get-tuple-element.225.rest_9_), channel_id=1, source_target_pairs={{0,1},{1,0},{2,3},{3,2},{4,5},{5,4},{6,7},{7,6},{8,9},{9,8},{10,11... | collective-permute-start | bytes 983048 | tf_op jit(solution)/shard_map/cond/branch_1_fun/ppermute | solution.py:90
  103.9 3.1 %collective-permute-start.13 = (bf16[2,448,512]{2,1,0:T(8,128)(2,1)S(1)}, bf16[2,448,512]{2,1,0:T(8,128)(2,1)S(1)}, u32[]{:S(2)}, u32[]{:S(2)}) collective-permute-start(bf16[2,448,512]{2,1,0:T(8,128)(2,1)S(1)} %get-tuple-element.97), channel_id=1, source_target_pairs={{0,1},{1,0},{2,3},{3,2},{4,5},{5,4},{6,7},{7,6},{8,9},{9,8},{10,11... | collective-permute-start | bytes 2752520 | tf_op jit(solution)/shard_map/cond/branch_1_fun/ppermute | solution.py:90
  104.5 3.3 %collective-permute-start.12 = (bf16[256,640]{1,0:T(8,128)(2,1)}, bf16[256,640]{1,0:T(8,128)(2,1)}, u32[]{:S(2)}, u32[]{:S(2)}) collective-permute-start(bf16[256,640]{1,0:T(8,128)(2,1)} %collective-permute-done.10), channel_id=1, source_target_pairs={{0,1},{1,0},{2,3},{3,2},{4,5},{5,4},{6,7},{7,6},{8,9},{9,8},{10,11... | collective-permute-start | bytes 983048 | tf_op jit(solution)/shard_map/cond/branch_1_fun/ppermute | solution.py:90
  107.8 10.8 %collective-permute-start.19 = (bf16[256,640]{1,0:T(8,128)(2,1)S(1)}, bf16[256,640]{1,0:T(8,128)(2,1)S(1)}, u32[]{:S(2)}, u32[]{:S(2)}) collective-permute-start(bf16[256,640]{1,0:T(8,128)(2,1)S(1)} %get-tuple-element.148.rest_0_), channel_id=1, source_target_pairs={{0,2},{1,3},{2,0},{3,1},{4,6},{5,7},{6,4},{7,5},{8,10},{9,11},{10,... | collective-permute-start | bytes 983048 | tf_op jit(solution)/shard_map/ppermute | solution.py:90
  113.3 12.3 %collective-permute-start.24 = (bf16[448,512]{1,0:T(8,128)(2,1)S(1)}, bf16[448,512]{1,0:T(8,128)(2,1)S(1)}, u32[]{:S(2)}, u32[]{:S(2)}) collective-permute-start(bf16[448,512]{1,0:T(8,128)(2,1)S(1)} %down_far.1), channel_id=1, source_target_pairs={{0,16},{16,0},{1,17},{17,1},{2,18},{18,2},{3,19},{19,3},{4,20},{20... | collective-permute-start | bytes 1376264 | tf_op jit(solution)/shard_map/ppermute | solution.py:90
  114.9 13.0 %collective-permute-start.25 = (bf16[448,512]{1,0:T(8,128)(2,1)S(1)}, bf16[448,512]{1,0:T(8,128)(2,1)S(1)}, u32[]{:S(2)}, u32[]{:S(2)}) collective-permute-start(bf16[448,512]{1,0:T(8,128)(2,1)S(1)} %get-tuple-element.159), channel_id=1, source_target_pairs={{0,2},{1,3},{2,0},{3,1},{4,6},{5,7},{6,4},{7,5},{8,10},{9,11},{10,... | collective-permute-start | bytes 1376264 | tf_op jit(solution)/shard_map/ppermute | solution.py:90
  115.0 3.6 %collective-permute-start.18 = (bf16[256,640]{1,0:T(8,128)(2,1)S(1)}, bf16[256,640]{1,0:T(8,128)(2,1)S(1)}, u32[]{:S(2)}, u32[]{:S(2)}) collective-permute-start(bf16[256,640]{1,0:T(8,128)(2,1)S(1)} %get-tuple-element.148.rest_0_), channel_id=1, source_target_pairs={{0,1},{1,0},{2,3},{3,2},{4,5},{5,4},{6,7},{7,6},{8,9},{9,8},{10,11... | collective-permute-start | bytes 983048 | tf_op jit(solution)/shard_map/ppermute | solution.py:90
  118.6 1.6 %collective-permute-start.20 = (bf16[256,640]{1,0:T(8,128)(2,1)S(1)}, bf16[256,640]{1,0:T(8,128)(2,1)S(1)}, u32[]{:S(2)}, u32[]{:S(2)}) collective-permute-start(bf16[256,640]{1,0:T(8,128)(2,1)S(1)} %collective-permute-done.19.rest_2_), channel_id=1, source_target_pairs={{0,1},{1,0},{2,3},{3,2},{4,5},{5,4},{6,7},{7,6},{8,9},{9,8},{10,11... | collective-permute-start | bytes 983048 | tf_op jit(solution)/shard_map/ppermute | solution.py:90
  128.2 7.1 %collective-permute-start.26 = (bf16[448,128]{1,0:T(8,128)(2,1)S(1)}, bf16[448,128]{1,0:T(8,128)(2,1)S(1)}, u32[]{:S(2)}, u32[]{:S(2)}) collective-permute-start(bf16[448,128]{1,0:T(8,128)(2,1)S(1)} %get-tuple-element.176), channel_id=1, source_target_pairs={{0,4},{4,0},{8,12},{12,8},{1,5},{5,1},{9,13},{13,9},{2,6},{6,2},{1... | collective-permute-start | bytes 344072 | tf_op jit(solution)/shard_map/ppermute | solution.py:90
  131.7 11.3 %collective-permute-start.27 = (bf16[448,128]{1,0:T(8,128)(2,1)S(1)}, bf16[448,128]{1,0:T(8,128)(2,1)S(1)}, u32[]{:S(2)}, u32[]{:S(2)}) collective-permute-start(bf16[448,128]{1,0:T(8,128)(2,1)S(1)} %get-tuple-element.178), channel_id=1, source_target_pairs={{0,8},{4,12},{8,0},{12,4},{1,9},{5,13},{9,1},{13,5},{2,10},{6,14},... | collective-permute-start | bytes 344072 | tf_op jit(solution)/shard_map/ppermute | solution.py:90
  132.9 10.1 %collective-permute-start.28 = (bf16[448,128]{1,0:T(8,128)(2,1)S(1)}, bf16[448,128]{1,0:T(8,128)(2,1)S(1)}, u32[]{:S(2)}, u32[]{:S(2)}) collective-permute-start(bf16[448,128]{1,0:T(8,128)(2,1)S(1)} %get-tuple-element.177), channel_id=1, source_target_pairs={{0,12},{4,8},{8,4},{12,0},{1,13},{5,9},{9,5},{13,1},{2,14},{6,10},... | collective-permute-start | bytes 344072 | tf_op jit(solution)/shard_map/ppermute | solution.py:90
  (4 other events, 14.7 us)

commit v5 on v4

--- a/solution.py
+++ b/solution.py
@@ -570,12 +570,12 @@
         sums = kept[0] + got[0], (kept[1] + got[1]).astype(BF)
         return [h, over_core, over_x, swap(over_x, "tensor", 1)], near, sums
 
-    far_hidden, first = lax.optimization_barrier((far_hidden, cross(packed[n_dp], 0)))
+    far_hidden, first = lax.optimization_barrier((far_hidden, cross(packed[2 * n_dp - 1], n_dp - 1)))
     gathered, (near_hidden, near_scale), (routed, routed_far) = apart(
         gather_step, far_hidden, tok_own, gu, give, keep
     )
     near_x, near_core = swap(near_hidden, "tensor", 2), swap(near_hidden, "tensor", 1)
-    down = [first] + [cross(packed[n_dp + r], r) for r in range(1, n_dp)]
+    down = [cross(packed[n_dp + r], r) for r in range(n_dp - 1)] + [first]
     far = shared_down(where, down, gathered, far_scale, width, True, None)
     gathered = [near_hidden, near_core, near_x, swap(near_x, "tensor", 1)]
     near = shared_down(where, down, gathered, near_scale, width, False, routed)

time: 144 us -> 141 us (0.979)
  starting transfers between devices: 44.6 us -> 34.2 us
  waiting for transfers between devices: 42 us -> 49.6 us
    ppermute x25, starting transfers between devices: 36.7 us -> 26.5 us  [swap(): return lax.ppermute(x, axis, [(i, i ^ bit) for i in range(n)])]
    ppermute x25, waiting for transfers between devices: 42 us -> 49.6 us  [swap(): return lax.ppermute(x, axis, [(i, i ^ bit) for i in range(n)])]
  transfers between devices with their start and end apart: 29 -> 29, of which waited for: 13 -> 14; matrix products, arithmetic and copies ran while one was open for 1% -> 1% of each run, Pallas kernels for 36% -> 37%
where the time goes in v5:
time: 141 us
  Pallas kernels  53.4 us (38%)
  waiting for transfers between devices  49.6 us (35%)
  starting transfers between devices  34.2 us (24%)
  other arithmetic  1.75 us (1%)
  local copies, waits for them, and re-layouts  1.66 us (1%)
    ppermute x25, waiting for transfers between devices, swap(): return lax.ppermute(x, axis, [(i, i ^ bit) for i in range(n)])  49.6 us
    pallas_call x1, Pallas kernels, routed_experts(): pl.pallas_call(kernel, grid=(e_dev,), out_shape=[jax.ShapeDtypeStruct((2,...  31.1 us
    ppermute x25, starting transfers between devices, swap(): return lax.ppermute(x, axis, [(i, i ^ bit) for i in range(n)])  26.5 us
    pallas_call x2, Pallas kernels, shared_hidden(): pl.pallas_call(kernel, out_shape=[jax.ShapeDtypeStruct((half, 2 * width),...  11.2 us
    ppermute x4, starting transfers between devices, cross(): return lax.ppermute(piece, ('dp', 'tensor'), route)  7.79 us
    pallas_call x2, Pallas kernels, shared_down(): pl.pallas_call(kernel, out_shape=jax.ShapeDtypeStruct((2 * half, n_tok),...  5.32 us
    pallas_call x1, Pallas kernels, pack(): pl.pallas_call(kernel, out_shape=[jax.ShapeDtypeStruct((d_part, 2 * width...  4.19 us
  transfers between devices with their start and end apart: 29, of which 14 were waited for; matrix products, arithmetic and copies ran while one was open for 1% of the time, Pallas kernels for 37%

profile of v5, /device:TPU:0, one launch (start us, length us, event | category | flops | bytes accessed | tf_op | source)
XLA Modules:
  0.0 140.9 jit_solution(14080881729162115568)
XLA Ops:
  0.1 1.6 %token_rows.1 = bf16[32,1920]{1,0:T(8,128)(2,1)S(1)} custom-call(s32[3]{0:T(128)S(1)} %pad_add_fusion.where_ref, bf16[128,1792]{1,0:T(8,128)(2,1)} %tok_ref.1, s32[8,128]{1,0:T(8,128)} %bitcast.19, f32[8,128]{1,0:T(8,128)} %bitcast.20), custom_call_target="tpu_custom_call" | custom-call | tf_op jit(solution)/shard_map/token_rows/pallas_call | solution.py:129
  1.7 15.5 %conditional.3 = (bf16[4,32,1920]{2,1,0:T(8,128)(2,1)S(1)}, bf16[448,640]{1,0:T(8,128)(2,1)}, bf16[448,640]{1,0:T(8,128)(2,1)}, bf16[448,640]{1,0:T(8,128)(2,1)}...) conditional(s32[]{:T(128)} %convert_element_type.38, () %tuple.36, ...), branch_computations={%region_0.0_spmd, %region_1.0_spmd} | conditional | flops 737280 | bytes 10846400 | solution.py:527
  1.7 3.1 %collective-permute-start.7 = (bf16[32,1920]{1,0:T(8,128)(2,1)S(1)}, bf16[32,1920]{1,0:T(8,128)(2,1)S(1)}, u32[]{:S(2)}, u32[]{:S(2)}) collective-permute-start(bf16[32,1920]{1,0:T(8,128)(2,1)S(1)} %get-tuple-element.51), channel_id=1, source_target_pairs={{0,4},{4,0},{8,12},{12,8},{1,5},{5,1},{9,13},{13,9},{2,6},{6,2},{1... | collective-permute-start | bytes 368648 | tf_op jit(solution)/shard_map/cond/branch_1_fun/ppermute | solution.py:90
  4.8 2.6 %collective-permute-start.8 = (bf16[32,1920]{1,0:T(8,128)(2,1)S(1)}, bf16[32,1920]{1,0:T(8,128)(2,1)S(1)}, u32[]{:S(2)}, u32[]{:S(2)}) collective-permute-start(bf16[32,1920]{1,0:T(8,128)(2,1)S(1)} %get-tuple-element.51), channel_id=1, source_target_pairs={{0,8},{4,12},{8,0},{12,4},{1,9},{5,13},{9,1},{13,5},{2,10},{6,14},... | collective-permute-start | bytes 368648 | tf_op jit(solution)/shard_map/cond/branch_1_fun/ppermute | solution.py:90
  7.4 4.2 %pack.1 = (bf16[448,640]{1,0:T(8,128)(2,1)}, bf16[448,640]{1,0:T(8,128)(2,1)}, bf16[448,640]{1,0:T(8,128)(2,1)}, bf16[448,640]{1,0:T(8,128)(2,1)}, bf16[224,640]...) custom-call(s32[3]{0:T(128)S(1)} %get-tuple-element.52.where_ref, ...), custom_call_target="tpu_custom_call" | custom-call | bytes 8388608 | tf_op jit(solution)/shard_map/cond/branch_1_fun/pack/pallas_call | solution.py:196
  11.6 5.5 %collective-permute-done.8 = bf16[32,1920]{1,0:T(8,128)(2,1)S(1)} collective-permute-done((bf16[32,1920]{1,0:T(8,128)(2,1)S(1)}, bf16[32,1920]{1,0:T(8,128)(2,1)S(1)}, u32[]{:S(2)}, u32[]{:S(2)}) %collective-permute-start.8) | collective-permute-done | bytes 122912 | tf_op jit(solution)/shard_map/cond/branch_1_fun/ppermute | solution.py:90
  17.2 1.9 %collective-permute-start.14 = (bf16[448,640]{1,0:T(8,128)(2,1)}, bf16[448,640]{1,0:T(8,128)(2,1)S(1)}, u32[]{:S(2)}, u32[]{:S(2)}) collective-permute-start(bf16[448,640]{1,0:T(8,128)(2,1)} %get-tuple-element.135), channel_id=1, source_target_pairs={{0,4},{4,0},{8,12},{12,8},{1,5},{5,1},{9,13},{13,9},{2,6},{6,2},{1... | collective-permute-start | bytes 1720328 | tf_op jit(solution)/shard_map/ppermute | solution.py:90
  21.7 50.2 %conditional.4 = (bf16[4,32,1920]{2,1,0:T(8,128)(2,1)S(1)}, bf16[4,32,1920]{2,1,0:T(8,128)(2,1)}, bf16[4,32,1920]{2,1,0:T(8,128)(2,1)}, bf16[4,32,1920]{2,1,0:T(...) conditional(s32[]{:T(128)} %convert_element_type.38, () %tuple.35, ...), branch_computations={%region_2.0_spmd, %region_3.0_spmd} | conditional | flops 10569646080 | bytes 69796200 | solution.py:527
  24.7 8.5 %collective-permute-done.1.rest_2_ = bf16[4,32,1920]{2,1,0:T(8,128)(2,1)} collective-permute-done((bf16[4,32,1920]{2,1,0:T(8,128)(2,1)S(1)}, bf16[4,32,1920]{2,1,0:T(8,128)(2,1)}, u32[]{:S(2)}, u32[]{:S(2)}) %collective-permute-start.1) | collective-permute-done | bytes 491552 | tf_op jit(solution)/shard_map/cond/branch_1_fun/ppermute | solution.py:90
  34.9 2.4 %collective-permute-done.3.rest_3_ = bf16[4,32,1920]{2,1,0:T(8,128)(2,1)} collective-permute-done((bf16[4,32,1920]{2,1,0:T(8,128)(2,1)}, bf16[4,32,1920]{2,1,0:T(8,128)(2,1)}, u32[]{:S(2)}, u32[]{:S(2)}) %collective-permute-start.3) | collective-permute-done | bytes 491552 | tf_op jit(solution)/shard_map/cond/branch_1_fun/ppermute | solution.py:90
  37.8 31.1 %routed.1 = (bf16[2,448,512]{2,1,0:T(8,128)(2,1)S(1)}, f32[2,448,512]{2,1,0:T(8,128)S(1)}) custom-call(s32[3]{0:T(128)S(1)} %get-tuple-element.69.where_ref, bf16[4,32,1920]{2,1,0:T(8,128)(2,1)S(1)} %get-tuple-element.207.rest_0_, bf16[4,32,1920]{2,1,0:T(8,128)(2,1)} %collective-permute-done.rest_1_, bf16[4,32,1920]{2,1,0:T(8,128)(2,1)} %collective-permute-done.1.rest_2_, ...), custom_call_target="tpu_custom_call" | custom-call | flops 10569646080 | bytes 55050240 | tf_op jit(solution)/shard_map/cond/branch_1_fun/routed/pallas_call | solution.py:319
  69.5 1.7 %collective-permute-done.5 = bf16[4,32,1920]{2,1,0:T(8,128)(2,1)} collective-permute-done((bf16[4,32,1920]{2,1,0:T(8,128)(2,1)}, bf16[4,32,1920]{2,1,0:T(8,128)(2,1)}, u32[]{:S(2)}, u32[]{:S(2)}) %collective-permute-start.5) | collective-permute-done | bytes 491552 | tf_op jit(solution)/shard_map/cond/branch_1_fun/ppermute | solution.py:90
  71.9 2.4 %collective-permute-start.17 = (bf16[224,640]{1,0:T(8,128)(2,1)}, bf16[224,640]{1,0:T(8,128)(2,1)S(1)}, u32[]{:S(2)}, u32[]{:S(2)}) collective-permute-start(bf16[224,640]{1,0:T(8,128)(2,1)} %get-tuple-element.140), channel_id=1, source_target_pairs={{0,12},{1,8},{2,4},{3,0},{4,13},{5,9},{6,5},{7,1},{8,14},{9,10},{1... | collective-permute-start | bytes 860168 | tf_op jit(solution)/shard_map/ppermute | solution.py:545
  74.3 1.6 %collective-permute-start.21 = (bf16[224,640]{1,0:T(8,128)(2,1)}, bf16[224,640]{1,0:T(8,128)(2,1)S(1)}, u32[]{:S(2)}, u32[]{:S(2)}) collective-permute-start(bf16[224,640]{1,0:T(8,128)(2,1)} %get-tuple-element.149), channel_id=1, source_target_pairs={{0,0},{1,4},{2,8},{3,12},{4,1},{5,5},{6,9},{7,13},{8,2},{9,6},{10,... | collective-permute-start | bytes 860168 | tf_op jit(solution)/shard_map/ppermute | solution.py:545
  78.8 2.4 %collective-permute-start.23 = (bf16[224,640]{1,0:T(8,128)(2,1)}, bf16[224,640]{1,0:T(8,128)(2,1)S(1)}, u32[]{:S(2)}, u32[]{:S(2)}) collective-permute-start(bf16[224,640]{1,0:T(8,128)(2,1)} %get-tuple-element.151), channel_id=1, source_target_pairs={{0,8},{1,12},{2,0},{3,4},{4,9},{5,13},{6,1},{7,5},{8,10},{9,14},{1... | collective-permute-start | bytes 860168 | tf_op jit(solution)/shard_map/ppermute | solution.py:545
  81.2 6.1 %shared_hidden.3 = (bf16[256,640]{1,0:T(8,128)(2,1)S(1)}, f32[1,512]{1,0:T(1,128)S(1)}) custom-call(s32[3]{0:T(128)} %copy-done.5, bf16[4,32,1920]{2,1,0:T(8,128)(2,1)} %get-tuple-element.130.rest_0_, bf16[4,32,1920]{2,1,0:T(8,128)(2,1)} %get-tuple-element.131.rest_1_, bf16[4,32,1920]{2,1,0:T(8,128)(2,1)} %get-tuple-element.132.rest_2_, ...), custom_call_target="tpu_custom_call" | custom-call | flops 1174405120 | bytes 4194304 | tf_op jit(solution)/shard_map/shared_hidden/pallas_call | solution.py:398
  87.4 19.4 %conditional.5 = (bf16[256,640]{1,0:T(8,128)(2,1)S(1)}, bf16[256,640]{1,0:T(8,128)(2,1)}, bf16[256,640]{1,0:T(8,128)(2,1)}, bf16[256,640]{1,0:T(8,128)(2,1)}, bf...) conditional(s32[]{:T(128)} %convert_element_type.38, () %tuple.34, ...), branch_computations={%region_4.0_spmd, %region_5.0_spmd} | conditional | flops 1175552000 | bytes 20250848 | solution.py:527
  87.4 2.5 %collective-permute-start.10 = (bf16[256,640]{1,0:T(8,128)(2,1)S(1)}, bf16[256,640]{1,0:T(8,128)(2,1)}, u32[]{:S(2)}, u32[]{:S(2)}) collective-permute-start(bf16[256,640]{1,0:T(8,128)(2,1)S(1)} %get-tuple-element.225.rest_9_), channel_id=1, source_target_pairs={{0,2},{1,3},{2,0},{3,1},{4,6},{5,7},{6,4},{7,5},{8,10},{9,11},{10,... | collective-permute-start | bytes 983048 | tf_op jit(solution)/shard_map/cond/branch_1_fun/ppermute | solution.py:90
  89.9 5.1 %shared_hidden.2 = (bf16[256,640]{1,0:T(8,128)(2,1)S(1)}, f32[1,512]{1,0:T(1,128)S(1)}) custom-call(s32[3]{0:T(128)S(1)} %get-tuple-element.80.where_ref, bf16[4,32,1920]{2,1,0:T(8,128)(2,1)S(1)} %get-tuple-element.81.rest_0_, bf16[4,32,1920]{2,1,0:T(8,128)(2,1)} %get-tuple-element.82.rest_1_, bf16[4,32,1920]{2,1,0:T(8,128)(2,1)} %get-tuple-element.83.rest_2_, ...), custom_call_target="tpu_custom_call" | custom-call | flops 1174405120 | bytes 4194304 | tf_op jit(solution)/shard_map/cond/branch_1_fun/shared_hidden/pallas_call | solution.py:398
  95.0 8.2 %collective-permute-done.10 = bf16[256,640]{1,0:T(8,128)(2,1)} collective-permute-done((bf16[256,640]{1,0:T(8,128)(2,1)S(1)}, bf16[256,640]{1,0:T(8,128)(2,1)}, u32[]{:S(2)}, u32[]{:S(2)}) %collective-permute-start.10) | collective-permute-done | bytes 327712 | tf_op jit(solution)/shard_map/cond/branch_1_fun/ppermute | solution.py:90
  103.7 2.4 %collective-permute-done.13 = bf16[2,448,512]{2,1,0:T(8,128)(2,1)S(1)} collective-permute-done((bf16[2,448,512]{2,1,0:T(8,128)(2,1)S(1)}, bf16[2,448,512]{2,1,0:T(8,128)(2,1)S(1)}, u32[]{:S(2)}, u32[]{:S(2)}) %collective-permute-start.13) | collective-permute-done | bytes 917536 | tf_op jit(solution)/shard_map/cond/branch_1_fun/ppermute | solution.py:90
  106.8 2.7 %collective-permute-start.19 = (bf16[256,640]{1,0:T(8,128)(2,1)S(1)}, bf16[256,640]{1,0:T(8,128)(2,1)S(1)}, u32[]{:S(2)}, u32[]{:S(2)}) collective-permute-start(bf16[256,640]{1,0:T(8,128)(2,1)S(1)} %get-tuple-element.148.rest_0_), channel_id=1, source_target_pairs={{0,2},{1,3},{2,0},{3,1},{4,6},{5,7},{6,4},{7,5},{8,10},{9,11},{10,... | collective-permute-start | bytes 983048 | tf_op jit(solution)/shard_map/ppermute | solution.py:90
  109.5 3.2 %down_far.1 = bf16[448,512]{1,0:T(8,128)(2,1)S(1)} custom-call(s32[3]{0:T(128)S(1)} %copy-done.6, f32[1,512]{1,0:T(1,128)S(1)} %get-tuple-element.154.scale_ref, bf16[256,640]{1,0:T(8,128)(2,1)S(1)} %get-tuple-element.155.rest_0_, bf16[256,640]{1,0:T(8,128)(2,1)} %get-tuple-element.156.rest_1_, bf16[256,640]{1,0:T(8,128)(2,1)} %get-tuple-element.157.rest_2_, ...), custom_call_target="tpu_custom_call" | custom-call | flops 704643072 | bytes 4194304 | tf_op jit(solution)/shard_map/down_far/pallas_call | solution.py:484
  112.7 1.6 %collective-permute-start.24 = (bf16[448,512]{1,0:T(8,128)(2,1)S(1)}, bf16[448,512]{1,0:T(8,128)(2,1)S(1)}, u32[]{:S(2)}, u32[]{:S(2)}) collective-permute-start(bf16[448,512]{1,0:T(8,128)(2,1)S(1)} %down_far.1), channel_id=1, source_target_pairs={{0,16},{16,0},{1,17},{17,1},{2,18},{18,2},{3,19},{19,3},{4,20},{20... | collective-permute-start | bytes 1376264 | tf_op jit(solution)/shard_map/ppermute | solution.py:90
  114.3 3.6 %collective-permute-done.19.rest_2_ = bf16[256,640]{1,0:T(8,128)(2,1)S(1)} collective-permute-done((bf16[256,640]{1,0:T(8,128)(2,1)S(1)}, bf16[256,640]{1,0:T(8,128)(2,1)S(1)}, u32[]{:S(2)}, u32[]{:S(2)}) %collective-permute-start.19) | collective-permute-done | bytes 327712 | tf_op jit(solution)/shard_map/ppermute | solution.py:90
  118.0 1.6 %collective-permute-done.20.rest_3_ = bf16[256,640]{1,0:T(8,128)(2,1)S(1)} collective-permute-done((bf16[256,640]{1,0:T(8,128)(2,1)S(1)}, bf16[256,640]{1,0:T(8,128)(2,1)S(1)}, u32[]{:S(2)}, u32[]{:S(2)}) %collective-permute-start.20) | collective-permute-done | bytes 327712 | tf_op jit(solution)/shard_map/ppermute | solution.py:90
  119.6 2.1 %down_near.1 = f32[448,512]{1,0:T(8,128)S(1)} custom-call(s32[3]{0:T(128)S(1)} %copy-done.6, f32[1,512]{1,0:T(1,128)S(1)} %get-tuple-element.147.scale_ref, bf16[256,640]{1,0:T(8,128)(2,1)S(1)} %get-tuple-element.148.rest_0_, bf16[256,640]{1,0:T(8,128)(2,1)S(1)} %collective-permute-done.18.rest_1_, bf16[256,640]{1,0:T(8,128)(2,1)S(1)} %collective-permute-done.19.rest_2_, ...), custom_call_target="tpu_custom_call" | custom-call | flops 704643072 | bytes 4194304 | tf_op jit(solution)/shard_map/down_near/pallas_call | solution.py:484
  121.7 3.4 %collective-permute-done.24 = bf16[448,512]{1,0:T(8,128)(2,1)S(1)} collective-permute-done((bf16[448,512]{1,0:T(8,128)(2,1)S(1)}, bf16[448,512]{1,0:T(8,128)(2,1)S(1)}, u32[]{:S(2)}, u32[]{:S(2)}) %collective-permute-start.24) | collective-permute-done | bytes 458784 | tf_op jit(solution)/shard_map/ppermute | solution.py:90
  125.1 2.2 %collective-permute-done.25 = bf16[448,512]{1,0:T(8,128)(2,1)S(1)} collective-permute-done((bf16[448,512]{1,0:T(8,128)(2,1)S(1)}, bf16[448,512]{1,0:T(8,128)(2,1)S(1)}, u32[]{:S(2)}, u32[]{:S(2)}) %collective-permute-start.25) | collective-permute-done | bytes 458784 | tf_op jit(solution)/shard_map/ppermute | solution.py:90
  127.6 3.8 %collective-permute-start.27 = (bf16[448,128]{1,0:T(8,128)(2,1)S(1)}, bf16[448,128]{1,0:T(8,128)(2,1)S(1)}, u32[]{:S(2)}, u32[]{:S(2)}) collective-permute-start(bf16[448,128]{1,0:T(8,128)(2,1)S(1)} %get-tuple-element.178), channel_id=1, source_target_pairs={{0,8},{4,12},{8,0},{12,4},{1,9},{5,13},{9,1},{13,5},{2,10},{6,14},... | collective-permute-start | bytes 344072 | tf_op jit(solution)/shard_map/ppermute | solution.py:90
  132.0 1.8 %collective-permute-done.26 = bf16[448,128]{1,0:T(8,128)(2,1)S(1)} collective-permute-done((bf16[448,128]{1,0:T(8,128)(2,1)S(1)}, bf16[448,128]{1,0:T(8,128)(2,1)S(1)}, u32[]{:S(2)}, u32[]{:S(2)}) %collective-permute-start.26) | collective-permute-done | bytes 114720 | tf_op jit(solution)/shard_map/ppermute | solution.py:90
  133.9 6.3 %collective-permute-done.27 = bf16[448,128]{1,0:T(8,128)(2,1)S(1)} collective-permute-done((bf16[448,128]{1,0:T(8,128)(2,1)S(1)}, bf16[448,128]{1,0:T(8,128)(2,1)S(1)}, u32[]{:S(2)}, u32[]{:S(2)}) %collective-permute-start.27) | collective-permute-done | bytes 114720 | tf_op jit(solution)/shard_map/ppermute | solution.py:90
  (60 shorter events, 15.1 us)
Async XLA Ops:
  0.1 21.6 %copy-start.5 = (s32[3]{0:T(128)}, s32[3]{0:T(128)S(1)}, u32[]{:S(2)}) copy-start(s32[3]{0:T(128)S(1)} %pad_add_fusion.where_ref) | copy-start | bytes 40
  1.7 9.9 %collective-permute-start.7 = (bf16[32,1920]{1,0:T(8,128)(2,1)S(1)}, bf16[32,1920]{1,0:T(8,128)(2,1)S(1)}, u32[]{:S(2)}, u32[]{:S(2)}) collective-permute-start(bf16[32,1920]{1,0:T(8,128)(2,1)S(1)} %get-tuple-element.51), channel_id=1, source_target_pairs={{0,4},{4,0},{8,12},{12,8},{1,5},{5,1},{9,13},{13,9},{2,6},{6,2},{1... | collective-permute-start | bytes 368648 | tf_op jit(solution)/shard_map/cond/branch_1_fun/ppermute | solution.py:90
  4.8 12.3 %collective-permute-start.8 = (bf16[32,1920]{1,0:T(8,128)(2,1)S(1)}, bf16[32,1920]{1,0:T(8,128)(2,1)S(1)}, u32[]{:S(2)}, u32[]{:S(2)}) collective-permute-start(bf16[32,1920]{1,0:T(8,128)(2,1)S(1)} %get-tuple-element.51), channel_id=1, source_target_pairs={{0,8},{4,12},{8,0},{12,4},{1,9},{5,13},{9,1},{13,5},{2,10},{6,14},... | collective-permute-start | bytes 368648 | tf_op jit(solution)/shard_map/cond/branch_1_fun/ppermute | solution.py:90
  7.4 9.7 %collective-permute-start.9 = (bf16[32,1920]{1,0:T(8,128)(2,1)S(1)}, bf16[32,1920]{1,0:T(8,128)(2,1)S(1)}, u32[]{:S(2)}, u32[]{:S(2)}) collective-permute-start(bf16[32,1920]{1,0:T(8,128)(2,1)S(1)} %get-tuple-element.51), channel_id=1, source_target_pairs={{0,12},{4,8},{8,4},{12,0},{1,13},{5,9},{9,5},{13,1},{2,14},{6,10},... | collective-permute-start | bytes 368648 | tf_op jit(solution)/shard_map/cond/branch_1_fun/ppermute | solution.py:90
  17.2 59.4 %collective-permute-start.14 = (bf16[448,640]{1,0:T(8,128)(2,1)}, bf16[448,640]{1,0:T(8,128)(2,1)S(1)}, u32[]{:S(2)}, u32[]{:S(2)}) collective-permute-start(bf16[448,640]{1,0:T(8,128)(2,1)} %get-tuple-element.135), channel_id=1, source_target_pairs={{0,4},{4,0},{8,12},{12,8},{1,5},{5,1},{9,13},{13,9},{2,6},{6,2},{1... | collective-permute-start | bytes 1720328 | tf_op jit(solution)/shard_map/ppermute | solution.py:90
  19.1 59.6 %collective-permute-start.15 = (bf16[448,640]{1,0:T(8,128)(2,1)}, bf16[448,640]{1,0:T(8,128)(2,1)S(1)}, u32[]{:S(2)}, u32[]{:S(2)}) collective-permute-start(bf16[448,640]{1,0:T(8,128)(2,1)} %get-tuple-element.136), channel_id=1, source_target_pairs={{0,8},{4,12},{8,0},{12,4},{1,9},{5,13},{9,1},{13,5},{2,10},{6,14},... | collective-permute-start | bytes 1720328 | tf_op jit(solution)/shard_map/ppermute | solution.py:90
  20.2 61.0 %collective-permute-start.16 = (bf16[448,640]{1,0:T(8,128)(2,1)}, bf16[448,640]{1,0:T(8,128)(2,1)}, u32[]{:S(2)}, u32[]{:S(2)}) collective-permute-start(bf16[448,640]{1,0:T(8,128)(2,1)} %get-tuple-element.137), channel_id=1, source_target_pairs={{0,12},{4,8},{8,4},{12,0},{1,13},{5,9},{9,5},{13,1},{2,14},{6,10},... | collective-permute-start | bytes 1720328 | tf_op jit(solution)/shard_map/ppermute | solution.py:90
  21.7 11.5 %collective-permute-start.1 = (bf16[4,32,1920]{2,1,0:T(8,128)(2,1)S(1)}, bf16[4,32,1920]{2,1,0:T(8,128)(2,1)}, u32[]{:S(2)}, u32[]{:S(2)}) collective-permute-start(bf16[4,32,1920]{2,1,0:T(8,128)(2,1)S(1)} %get-tuple-element.207.rest_0_), channel_id=1, source_target_pairs={{0,2},{1,3},{2,0},{3,1},{4,6},{5,7},{6,4},{7,5},{8,10},{9,11},{10,... | collective-permute-start | bytes 1474568 | tf_op jit(solution)/shard_map/cond/branch_1_fun/ppermute | solution.py:90
  23.2 11.2 %collective-permute-start.2 = (bf16[4,32,1920]{2,1,0:T(8,128)(2,1)S(1)}, bf16[4,32,1920]{2,1,0:T(8,128)(2,1)}, u32[]{:S(2)}, u32[]{:S(2)}) collective-permute-start(bf16[4,32,1920]{2,1,0:T(8,128)(2,1)S(1)} %get-tuple-element.207.rest_0_), channel_id=1, source_target_pairs={{0,16},{16,0},{1,17},{17,1},{2,18},{18,2},{3,19},{19,3},{4,20},{20... | collective-permute-start | bytes 1474568 | tf_op jit(solution)/shard_map/cond/branch_1_fun/ppermute | solution.py:90
  34.4 2.9 %collective-permute-start.3 = (bf16[4,32,1920]{2,1,0:T(8,128)(2,1)}, bf16[4,32,1920]{2,1,0:T(8,128)(2,1)}, u32[]{:S(2)}, u32[]{:S(2)}) collective-permute-start(bf16[4,32,1920]{2,1,0:T(8,128)(2,1)} %collective-permute-done.1.rest_2_), channel_id=1, source_target_pairs={{0,1},{1,0},{2,3},{3,2},{4,5},{5,4},{6,7},{7,6},{8,9},{9,8},{10,11... | collective-permute-start | bytes 1474568 | tf_op jit(solution)/shard_map/cond/branch_1_fun/ppermute | solution.py:90
  34.4 3.4 %collective-permute-start = (bf16[4,32,1920]{2,1,0:T(8,128)(2,1)S(1)}, bf16[4,32,1920]{2,1,0:T(8,128)(2,1)}, u32[]{:S(2)}, u32[]{:S(2)}) collective-permute-start(bf16[4,32,1920]{2,1,0:T(8,128)(2,1)S(1)} %get-tuple-element.207.rest_0_), channel_id=1, source_target_pairs={{0,1},{1,0},{2,3},{3,2},{4,5},{5,4},{6,7},{7,6},{8,9},{9,8},{10,11... | collective-permute-start | bytes 1474568 | tf_op jit(solution)/shard_map/cond/branch_1_fun/ppermute | solution.py:90
  37.3 31.6 %collective-permute-start.4 = (bf16[4,32,1920]{2,1,0:T(8,128)(2,1)}, bf16[4,32,1920]{2,1,0:T(8,128)(2,1)}, u32[]{:S(2)}, u32[]{:S(2)}) collective-permute-start(bf16[4,32,1920]{2,1,0:T(8,128)(2,1)} %collective-permute-done.2), channel_id=1, source_target_pairs={{0,2},{1,3},{2,0},{3,1},{4,6},{5,7},{6,4},{7,5},{8,10},{9,11},{10,... | collective-permute-start | bytes 1474568 | tf_op jit(solution)/shard_map/cond/branch_1_fun/ppermute | solution.py:90
  68.9 2.3 %collective-permute-start.5 = (bf16[4,32,1920]{2,1,0:T(8,128)(2,1)}, bf16[4,32,1920]{2,1,0:T(8,128)(2,1)}, u32[]{:S(2)}, u32[]{:S(2)}) collective-permute-start(bf16[4,32,1920]{2,1,0:T(8,128)(2,1)} %collective-permute-done.2), channel_id=1, source_target_pairs={{0,1},{1,0},{2,3},{3,2},{4,5},{5,4},{6,7},{7,6},{8,9},{9,8},{10,11... | collective-permute-start | bytes 1474568 | tf_op jit(solution)/shard_map/cond/branch_1_fun/ppermute | solution.py:90
  69.0 2.9 %collective-permute-start.6 = (bf16[4,32,1920]{2,1,0:T(8,128)(2,1)}, bf16[4,32,1920]{2,1,0:T(8,128)(2,1)}, u32[]{:S(2)}, u32[]{:S(2)}) collective-permute-start(bf16[4,32,1920]{2,1,0:T(8,128)(2,1)} %collective-permute-done.4), channel_id=1, source_target_pairs={{0,1},{1,0},{2,3},{3,2},{4,5},{5,4},{6,7},{7,6},{8,9},{9,8},{10,11... | collective-permute-start | bytes 1474568 | tf_op jit(solution)/shard_map/cond/branch_1_fun/ppermute | solution.py:90
  71.9 15.4 %collective-permute-start.17 = (bf16[224,640]{1,0:T(8,128)(2,1)}, bf16[224,640]{1,0:T(8,128)(2,1)S(1)}, u32[]{:S(2)}, u32[]{:S(2)}) collective-permute-start(bf16[224,640]{1,0:T(8,128)(2,1)} %get-tuple-element.140), channel_id=1, source_target_pairs={{0,12},{1,8},{2,4},{3,0},{4,13},{5,9},{6,5},{7,1},{8,14},{9,10},{1... | collective-permute-start | bytes 860168 | tf_op jit(solution)/shard_map/ppermute | solution.py:545
  74.3 35.2 %collective-permute-start.21 = (bf16[224,640]{1,0:T(8,128)(2,1)}, bf16[224,640]{1,0:T(8,128)(2,1)S(1)}, u32[]{:S(2)}, u32[]{:S(2)}) collective-permute-start(bf16[224,640]{1,0:T(8,128)(2,1)} %get-tuple-element.149), channel_id=1, source_target_pairs={{0,0},{1,4},{2,8},{3,12},{4,1},{5,5},{6,9},{7,13},{8,2},{9,6},{10,... | collective-permute-start | bytes 860168 | tf_op jit(solution)/shard_map/ppermute | solution.py:545
  77.4 32.0 %collective-permute-start.22 = (bf16[224,640]{1,0:T(8,128)(2,1)}, bf16[224,640]{1,0:T(8,128)(2,1)S(1)}, u32[]{:S(2)}, u32[]{:S(2)}) collective-permute-start(bf16[224,640]{1,0:T(8,128)(2,1)} %get-tuple-element.150), channel_id=1, source_target_pairs={{0,4},{1,0},{2,12},{3,8},{4,5},{5,1},{6,13},{7,9},{8,6},{9,2},{10,... | collective-permute-start | bytes 860168 | tf_op jit(solution)/shard_map/ppermute | solution.py:545
  78.8 30.7 %collective-permute-start.23 = (bf16[224,640]{1,0:T(8,128)(2,1)}, bf16[224,640]{1,0:T(8,128)(2,1)S(1)}, u32[]{:S(2)}, u32[]{:S(2)}) collective-permute-start(bf16[224,640]{1,0:T(8,128)(2,1)} %get-tuple-element.151), channel_id=1, source_target_pairs={{0,8},{1,12},{2,0},{3,4},{4,9},{5,13},{6,1},{7,5},{8,10},{9,14},{1... | collective-permute-start | bytes 860168 | tf_op jit(solution)/shard_map/ppermute | solution.py:545
  81.2 6.1 %copy-start.4 = (bf16[448,640]{1,0:T(8,128)(2,1)S(1)}, bf16[448,640]{1,0:T(8,128)(2,1)}, u32[]{:S(2)}) copy-start(bf16[448,640]{1,0:T(8,128)(2,1)} %copy-done.3) | copy-start | bytes 1720324
  81.2 6.1 %copy-start.6 = (s32[3]{0:T(128)S(1)}, s32[3]{0:T(128)}, u32[]{:S(2)}) copy-start(s32[3]{0:T(128)} %copy-done.5) | copy-start | bytes 40
  87.4 15.8 %collective-permute-start.10 = (bf16[256,640]{1,0:T(8,128)(2,1)S(1)}, bf16[256,640]{1,0:T(8,128)(2,1)}, u32[]{:S(2)}, u32[]{:S(2)}) collective-permute-start(bf16[256,640]{1,0:T(8,128)(2,1)S(1)} %get-tuple-element.225.rest_9_), channel_id=1, source_target_pairs={{0,2},{1,3},{2,0},{3,1},{4,6},{5,7},{6,4},{7,5},{8,10},{9,11},{10,... | collective-permute-start | bytes 983048 | tf_op jit(solution)/shard_map/cond/branch_1_fun/ppermute | solution.py:90
  89.8 13.3 %collective-permute-start.11 = (bf16[256,640]{1,0:T(8,128)(2,1)S(1)}, bf16[256,640]{1,0:T(8,128)(2,1)}, u32[]{:S(2)}, u32[]{:S(2)}) collective-permute-start(bf16[256,640]{1,0:T(8,128)(2,1)S(1)} %get-tuple-element.225.rest_9_), channel_id=1, source_target_pairs={{0,1},{1,0},{2,3},{3,2},{4,5},{5,4},{6,7},{7,6},{8,9},{9,8},{10,11... | collective-permute-start | bytes 983048 | tf_op jit(solution)/shard_map/cond/branch_1_fun/ppermute | solution.py:90
  103.1 2.9 %collective-permute-start.13 = (bf16[2,448,512]{2,1,0:T(8,128)(2,1)S(1)}, bf16[2,448,512]{2,1,0:T(8,128)(2,1)S(1)}, u32[]{:S(2)}, u32[]{:S(2)}) collective-permute-start(bf16[2,448,512]{2,1,0:T(8,128)(2,1)S(1)} %get-tuple-element.97), channel_id=1, source_target_pairs={{0,1},{1,0},{2,3},{3,2},{4,5},{5,4},{6,7},{7,6},{8,9},{9,8},{10,11... | collective-permute-start | bytes 2752520 | tf_op jit(solution)/shard_map/cond/branch_1_fun/ppermute | solution.py:90
  103.1 3.7 %collective-permute-start.12 = (bf16[256,640]{1,0:T(8,128)(2,1)}, bf16[256,640]{1,0:T(8,128)(2,1)}, u32[]{:S(2)}, u32[]{:S(2)}) collective-permute-start(bf16[256,640]{1,0:T(8,128)(2,1)} %collective-permute-done.10), channel_id=1, source_target_pairs={{0,1},{1,0},{2,3},{3,2},{4,5},{5,4},{6,7},{7,6},{8,9},{9,8},{10,11... | collective-permute-start | bytes 983048 | tf_op jit(solution)/shard_map/cond/branch_1_fun/ppermute | solution.py:90
  106.8 11.1 %collective-permute-start.19 = (bf16[256,640]{1,0:T(8,128)(2,1)S(1)}, bf16[256,640]{1,0:T(8,128)(2,1)S(1)}, u32[]{:S(2)}, u32[]{:S(2)}) collective-permute-start(bf16[256,640]{1,0:T(8,128)(2,1)S(1)} %get-tuple-element.148.rest_0_), channel_id=1, source_target_pairs={{0,2},{1,3},{2,0},{3,1},{4,6},{5,7},{6,4},{7,5},{8,10},{9,11},{10,... | collective-permute-start | bytes 983048 | tf_op jit(solution)/shard_map/ppermute | solution.py:90
  112.7 12.3 %collective-permute-start.24 = (bf16[448,512]{1,0:T(8,128)(2,1)S(1)}, bf16[448,512]{1,0:T(8,128)(2,1)S(1)}, u32[]{:S(2)}, u32[]{:S(2)}) collective-permute-start(bf16[448,512]{1,0:T(8,128)(2,1)S(1)} %down_far.1), channel_id=1, source_target_pairs={{0,16},{16,0},{1,17},{17,1},{2,18},{18,2},{3,19},{19,3},{4,20},{20... | collective-permute-start | bytes 1376264 | tf_op jit(solution)/shard_map/ppermute | solution.py:90
  114.3 13.0 %collective-permute-start.25 = (bf16[448,512]{1,0:T(8,128)(2,1)S(1)}, bf16[448,512]{1,0:T(8,128)(2,1)S(1)}, u32[]{:S(2)}, u32[]{:S(2)}) collective-permute-start(bf16[448,512]{1,0:T(8,128)(2,1)S(1)} %get-tuple-element.159), channel_id=1, source_target_pairs={{0,2},{1,3},{2,0},{3,1},{4,6},{5,7},{6,4},{7,5},{8,10},{9,11},{10,... | collective-permute-start | bytes 1376264 | tf_op jit(solution)/shard_map/ppermute | solution.py:90
  114.3 3.6 %collective-permute-start.18 = (bf16[256,640]{1,0:T(8,128)(2,1)S(1)}, bf16[256,640]{1,0:T(8,128)(2,1)S(1)}, u32[]{:S(2)}, u32[]{:S(2)}) collective-permute-start(bf16[256,640]{1,0:T(8,128)(2,1)S(1)} %get-tuple-element.148.rest_0_), channel_id=1, source_target_pairs={{0,1},{1,0},{2,3},{3,2},{4,5},{5,4},{6,7},{7,6},{8,9},{9,8},{10,11... | collective-permute-start | bytes 983048 | tf_op jit(solution)/shard_map/ppermute | solution.py:90
  118.0 1.6 %collective-permute-start.20 = (bf16[256,640]{1,0:T(8,128)(2,1)S(1)}, bf16[256,640]{1,0:T(8,128)(2,1)S(1)}, u32[]{:S(2)}, u32[]{:S(2)}) collective-permute-start(bf16[256,640]{1,0:T(8,128)(2,1)S(1)} %collective-permute-done.19.rest_2_), channel_id=1, source_target_pairs={{0,1},{1,0},{2,3},{3,2},{4,5},{5,4},{6,7},{7,6},{8,9},{9,8},{10,11... | collective-permute-start | bytes 983048 | tf_op jit(solution)/shard_map/ppermute | solution.py:90
  127.6 6.3 %collective-permute-start.26 = (bf16[448,128]{1,0:T(8,128)(2,1)S(1)}, bf16[448,128]{1,0:T(8,128)(2,1)S(1)}, u32[]{:S(2)}, u32[]{:S(2)}) collective-permute-start(bf16[448,128]{1,0:T(8,128)(2,1)S(1)} %get-tuple-element.176), channel_id=1, source_target_pairs={{0,4},{4,0},{8,12},{12,8},{1,5},{5,1},{9,13},{13,9},{2,6},{6,2},{1... | collective-permute-start | bytes 344072 | tf_op jit(solution)/shard_map/ppermute | solution.py:90
  127.6 12.5 %collective-permute-start.27 = (bf16[448,128]{1,0:T(8,128)(2,1)S(1)}, bf16[448,128]{1,0:T(8,128)(2,1)S(1)}, u32[]{:S(2)}, u32[]{:S(2)}) collective-permute-start(bf16[448,128]{1,0:T(8,128)(2,1)S(1)} %get-tuple-element.178), channel_id=1, source_target_pairs={{0,8},{4,12},{8,0},{12,4},{1,9},{5,13},{9,1},{13,5},{2,10},{6,14},... | collective-permute-start | bytes 344072 | tf_op jit(solution)/shard_map/ppermute | solution.py:90
  131.4 8.8 %collective-permute-start.28 = (bf16[448,128]{1,0:T(8,128)(2,1)S(1)}, bf16[448,128]{1,0:T(8,128)(2,1)S(1)}, u32[]{:S(2)}, u32[]{:S(2)}) collective-permute-start(bf16[448,128]{1,0:T(8,128)(2,1)S(1)} %get-tuple-element.177), channel_id=1, source_target_pairs={{0,12},{4,8},{8,4},{12,0},{1,13},{5,9},{9,5},{13,1},{2,14},{6,10},... | collective-permute-start | bytes 344072 | tf_op jit(solution)/shard_map/ppermute | solution.py:90
  (4 other events, 15.5 us)
